TPU v7x, 256 devices: a whole 4x4x8 slice. The times are simulated.
256 devices in a mesh: slab: 32 (over z, y), coil: 8 (over x, core).
Axes of the slice: x: 4, y: 4, z: 8, core: 2. Of those that a mesh axis runs over, the one named last changes fastest.
Arguments:
- image_x: float32 [384, 384, 32], P('slab'), may hold values from -6 to 6
- residual: float32 [384, 384, 32], P('slab'), may hold values from -15 to 15
- direction: float32 [384, 384, 32], P('slab'), may hold values from -15 to 15
- sensitivity: bfloat16 [384, 384, 1024], P('slab', None, 'coil'), may hold values from -0.29882812 to 0.29882812
- interp: float32 [32, 32, 4, 64, 128], P('slab'), may hold values from -0.75 to 0.75
- slot_tile: int32 [32, 32, 4], P('slab'), may hold values from 0 to 71
- counts: int32 [32, 32, 4], P('slab'), may hold values from 0 to 128, as said below
Outputs:
- next_image: float32 [384, 384, 32], P('slab')
- next_residual: float32 [384, 384, 32], P('slab')
- next_direction: float32 [384, 384, 32], P('slab')
Inputs may be any that keep to these rules, and one draw needn't show every extreme that they name: `counts`: 0 marks an empty slot; some block in every draw has all 128 samples live.
All inputs are finite; a program needn't handle non-finite values.
Results may differ from a plain program's by a relative error of at most 0.0003.
Values sent between devices are 32-bit elements; how exact they have to be, the bound alone decides.
No kernel may reach another device: no remote copies, remote signals or barrier semaphores. Data moves between devices by JAX's collectives and lax.ppermute only.
A program may use at most 128 MiB of HBM per device.

v0:
```python
import math

import jax
import jax.numpy as jnp
from jax import lax
from jax.sharding import PartitionSpec as P

TX = 16
TY = 4


def dft_tables(length):
    positions = jnp.arange(length, dtype=jnp.int32)
    products = positions[:, None] * positions[None, :] % length
    phases = products.astype(jnp.float32) * (2.0 * math.pi / length)
    norm_scale = 1.0 / math.sqrt(length)
    return (jnp.cos(phases) * norm_scale, -jnp.sin(phases) * norm_scale)


def column_tables(width_cols, planes):
    index = jnp.arange(width_cols, dtype=jnp.int32)
    coil_of = index // (2 * planes)
    part_of = index // planes % 2
    plane_of = index % planes
    same = (coil_of[:, None] == coil_of[None, :]) & (plane_of[:, None] == plane_of[None, :])
    forward = same & (part_of[:, None] == 0) & (part_of[None, :] == 1)
    backward = same & (part_of[:, None] == 1) & (part_of[None, :] == 0)
    swapper = forward.astype(jnp.float32) - backward.astype(jnp.float32)
    real_copy = (same & (part_of[:, None] == 0)).astype(jnp.float32)
    imag_copy = (same & (part_of[:, None] == 1)).astype(jnp.float32)
    outputs = jnp.arange(2 * planes, dtype=jnp.int32)
    coil_adder = ((index % (2 * planes))[:, None] == outputs[None, :]).astype(jnp.float32)
    return (swapper, real_copy, imag_copy, coil_adder)


def mix_columns(source, table):
    return jnp.einsum("abq,qp->abp", source, table, precision=lax.Precision.HIGHEST)


def transform_axis(source, real_table, imag_table, swapper, pattern):
    part_real = jnp.einsum(pattern, real_table, source, precision=lax.Precision.HIGHEST)
    part_imag = jnp.einsum(pattern, imag_table, source, precision=lax.Precision.HIGHEST)
    return part_real + mix_columns(part_imag, swapper)


def grid_blocks(weights, filled, values):
    samples = jnp.einsum("rjcs,rjcq->rjsq", weights, values, precision=lax.Precision.HIGHEST)
    sample_ids = jnp.arange(weights.shape[3], dtype=jnp.int32)
    live_mask = (sample_ids[None, None, :] < filled[:, :, None]).astype(jnp.float32)
    samples = samples * live_mask[..., None]
    return jnp.einsum("rjcs,rjsq->rjcq", weights, samples, precision=lax.Precision.HIGHEST)


def body(image_x, residual, direction, sensitivity, interp, slot_tile, counts):
    slab_count = lax.axis_size("slab")
    rows_dev, width_y, planes_two = direction.shape
    planes = planes_two // 2
    coils_dev = sensitivity.shape[2] // planes_two
    rows_all = rows_dev * slab_count
    cols_dev = width_y // slab_count
    width_cols = coils_dev * planes_two
    cells = TX * TY
    swapper, real_copy, imag_copy, coil_adder = column_tables(width_cols, planes)
    coil_maps = sensitivity.astype(jnp.float32)
    maps_real = mix_columns(coil_maps, real_copy)
    maps_imag = mix_columns(coil_maps, imag_copy)
    dir_wide = jnp.tile(direction, (1, 1, coils_dev))
    coil_image = maps_real * dir_wide + maps_imag * mix_columns(dir_wide, swapper)
    ytab_real, ytab_imag = dft_tables(width_y)
    xtab_real, xtab_imag = dft_tables(rows_all)
    along_y = transform_axis(coil_image, ytab_real, ytab_imag, swapper, "kb,abq->akq")
    pencils = lax.all_to_all(along_y, "slab", split_axis=1, concat_axis=0, tiled=True)
    spectrum = transform_axis(pencils, xtab_real, xtab_imag, swapper, "ka,abq->kbq")
    tiles = spectrum.reshape(rows_all // TX, TX, cols_dev // TY, TY, width_cols)
    tiles = jnp.transpose(tiles, (0, 2, 1, 3, 4)).reshape(-1, cells, width_cols)
    tile_count = tiles.shape[0]
    owned_tiles = slot_tile[0].reshape(-1)
    blocks = interp.shape[2]
    picked = jnp.take(tiles, owned_tiles, axis=0).reshape(slab_count, blocks, cells, width_cols)
    arrived = lax.all_to_all(picked, "slab", split_axis=0, concat_axis=0, tiled=True)
    gridded = grid_blocks(interp[0], counts[0], arrived)
    returned = lax.all_to_all(gridded, "slab", split_axis=0, concat_axis=0, tiled=True)
    selector = (owned_tiles[None, :] == jnp.arange(tile_count, dtype=jnp.int32)[:, None]).astype(
        jnp.float32
    )
    summed = jnp.dot(
        selector,
        returned.reshape(slab_count * blocks, cells * width_cols),
        precision=lax.Precision.HIGHEST,
    )
    grid_cells = summed.reshape(rows_all // TX, cols_dev // TY, TX, TY, width_cols)
    grid_cells = jnp.transpose(grid_cells, (0, 2, 1, 3, 4)).reshape(rows_all, cols_dev, width_cols)
    inverse_x = transform_axis(grid_cells, xtab_real, -xtab_imag, swapper, "ka,abq->kbq")
    slab_rows = lax.all_to_all(inverse_x, "slab", split_axis=0, concat_axis=1, tiled=True)
    coil_back = transform_axis(slab_rows, ytab_real, -ytab_imag, swapper, "kb,abq->akq")
    weighted_back = maps_real * coil_back - maps_imag * mix_columns(coil_back, swapper)
    local_sum = mix_columns(weighted_back, coil_adder)
    applied = lax.psum(local_sum, "coil")
    norm_now = lax.psum(jnp.sum(residual * residual), "slab")
    curvature = lax.psum(jnp.sum(direction * applied), "slab")
    step_size = norm_now / curvature
    next_image = image_x + step_size * direction
    next_residual = residual - step_size * applied
    norm_next = lax.psum(jnp.sum(next_residual * next_residual), "slab")
    next_direction = next_residual + norm_next / norm_now * direction
    return (next_image, next_residual, next_direction)


def solution(mesh):
    return jax.shard_map(
        body,
        mesh=mesh,
        in_specs=(
            P("slab", None, None),
            P("slab", None, None),
            P("slab", None, None),
            P("slab", None, "coil"),
            P("slab", None, None, None, None),
            P("slab", None, None),
            P("slab", None, None),
        ),
        out_specs=(P("slab", None, None), P("slab", None, None), P("slab", None, None)),
        check_vma=False,
    )
```

profile of v0, /device:TPU:8, one launch (start us, length us, event | category | flops | bytes accessed | tf_op | source)
XLA Modules:
  0.0 770.7 jit_solution(10634072767218710095)
XLA Ops:
  13.2 7.1 fusion.31
  20.3 7.3 fusion.37
  35.0 11.9 %all-to-all-start = ((f32[12,384,128]{2,0,1:T(8,128)}), f32[12,384,128]{2,0,1:T(8,128)}, u32[]{:S(2)}, u32[]{:S(2)}) async-start(f32[12,384,128]{2,0,1:T(8,128)} %copy.50), calls=%async_computation | async-start | bytes 6291456 | tf_op jit(solution)/shard_map/all_to_all | solution.py:72
  47.2 71.0 %all-to-all-done = f32[12,384,128]{2,0,1:T(8,128)} async-done(((f32[12,384,128]{2,0,1:T(8,128)}), f32[12,384,128]{2,0,1:T(8,128)}, u32[]{:S(2)}, u32[]{:S(2)}) %all-to-all-start) | async-done | bytes 2359328 | tf_op jit(solution)/shard_map/all_to_all | solution.py:72
  126.5 7.8 %fusion.29 = f32[384,12,128]{2,0,1:T(8,128)S(1)} fusion(f32[384,12,128]{2,0,1:T(8,128)} %all_to_all.35), kind=kOutput, calls=%fused_computation.33 | convolution fusion | flops 2719531008 | bytes 4718592 | tf_op jit(solution)/shard_map/ka,abq->kbq/dot_general | solution.py:42
  136.5 6.3 convolution_add_fusion.1
  154.8 7.5 all-to-all-start.1
  162.5 93.0 %all-to-all-done.1 = f32[32,4,64,128]{3,2,1,0:T(8,128)} async-done(((f32[32,4,64,128]{3,2,1,0:T(8,128)}), f32[32,4,64,128]{3,2,1,0:T(8,128)}, u32[]{:S(2)}, u32[]{:S(2)}) %all-to-all-start.1) | async-done | bytes 4194336 | tf_op jit(solution)/shard_map/all_to_all | solution.py:80
  255.6 16.7 %fusion.3 = f32[32,4,128,128]{3,2,1,0:T(8,128)S(1)} fusion(f32[32,4,64,128]{3,2,1,0:T(8,128)} %all-to-all-done.1, f32[1,32,4,64,128]{4,3,2,1,0:T(8,128)} %param.11), kind=kOutput, calls=%fused_computation.5 | convolution fusion | flops 1610612736 | bytes 16777216 | tf_op jit(solution)/shard_map/rjcs,rjcq->rjsq/dot_general | solution.py:47
  272.3 17.8 %fusion.14 = f32[32,4,64,128]{3,2,1,0:T(8,128)} fusion(f32[1,32,4,64,128]{4,3,2,1,0:T(8,128)S(1)} %copy-done.6, f32[32,4,128,128]{3,2,1,0:T(8,128)S(1)} %fusion.3, f32[32,4,128]{2,1,0:T(4,128)S(1)} %fusion.85), kind=kOutput, calls=%fused_computation.21 | convolution fusion | flops 1612709888 | bytes 16842752 | tf_op jit(solution)/shard_map/rjcs,rjsq->rjcq/dot_general | solution.py:51
  290.1 7.6 all-to-all-start.2
  297.9 93.8 %all-to-all-done.2 = f32[32,4,64,128]{3,2,1,0:T(8,128)} async-done(((f32[32,4,64,128]{3,2,1,0:T(8,128)}), f32[32,4,64,128]{3,2,1,0:T(8,128)}, u32[]{:S(2)}, u32[]{:S(2)}) %all-to-all-start.2) | async-done | bytes 4194336 | tf_op jit(solution)/shard_map/all_to_all | solution.py:82
  391.6 7.4 copy.91
  399.1 5.6 copy.56
  404.7 4.8 convolution_bitcast_fusion
  410.8 6.2 fusion.27
  419.1 6.3 convolution_add_fusion
  428.6 7.4 all-to-all-start.3
  436.6 70.9 %all-to-all-done.3 = f32[384,12,128]{2,1,0:T(8,128)} async-done(((f32[384,12,128]{2,1,0:T(8,128)}), f32[384,12,128]{2,1,0:T(8,128)}, u32[]{:S(2)}, u32[]{:S(2)}) %all-to-all-start.3) | async-done | bytes 2359328 | tf_op jit(solution)/shard_map/all_to_all | solution.py:94
  515.6 11.7 %fusion.25 = f32[12,128,384]{2,1,0:T(8,128)S(1)} fusion(f32[12,384,128]{2,1,0:T(8,128)} %all_to_all.41), kind=kOutput, calls=%fused_computation.29 | convolution fusion | flops 2719678464 | bytes 4718592 | tf_op jit(solution)/shard_map/kb,abq->akq/dot_general | solution.py:42
  527.3 10.4 %fusion.33 = f32[12,128,384]{2,1,0:T(8,128)S(1)} fusion(f32[12,384,128]{2,1,0:T(8,128)S(1)} %copy-done.5), kind=kOutput, calls=%fused_computation.37 | convolution fusion | flops 2719383552 | bytes 4718592 | tf_op jit(solution)/shard_map/kb,abq->akq/dot_general | solution.py:41
  545.3 64.0 %all-reduce.3.cloned.1.call-done = f32[12,384,32]{1,2,0:T(8,128)} async-done(((f32[12,384,32]{1,2,0:T(8,128)}), f32[12,384,32]{1,2,0:T(8,128)}) %all-reduce.3.cloned.1.call-update) | async-done | bytes 589840 | tf_op jit(solution)/shard_map/psum | solution.py:98
  611.1 71.8 %all-reduce = (f32[]{:T(128)}, f32[]{:T(128)}) all-reduce(f32[]{:T(128)} %multiply_reduce_fusion.2, f32[]{:T(128)} %multiply_reduce_fusion.1), channel_id=1, replica_groups=mesh['slab'=32,'coil'=8] {'slab'}, use_global_device_ids=true, to_apply=%region_1.2 | all-reduce | flops 2 | bytes 16 | tf_op jit(solution)/shard_map/psum | solution.py:99
  686.2 74.7 %psum.31 = f32[]{:T(128)} all-reduce(f32[]{:T(128)} %get-tuple-element.5), channel_id=1, replica_groups=mesh['slab'=32,'coil'=8] {'slab'}, use_global_device_ids=true, to_apply=%region_6.7 | all-reduce | flops 1 | bytes 8 | tf_op jit(solution)/shard_map/psum | solution.py:104
  (73 shorter events, 64.0 us)
Async XLA Ops:
  7.2 1.3 copy-start
  9.1 1.1 copy-start.7
  10.1 3.1 copy-start.2
  35.0 11.9 %copy-start.14 = (s32[1,32,4]{1,2,0:T(4,128)S(1)}, s32[1,32,4]{1,2,0:T(4,128)}, u32[]{:S(2)}) copy-start(s32[1,32,4]{1,2,0:T(4,128)} %param.12) | copy-start | bytes 1540
  35.0 83.2 %all-to-all-start = ((f32[12,384,128]{2,0,1:T(8,128)}), f32[12,384,128]{2,0,1:T(8,128)}, u32[]{:S(2)}, u32[]{:S(2)}) async-start(f32[12,384,128]{2,0,1:T(8,128)} %copy.50), calls=%async_computation | async-start | bytes 6291456 | tf_op jit(solution)/shard_map/all_to_all | solution.py:72
  134.3 2.2 copy-start.4
  154.8 7.5 copy-start.15
  154.8 100.8 %all-to-all-start.1 = ((f32[32,4,64,128]{3,2,1,0:T(8,128)}), f32[32,4,64,128]{3,2,1,0:T(8,128)}, u32[]{:S(2)}, u32[]{:S(2)}) async-start(f32[32,4,64,128]{3,2,1,0:T(8,128)} %broadcast_select_fusion), calls=%async_computation.1 | async-start | bytes 8388608 | tf_op jit(solution)/shard_map/all_to_all | solution.py:80
  255.6 16.7 %copy-start.6 = (f32[1,32,4,64,128]{4,3,2,1,0:T(8,128)S(1)}, f32[1,32,4,64,128]{4,3,2,1,0:T(8,128)}, u32[]{:S(2)}) copy-start(f32[1,32,4,64,128]{4,3,2,1,0:T(8,128)} %param.11) | copy-start | bytes 12582916
  290.1 101.5 %all-to-all-start.2 = ((f32[32,4,64,128]{3,2,1,0:T(8,128)}), f32[32,4,64,128]{3,2,1,0:T(8,128)}, u32[]{:S(2)}, u32[]{:S(2)}) async-start(f32[32,4,64,128]{3,2,1,0:T(8,128)} %fusion.14), calls=%async_computation.2 | async-start | bytes 8388608 | tf_op jit(solution)/shard_map/all_to_all | solution.py:82
  428.6 78.9 %all-to-all-start.3 = ((f32[384,12,128]{2,1,0:T(8,128)}), f32[384,12,128]{2,1,0:T(8,128)}, u32[]{:S(2)}, u32[]{:S(2)}) async-start(f32[384,12,128]{2,1,0:T(8,128)} %copy.58), calls=%async_computation.3 | async-start | bytes 6291456 | tf_op jit(solution)/shard_map/all_to_all | solution.py:94
  436.0 173.3 %all-reduce.3.cloned.1.call-start = ((), (), s32[]{:S(2)}) async-start(), calls=%async_computation.4 | async-start | bytes 1179648 | tf_op jit(solution)/shard_map/psum | solution.py:98
  515.5 11.7 %copy-start.5 = (f32[12,384,128]{2,1,0:T(8,128)S(1)}, f32[12,384,128]{2,1,0:T(8,128)}, u32[]{:S(2)}) copy-start(f32[12,384,128]{2,1,0:T(8,128)} %all_to_all.41) | copy-start | bytes 7077892
  540.1 2.4 copy-start.3
  540.1 2.4 copy-start.16
  542.5 2.1 copy-start.10
  542.5 66.8 %copy-start.8 = (f32[12,384,32]{1,2,0:T(8,128)S(1)}, f32[12,384,32]{1,2,0:T(8,128)}, u32[]{:S(2)}) copy-start(f32[12,384,32]{1,2,0:T(8,128)} %param.9) | copy-start | bytes 1769476
  544.5 139.8 %copy-start.11 = (f32[12,384,32]{1,2,0:T(8,128)S(1)}, f32[12,384,32]{1,2,0:T(8,128)}, u32[]{:S(2)}) copy-start(f32[12,384,32]{1,2,0:T(8,128)} %param.8) | copy-start | bytes 1769476
  544.5 217.7 %copy-start.9 = (f32[12,384,32]{1,2,0:T(8,128)S(1)}, f32[12,384,32]{1,2,0:T(8,128)}, u32[]{:S(2)}) copy-start(f32[12,384,32]{1,2,0:T(8,128)} %param.9) | copy-start | bytes 1769476
  544.5 217.7 %copy-start.13 = (f32[12,384,32]{1,2,0:T(8,128)S(1)}, f32[12,384,32]{1,2,0:T(8,128)}, u32[]{:S(2)}) copy-start(f32[12,384,32]{1,2,0:T(8,128)} %param.7) | copy-start | bytes 1769476
  682.9 80.5 %copy-start.1 = (bf16[12,384,128]{2,1,0:T(8,128)(2,1)S(1)}, bf16[12,384,128]{2,1,0:T(8,128)(2,1)}, u32[]{:S(2)}) copy-start(bf16[12,384,128]{2,1,0:T(8,128)(2,1)} %param.10) | copy-start | bytes 3538948
  686.2 77.3 %copy-start.12 = (f32[12,384,32]{1,2,0:T(8,128)}, f32[12,384,32]{1,2,0:T(8,128)S(1)}, u32[]{:S(2)}) copy-start(f32[12,384,32]{1,2,0:T(8,128)S(1)} %get-tuple-element.6) | copy-start | bytes 1769476
Sparse Core Ops, SparseCore 0:
  544.7 64.5 all-reduce.2
where the time goes:
time: 780 us; the launch traced here: 771 us
  waiting for transfers between devices  393 us (50%)
  blocking collectives  147 us (19%)
  matrix products  121 us (16%)
  local copies, waits for them, and re-layouts  47.3 us (6%)
  starting transfers between devices  34.5 us (4%)
  between operations  17.6 us (2%)
  other arithmetic  10.7 us (1%)
    all_to_all x1, waiting for transfers between devices, body(): lax.all_to_all(gridded, 'slab', split_axis=0, concat_axis=0, tiled=True)  93.8 us
    all_to_all x1, waiting for transfers between devices, body(): lax.all_to_all(picked, 'slab', split_axis=0, concat_axis=0, tiled=True)  93 us
    psum x1, blocking collectives, body(): norm_next = lax.psum(jnp.sum(next_residual * next_residual), 'slab')  74.7 us
    psum x1, blocking collectives, body(): norm_now = lax.psum(jnp.sum(residual * residual), 'slab')  71.8 us
    all_to_all x1, waiting for transfers between devices, body(): lax.all_to_all(along_y, 'slab', split_axis=1, concat_axis=0, tiled=True)  71 us
    all_to_all x1, waiting for transfers between devices, body(): lax.all_to_all(inverse_x, 'slab', split_axis=0, concat_axis=1, tiled=True)  70.9 us
    psum x1, waiting for transfers between devices, body(): applied = lax.psum(local_sum, 'coil')  64 us
    dot_general x4, matrix products, transform_axis(): jnp.einsum(pattern, imag_table, source, precision=lax.Precision.HIGHEST)  32.8 us
  transfers between devices with their start and end apart: 5, of which 5 were waited for; matrix products, arithmetic and copies ran while one was open for 0% of the time, Pallas kernels for 0%

commit v1 on v0

v1 whole, which is shorter than its diff:
```python
import jax
import jax.numpy as jnp
import ml_dtypes
import numpy as np
from jax import lax
from jax.experimental import pallas as pl
from jax.experimental.pallas import tpu as pltpu
from jax.sharding import Mesh
from jax.sharding import PartitionSpec as P

N = 384
SLABS = 32
ROWS = 12
PAIRS = ROWS // 2
LANES = 128
PLANES = 16
TX = 16
TY = 4
CELLS = TX * TY
TILES = 72
CAP = 4
SB = 128
SLAB = ("z", "y")
COIL = ("x", "core")
ALL = ("z", "y", "x", "core")
VMEM_LIMIT = 56 * 1024 * 1024
F32 = jnp.float32
BF16 = jnp.bfloat16
NT = (((1,), (1,)), ((), ()))


def split_table(table):
    table = table.astype(np.float32)
    high = table.astype(ml_dtypes.bfloat16)
    low = (table - high.astype(np.float32)).astype(ml_dtypes.bfloat16)
    return high, low


def dft_tables():
    pos = np.arange(N)
    phase = (pos[:, None] * pos[None, :] % N) * (2.0 * np.pi / N)
    real = np.cos(phase) / np.sqrt(N)
    imag = -np.sin(phase) / np.sqrt(N)
    base = ROWS * np.arange(SLABS)[:, None]
    rows = np.concatenate([(base + np.arange(8)).reshape(-1), (base + np.arange(8, ROWS)).reshape(-1)])
    cols = np.concatenate([(base + 2 * np.arange(PAIRS) + i).reshape(-1) for i in range(2)])
    return split_table(np.concatenate([real[rows], imag[rows]])), split_table(np.concatenate([real[:, cols], imag[:, cols]]))


def split(value):
    high = value.astype(BF16)
    return high, (value - high.astype(F32)).astype(BF16)


def dot(a, b):
    return jnp.dot(a, b, preferred_element_type=F32)


def dot3(a_high, a_low, b_high, b_low):
    return dot(a_high, b_high) + (dot(a_high, b_low) + dot(a_low, b_high))


def dot_nt(a, b):
    return lax.dot_general(a, b, NT, preferred_element_type=F32)


def imag_lanes(shape):
    return lax.broadcasted_iota(jnp.int32, shape, 1) // PLANES % 2 == 1


def times_i(value, imag):
    lanes = value.shape[1]
    return jnp.where(imag, pltpu.roll(value, PLANES, 1), -pltpu.roll(value, lanes - PLANES, 1))


def spread_maps(maps, imag):
    real_part = jnp.where(imag, pltpu.roll(maps, PLANES, 1), maps)
    imag_part = jnp.where(imag, maps, pltpu.roll(maps, LANES - PLANES, 1))
    return real_part, imag_part


def store_outgoing(out_ref, start, even, odd):
    out_ref[:, start:start + 8, :] = even[:256].reshape(SLABS, 8, LANES)
    out_ref[:, start + 8:start + 16, :] = odd[:256].reshape(SLABS, 8, LANES)
    lower = lax.broadcasted_iota(jnp.int32, (8, LANES), 0) < 4
    for m in range(SLABS // 2):
        first = even[256 + 8 * m:264 + 8 * m]
        second = odd[256 + 8 * m:264 + 8 * m]
        out_ref[2 * m, start + 16:start + 24, :] = jnp.where(lower, first, pltpu.roll(second, 4, 0))
        out_ref[2 * m + 1, start + 16:start + 24, :] = jnp.where(lower, pltpu.roll(first, 4, 0), second)


def arrived_rows(ref, index):
    parts = []
    for i in range(2):
        start = i * 8 + index if index < 8 else 16 + 4 * i + index - 8
        parts.append(ref[pl.ds(start, SLABS * PAIRS, stride=24), :])
    return jnp.concatenate(parts, axis=0)


def gram_kernel(coil_ref, counts_ref, w_ref, out_ref, scratch):
    step = pl.program_id(0)
    owners = w_ref.shape[0]
    coil = coil_ref[0]
    lane = lax.broadcasted_iota(jnp.int32, (8, SB), 1)
    for o in range(owners):
        for j in range(CAP):
            for v in range(TY):
                at = (j * TY + v) * TX
                scratch[o % 2, at:at + TX, :] = w_ref[o, j, pl.ds(v, TX, stride=TY), :]
        rows = []
        for j in range(CAP):
            mine = scratch[o % 2, pl.ds(pl.multiple_of(j * CELLS + coil * 8, 8), 8), :]
            live = counts_ref[(step * owners + o) * CAP + j]
            rows.append(jnp.where(lane < live, mine, 0.0))
        l_high, l_low = split(jnp.concatenate(rows, axis=0))
        r_high, r_low = split(scratch[o % 2])
        gram = dot_nt(l_high, r_high) + (dot_nt(l_high, r_low) + dot_nt(l_low, r_high))
        for m in range(CAP // 2):
            first = gram[16 * m:16 * m + 8, LANES * m:LANES * (m + 1)]
            second = gram[16 * m + 8:16 * m + 16, LANES * m:LANES * (m + 1)]
            out_ref[o, 8 * m:8 * m + 8, :] = jnp.where(lane < CELLS, first, second)


def gram_rows(interp, counts, coil):
    owners = 4
    return pl.pallas_call(
        gram_kernel,
        grid=(SLABS // owners,),
        in_specs=[
            pl.BlockSpec(memory_space=pltpu.SMEM),
            pl.BlockSpec(memory_space=pltpu.SMEM),
            pl.BlockSpec((owners, CAP, CELLS, SB), lambda i: (i, 0, 0, 0)),
        ],
        out_specs=pl.BlockSpec((owners, 16, LANES), lambda i: (i, 0, 0)),
        out_shape=jax.ShapeDtypeStruct((SLABS, 16, LANES), F32),
        scratch_shapes=[pltpu.VMEM((2, CAP * CELLS, SB), F32)],
        compiler_params=pltpu.CompilerParams(vmem_limit_bytes=VMEM_LIMIT),
        name="gram_rows",
    )(coil, counts, interp)


def gram_sum_kernel(tiles_ref, in_ref, out_ref, total):
    total[...] = jnp.zeros_like(total)
    lane = lax.broadcasted_iota(jnp.int32, (8, LANES), 1)

    def add(r, carry):
        for j in range(CAP):
            tile = tiles_ref[r * CAP + j]
            piece = in_ref[r, 8 * (j // 2):8 * (j // 2) + 8, :]
            keep = lane < CELLS if j % 2 == 0 else lane >= CELLS
            total[tile] = total[tile] + jnp.where(keep, piece, 0.0)
        return carry

    lax.fori_loop(0, SLABS, add, 0)
    groups = N // TX // 2
    for b in range(ROWS // TY):
        for m in range(groups):
            first = total[2 * m * 3 + b]
            second = total[(2 * m + 1) * 3 + b]
            first = first + pltpu.roll(first, CELLS, 1)
            second = second + pltpu.roll(second, CELLS, 1)
            at = (b * groups + m) * 8
            out_ref[at:at + 8, :] = jnp.where(lane < CELLS, first, second)


def gram_sum(arrived, tiles):
    return pl.pallas_call(
        gram_sum_kernel,
        in_specs=[pl.BlockSpec(memory_space=pltpu.SMEM), pl.BlockSpec(memory_space=pltpu.VMEM)],
        out_specs=pl.BlockSpec(memory_space=pltpu.VMEM),
        out_shape=jax.ShapeDtypeStruct((TILES // 2 * 8, LANES), F32),
        scratch_shapes=[pltpu.VMEM((TILES, 8, LANES), F32)],
        compiler_params=pltpu.CompilerParams(vmem_limit_bytes=VMEM_LIMIT),
        name="gram_sum",
    )(tiles, arrived)


def forward_y_kernel(d_ref, s_ref, th_ref, tl_ref, out_ref):
    imag = imag_lanes((N, LANES))
    images = []
    for i in range(2):
        d = d_ref[i]
        wide = jnp.concatenate([d] * (LANES // (2 * PLANES)), axis=0).T
        real_map, imag_map = spread_maps(s_ref[i].astype(F32), imag)
        images.append(real_map * wide + imag_map * times_i(wide, imag))
    x_high, x_low = split(jnp.concatenate(images, axis=1))
    both = dot3(th_ref[...], tl_ref[...], x_high, x_low)
    done = []
    for i in range(2):
        half = both[:, LANES * i:LANES * (i + 1)]
        done.append(half[:N] + times_i(half[N:], imag))
    store_outgoing(out_ref, 0, done[0], done[1])


def forward_y(direction, maps, table):
    return pl.pallas_call(
        forward_y_kernel,
        grid=(PAIRS,),
        in_specs=[
            pl.BlockSpec((2, 2 * PLANES, N), lambda i: (i, 0, 0)),
            pl.BlockSpec((2, N, LANES), lambda i: (i, 0, 0)),
            pl.BlockSpec((2 * N, N), lambda i: (0, 0)),
            pl.BlockSpec((2 * N, N), lambda i: (0, 0)),
        ],
        out_specs=pl.BlockSpec((SLABS, 24, LANES), lambda i: (0, i, 0)),
        out_shape=jax.ShapeDtypeStruct((SLABS, 24 * PAIRS, LANES), F32),
        compiler_params=pltpu.CompilerParams(vmem_limit_bytes=VMEM_LIMIT),
        name="forward_y",
    )(direction, maps, *table)


def middle_kernel(in_ref, g_ref, fh_ref, fl_ref, bh_ref, bl_ref, out_ref, curve_ref, grid_ref):
    imag = imag_lanes((N, LANES))
    for p in range(PAIRS):
        x = jnp.concatenate([arrived_rows(in_ref, 2 * p), arrived_rows(in_ref, 2 * p + 1)], axis=1)
        x_high, x_low = split(x)
        both = dot3(fh_ref[...], fl_ref[...], x_high, x_low)
        for i in range(2):
            half = both[:, LANES * i:LANES * (i + 1)]
            grid_ref[2 * p + i] = half[:N] + times_i(half[N:], imag)
    left = lax.broadcasted_iota(jnp.int32, (CELLS, LANES), 1) < CELLS
    curve = jnp.zeros((8, LANES), F32)
    groups = N // TX // 2
    for b in range(ROWS // TY):
        for m in range(groups):
            at = (b * groups + m) * 8
            packed = jnp.concatenate([g_ref[c, at:at + 8, :] for c in range(8)], axis=0)
            weights = jnp.concatenate([jnp.where(left, packed, 0.0), jnp.where(left, 0.0, packed)], axis=0)
            tile = jnp.concatenate(
                [grid_ref[b * TY + v, (2 * m + h) * TX:(2 * m + h + 1) * TX, :] for h in range(2) for v in range(TY)],
                axis=0,
            )
            applied = dot3(*split(weights), *split(tile))
            product = tile * applied
            curve = curve + jnp.sum(product.reshape(2 * CELLS // 8, 8, LANES), axis=0)
            for h in range(2):
                for v in range(TY):
                    grid_ref[b * TY + v, (2 * m + h) * TX:(2 * m + h + 1) * TX, :] = applied[
                        h * CELLS + v * TX:h * CELLS + (v + 1) * TX
                    ]
    curve_ref[...] = curve
    for p in range(PAIRS):
        x_high, x_low = split(jnp.concatenate([grid_ref[2 * p], grid_ref[2 * p + 1]], axis=1))
        both = dot3(bh_ref[...], bl_ref[...], x_high, x_low)
        done = []
        for i in range(2):
            half = both[:, LANES * i:LANES * (i + 1)]
            done.append(half[:N] - times_i(half[N:], imag))
        store_outgoing(out_ref, 24 * p, done[0], done[1])


def middle(arrived, grams, table_in, table_out):
    vmem = pl.BlockSpec(memory_space=pltpu.VMEM)
    return pl.pallas_call(
        middle_kernel,
        in_specs=[vmem] * 6,
        out_specs=[vmem, vmem],
        out_shape=[
            jax.ShapeDtypeStruct((SLABS, 24 * PAIRS, LANES), F32),
            jax.ShapeDtypeStruct((8, LANES), F32),
        ],
        scratch_shapes=[pltpu.VMEM((ROWS, N, LANES), F32)],
        compiler_params=pltpu.CompilerParams(vmem_limit_bytes=VMEM_LIMIT),
        name="middle",
    )(arrived, grams, *table_in, *table_out)


def backward_y_kernel(in_ref, s_ref, th_ref, tl_ref, out_ref):
    imag = imag_lanes((N, LANES))
    adder = (
        lax.broadcasted_iota(jnp.int32, (2 * PLANES, LANES), 1) % (2 * PLANES)
        == lax.broadcasted_iota(jnp.int32, (2 * PLANES, LANES), 0)
    ).astype(BF16)
    for p in range(PAIRS):
        x = jnp.concatenate([arrived_rows(in_ref, 2 * p), arrived_rows(in_ref, 2 * p + 1)], axis=1)
        x_high, x_low = split(x)
        both = dot3(th_ref[...], tl_ref[...], x_high, x_low)
        for i in range(2):
            half = both[:, LANES * i:LANES * (i + 1)]
            back = half[:N] - times_i(half[N:], imag)
            real_map, imag_map = spread_maps(s_ref[2 * p + i].astype(F32), imag)
            high, low = split(real_map * back - imag_map * times_i(back, imag))
            out_ref[2 * p + i] = dot_nt(adder, high) + dot_nt(adder, low)


def backward_y(arrived, maps, table):
    vmem = pl.BlockSpec(memory_space=pltpu.VMEM)
    return pl.pallas_call(
        backward_y_kernel,
        in_specs=[vmem] * 4,
        out_specs=vmem,
        out_shape=jax.ShapeDtypeStruct((ROWS, 2 * PLANES, N), F32),
        compiler_params=pltpu.CompilerParams(vmem_limit_bytes=VMEM_LIMIT),
        name="backward_y",
    )(arrived, maps, *table)


def all_sum(value, axis, count):
    step = 1
    while step < count:
        value = value + lax.ppermute(value, axis, [(i, i ^ step) for i in range(count)])
        step *= 2
    return value


def body(image_x, residual, direction, sensitivity, interp, slot_tile, counts):
    rows_table, cols_table = dft_tables()
    rows_table = tuple(jnp.asarray(t) for t in rows_table)
    cols_table = tuple(jnp.asarray(t) for t in cols_table)
    image_t, residual_t, direction_t = (jnp.transpose(a, (0, 2, 1)) for a in (image_x, residual, direction))
    coil = lax.axis_index(COIL).astype(jnp.int32)
    core = lax.axis_index("core")
    xpos = lax.axis_index("x")

    grams = gram_rows(interp[0], counts[0].reshape(-1), coil.reshape(1))
    grams = lax.all_to_all(grams, SLAB, split_axis=0, concat_axis=0, tiled=True)
    grams = gram_sum(grams, slot_tile[0].reshape(-1))
    grams = lax.all_gather(grams, COIL, axis=0, tiled=False)

    outgoing = forward_y(direction_t, sensitivity, rows_table)
    pencils = lax.all_to_all(outgoing, SLAB, split_axis=0, concat_axis=0, tiled=True)
    outgoing, curve = middle(pencils.reshape(-1, LANES), grams, cols_table, rows_table)
    norms = jnp.stack([jnp.sum(curve), 0.125 * jnp.sum(residual * residual)])
    norms = jnp.broadcast_to(norms[:, None, None], (2, 4, LANES)).reshape(8, LANES)
    norms = all_sum(all_sum(norms, COIL, 8), SLAB, SLABS)
    slab_rows = lax.all_to_all(outgoing, SLAB, split_axis=0, concat_axis=0, tiled=True)
    local = backward_y(slab_rows.reshape(-1, LANES), sensitivity, cols_table)

    curvature = norms[0, 0]
    norm_now = norms[4, 0]
    step_size = norm_now / curvature
    halves = local.reshape(2, N // 2, N)
    kept = lax.dynamic_index_in_dim(halves, core, 0, keepdims=False)
    sent = lax.dynamic_index_in_dim(halves, 1 - core, 0, keepdims=False)
    kept = kept + lax.ppermute(sent, "core", [(0, 1), (1, 0)])
    shares = lax.all_to_all(kept.reshape(4, N // 8, N), "x", split_axis=0, concat_axis=0, tiled=True)
    applied = jnp.sum(shares, axis=0)
    own = lax.dynamic_slice_in_dim(residual_t.reshape(N, N), core * (N // 2) + xpos * (N // 8), N // 8, 0)
    own = own - step_size * applied
    norm_next = jnp.broadcast_to(jnp.sum(own * own), (256, 1, LANES))
    norm_next = jnp.sum(lax.all_to_all(norm_next, ALL, split_axis=0, concat_axis=0, tiled=True)[:, 0, 0])
    other = lax.ppermute(own, "core", [(0, 1), (1, 0)])
    both = jnp.where(core == 0, jnp.stack([own, other]), jnp.stack([other, own]))
    full = jnp.zeros((2, 4, N // 8, N), F32)
    full = lax.dynamic_update_slice(full, both[:, None], (0, xpos, 0, 0))
    for d in range(1, 4):
        got = lax.ppermute(both, "x", [(i, (i + d) % 4) for i in range(4)])
        full = lax.dynamic_update_slice(full, got[:, None], (0, (xpos + 4 - d) % 4, 0, 0))
    next_residual = full.reshape(ROWS, 2 * PLANES, N)
    next_image = image_t + step_size * direction_t
    next_direction = next_residual + norm_next / norm_now * direction_t
    return tuple(jnp.transpose(a, (0, 2, 1)) for a in (next_image, next_residual, next_direction))


def solution(mesh):
    fine = Mesh(mesh.devices.reshape(8, 4, 4, 2), ALL)
    rows = P(SLAB, None, None)
    return jax.shard_map(
        body,
        mesh=fine,
        in_specs=(
            rows,
            rows,
            rows,
            P(SLAB, None, COIL),
            P(SLAB, None, None, None, None),
            rows,
            rows,
        ),
        out_specs=(rows, rows, rows),
        check_vma=False,
    )
```

time: 780 us -> 276 us (0.35)
  waiting for transfers between devices: 393 us -> 134 us
  blocking collectives: 147 us -> 0 us
  matrix products: 121 us -> 0 us
  Pallas kernels: 0 us -> 47.7 us
  local copies, waits for them, and re-layouts: 47.3 us -> 8.34 us
  starting transfers between devices: 34.5 us -> 58.9 us
    all_to_all x4 -> x5, waiting for transfers between devices: 329 us -> 76.4 us  [the longest x2 75.6 us: body(): lax.all_to_all(outgoing, SLAB, split_axis=0, concat_axis=0, tiled=True)]
    psum x2 -> x0, blocking collectives: 147 us -> none  [the longest x1 74.7 us: body(): norm_next = lax.psum(jnp.sum(next_residual * next_residual), 'slab')]
    dot_general x20 -> x0, matrix products: 121 us -> none  [the longest x4 32.8 us: transform_axis(): jnp.einsum(pattern, imag_table, source, precision=lax.Precision.HIGHEST)]
    psum x1 -> x0, waiting for transfers between devices: 64 us -> none  [body(): applied = lax.psum(local_sum, 'coil')]
    pallas_call x0 -> x5, Pallas kernels: none -> 47.7 us  [the longest x1 14.4 us: backward_y(): pl.pallas_call(backward_y_kernel, in_specs=[vmem] * 4, out_specs=vmem, ou...]
    ppermute x0 -> x13, waiting for transfers between devices: none -> 30.1 us  [the longest x8 21.6 us: all_sum(): lax.ppermute(value, axis, [(i, i ^ step) for i in range(count)])]
    all_gather x0 -> x1, waiting for transfers between devices: none -> 27.4 us  [body(): grams = lax.all_gather(grams, COIL, axis=0, tiled=False)]
    ppermute x0 -> x13, starting transfers between devices: none -> 17.8 us  [the longest x8 12.9 us: all_sum(): lax.ppermute(value, axis, [(i, i ^ step) for i in range(count)])]
  transfers between devices with their start and end apart: 5 -> 19, of which waited for: 5 -> 15; matrix products, arithmetic and copies ran while one was open for 0% -> 3% of each run, Pallas kernels for 0% -> 5%
where the time goes in v1:
time: 276 us; the launch traced here: 274 us
  waiting for transfers between devices  134 us (49%)
  starting transfers between devices  58.9 us (21%)
  Pallas kernels  47.7 us (17%)
  between operations  17.5 us (6%)
  local copies, waits for them, and re-layouts  8.34 us (3%)
  other arithmetic  7.29 us (3%)
    all_to_all x2, waiting for transfers between devices, body(): lax.all_to_all(outgoing, SLAB, split_axis=0, concat_axis=0, tiled=True)  75.6 us
    all_gather x1, waiting for transfers between devices, body(): grams = lax.all_gather(grams, COIL, axis=0, tiled=False)  27.4 us
    ppermute x8, waiting for transfers between devices, all_sum(): lax.ppermute(value, axis, [(i, i ^ step) for i in range(count)])  21.6 us
    all_to_all x2, starting transfers between devices, body(): lax.all_to_all(outgoing, SLAB, split_axis=0, concat_axis=0, tiled=True)  16.4 us
    pallas_call x1, Pallas kernels, backward_y(): pl.pallas_call(backward_y_kernel, in_specs=[vmem] * 4, out_specs=vmem, ou...  14.4 us
    pallas_call x1, Pallas kernels, middle(): pl.pallas_call(middle_kernel, in_specs=[vmem] * 6, out_specs=[vmem, vmem]...  13.2 us
    ppermute x8, starting transfers between devices, all_sum(): lax.ppermute(value, axis, [(i, i ^ step) for i in range(count)])  12.9 us
    all_to_all x1, starting transfers between devices, body(): grams = lax.all_to_all(grams, SLAB, split_axis=0, concat_axis=0, tiled=True)  11.7 us
  transfers between devices with their start and end apart: 19, of which 15 were waited for; matrix products, arithmetic and copies ran while one was open for 3% of the time, Pallas kernels for 5%

profile of v1, /device:TPU:8, one launch (start us, length us, event | category | flops | bytes accessed | tf_op | source)
XLA Modules:
  0.0 273.5 jit_solution(18444733500178285189)
XLA Ops:
  8.6 7.1 %gram_rows.1 = f32[32,16,128]{2,1,0:T(8,128)} custom-call(s32[1]{0:T(128)} %bitcast.2.coil_ref, s32[128]{0:T(128)} %reshape_squeeze.7.counts_ref, f32[32,4,64,128]{3,2,1,0:T(8,128)} %bitcast.42), custom_call_target="tpu_custom_call" | custom-call | tf_op jit(solution)/shard_map/gram_rows/pallas_call | solution.py:127
  15.7 11.7 %all-to-all-start.1 = ((f32[32,16,128]{2,1,0:T(8,128)}), f32[32,16,128]{2,1,0:T(8,128)S(1)}, u32[]{:S(2)}, u32[]{:S(2)}) async-start(f32[32,16,128]{2,1,0:T(8,128)} %gram_rows.1), calls=%async_computation.1 | async-start | bytes 524288 | tf_op jit(solution)/shard_map/all_to_all | solution.py:317
  27.4 10.7 %forward_y.1 = f32[32,144,128]{2,1,0:T(8,128)} custom-call(f32[12,32,384]{2,1,0:T(8,128)} %bitcast.41, bf16[12,384,128]{2,1,0:T(8,128)(2,1)} %s_ref.3, bf16[768,384]{1,0:T(8,128)(2,1)} %constant.67.clone.th_ref.bh_ref, bf16[768,384]{1,0:T(8,128)(2,1)} %constant.68.clone.tl_ref.bl_ref), custom_call_target="tpu_custom_call" | custom-call | tf_op jit(solution)/shard_map/forward_y/pallas_call | solution.py:197
  38.6 9.3 %all-to-all-start = ((f32[32,144,128]{2,1,0:T(8,128)}), f32[32,144,128]{2,1,0:T(8,128)S(1)}, u32[]{:S(2)}, u32[]{:S(2)}) async-start(f32[32,144,128]{2,1,0:T(8,128)} %forward_y.1), calls=%async_computation | async-start | bytes 4718592 | tf_op jit(solution)/shard_map/all_to_all | solution.py:322
  48.7 2.2 gram_sum.1
  51.0 27.4 %all-gather.3.cloned.1.call-done = f32[2304,128]{1,0:T(8,128)} async-done(((f32[288,128]{1,0:T(8,128)}), f32[2304,128]{1,0:T(8,128)}) %all-gather.3.cloned.1.call-update) | async-done | bytes 1179664 | tf_op jit(solution)/shard_map/all_gather | solution.py:319
  78.3 23.9 %all-to-all-done = f32[32,144,128]{2,1,0:T(8,128)S(1)} async-done(((f32[32,144,128]{2,1,0:T(8,128)}), f32[32,144,128]{2,1,0:T(8,128)S(1)}, u32[]{:S(2)}, u32[]{:S(2)}) %all-to-all-start) | async-done | bytes 2359328 | tf_op jit(solution)/shard_map/all_to_all | solution.py:322
  103.6 13.2 %middle.1 = (f32[32,144,128]{2,1,0:T(8,128)}, f32[8,128]{1,0:T(8,128)}) custom-call(f32[4608,128]{1,0:T(8,128)} %bitcast.39, f32[8,288,128]{2,1,0:T(8,128)} %bitcast.47, bf16[768,384]{1,0:T(8,128)(2,1)} %constant.69.clone.fh_ref.th_ref, bf16[768,384]{1,0:T(8,128)(2,1)} %constant.70.clone.fl_ref.tl_ref, bf16[768,384]{1,0:T(8,128)(2,1)} %constant.67.clone.th_ref.bh_ref, ...), custom_call_target="tpu_custom_call" | custom-call | tf_op jit(solution)/shard_map/middle/pallas_call | solution.py:255
  116.8 7.1 %all-to-all-start.2 = ((f32[32,144,128]{2,1,0:T(8,128)}), f32[32,144,128]{2,1,0:T(8,128)S(1)}, u32[]{:S(2)}, u32[]{:S(2)}) async-start(f32[32,144,128]{2,1,0:T(8,128)} %get-tuple-element.6), calls=%async_computation.2 | async-start | bytes 4718592 | tf_op jit(solution)/shard_map/all_to_all | solution.py:327
  125.9 51.7 %all-to-all-done.2 = f32[32,144,128]{2,1,0:T(8,128)S(1)} async-done(((f32[32,144,128]{2,1,0:T(8,128)}), f32[32,144,128]{2,1,0:T(8,128)S(1)}, u32[]{:S(2)}, u32[]{:S(2)}) %all-to-all-start.2) | async-done | bytes 2359328 | tf_op jit(solution)/shard_map/all_to_all | solution.py:327
  179.1 14.4 %backward_y.1 = f32[12,32,384]{2,1,0:T(8,128)} custom-call(f32[4608,128]{1,0:T(8,128)} %bitcast.40, bf16[12,384,128]{2,1,0:T(8,128)(2,1)} %s_ref.3, bf16[768,384]{1,0:T(8,128)(2,1)} %constant.69.clone.fh_ref.th_ref, bf16[768,384]{1,0:T(8,128)(2,1)} %constant.70.clone.fl_ref.tl_ref), custom_call_target="tpu_custom_call" | custom-call | tf_op jit(solution)/shard_map/backward_y/pallas_call | solution.py:289
  200.2 4.0 %all-to-all-start.3 = ((f32[4,48,384]{2,1,0:T(8,128)}), f32[4,48,384]{2,1,0:T(8,128)S(1)}, u32[]{:S(2)}, u32[]{:S(2)}) async-start(f32[4,48,384]{2,1,0:T(8,128)} %bitcast.15), calls=%async_computation.3 | async-start | bytes 589824 | tf_op jit(solution)/shard_map/all_to_all | solution.py:337
  204.3 3.6 %collective-permute-start.2 = (f32[8,128]{1,0:T(8,128)S(1)}, f32[8,128]{1,0:T(8,128)S(1)}, u32[]{:S(2)}, u32[]{:S(2)}) collective-permute-start(f32[8,128]{1,0:T(8,128)S(1)} %fusion.2), channel_id=1, source_target_pairs={{0,4},{1,5},{2,6},{3,7},{4,0},{5,1},{6,2},{7,3},{8,12},{9,13},{10,... | collective-permute-start | bytes 12296 | tf_op jit(solution)/shard_map/ppermute | solution.py:302
  207.8 3.7 %collective-permute-done.2 = f32[8,128]{1,0:T(8,128)S(1)} collective-permute-done((f32[8,128]{1,0:T(8,128)S(1)}, f32[8,128]{1,0:T(8,128)S(1)}, u32[]{:S(2)}, u32[]{:S(2)}) %collective-permute-start.2) | collective-permute-done | bytes 4128 | tf_op jit(solution)/shard_map/ppermute | solution.py:302
  211.6 3.6 %collective-permute-done.3 = f32[8,128]{1,0:T(8,128)S(1)} collective-permute-done((f32[8,128]{1,0:T(8,128)S(1)}, f32[8,128]{1,0:T(8,128)S(1)}, u32[]{:S(2)}, u32[]{:S(2)}) %collective-permute-start.3) | collective-permute-done | bytes 4128 | tf_op jit(solution)/shard_map/ppermute | solution.py:302
  217.3 3.0 %collective-permute-done.4 = f32[8,128]{1,0:T(8,128)S(1)} collective-permute-done((f32[8,128]{1,0:T(8,128)S(1)}, f32[8,128]{1,0:T(8,128)S(1)}, u32[]{:S(2)}, u32[]{:S(2)}) %collective-permute-start.4) | collective-permute-done | bytes 4128 | tf_op jit(solution)/shard_map/ppermute | solution.py:302
  221.7 2.2 collective-permute-done.5
  225.4 3.0 %collective-permute-done.6 = f32[8,128]{1,0:T(8,128)S(1)} collective-permute-done((f32[8,128]{1,0:T(8,128)S(1)}, f32[8,128]{1,0:T(8,128)S(1)}, u32[]{:S(2)}, u32[]{:S(2)}) %collective-permute-start.6) | collective-permute-done | bytes 4128 | tf_op jit(solution)/shard_map/ppermute | solution.py:302
  228.4 2.3 collective-permute-start.7
  230.7 5.2 %collective-permute-done.7 = f32[8,128]{1,0:T(8,128)S(1)} collective-permute-done((f32[8,128]{1,0:T(8,128)S(1)}, f32[8,128]{1,0:T(8,128)S(1)}, u32[]{:S(2)}, u32[]{:S(2)}) %collective-permute-start.7) | collective-permute-done | bytes 4128 | tf_op jit(solution)/shard_map/ppermute | solution.py:302
  242.7 8.9 %all-to-all-start.4 = ((f32[256,1,128]{2,1,0:T(1,128)}), f32[256,1,128]{2,1,0:T(1,128)S(1)}, u32[]{:S(2)}, u32[]{:S(2)}) async-start(f32[256,1,128]{2,1,0:T(1,128)} %broadcast_in_dim.33), calls=%async_computation.4 | async-start | bytes 262144 | tf_op jit(solution)/shard_map/all_to_all | solution.py:342
  251.6 3.1 %collective-permute-start.11 = (f32[2,48,384]{2,1,0:T(8,128)S(1)}, f32[2,48,384]{2,1,0:T(8,128)S(1)}, u32[]{:S(2)}, u32[]{:S(2)}) collective-permute-start(f32[2,48,384]{2,1,0:T(8,128)S(1)} %maximum_select_fusion.1), channel_id=1, source_target_pairs={{0,4},{2,6},{4,0},{6,2},{1,5},{3,7},{5,1},{7,3},{8,12},{10,14},{12... | collective-permute-start | bytes 442376 | tf_op jit(solution)/shard_map/ppermute | solution.py:348
  256.0 4.0 %collective-permute-done.11 = f32[2,48,384]{2,1,0:T(8,128)S(1)} collective-permute-done((f32[2,48,384]{2,1,0:T(8,128)S(1)}, f32[2,48,384]{2,1,0:T(8,128)S(1)}, u32[]{:S(2)}, u32[]{:S(2)}) %collective-permute-start.11) | collective-permute-done | bytes 147488 | tf_op jit(solution)/shard_map/ppermute | solution.py:348
  260.0 3.2 %collective-permute-done.12 = f32[2,48,384]{2,1,0:T(8,128)S(1)} collective-permute-done((f32[2,48,384]{2,1,0:T(8,128)S(1)}, f32[2,48,384]{2,1,0:T(8,128)S(1)}, u32[]{:S(2)}, u32[]{:S(2)}) %collective-permute-start.12) | collective-permute-done | bytes 147488 | tf_op jit(solution)/shard_map/ppermute | solution.py:348
  (71 shorter events, 27.5 us)
Async XLA Ops:
  15.7 22.9 %all-to-all-start.1 = ((f32[32,16,128]{2,1,0:T(8,128)}), f32[32,16,128]{2,1,0:T(8,128)S(1)}, u32[]{:S(2)}, u32[]{:S(2)}) async-start(f32[32,16,128]{2,1,0:T(8,128)} %gram_rows.1), calls=%async_computation.1 | async-start | bytes 524288 | tf_op jit(solution)/shard_map/all_to_all | solution.py:317
  38.1 9.9 %copy-start.8 = (s32[1,32,4]{1,2,0:T(4,128)S(1)}, s32[1,32,4]{1,2,0:T(4,128)}, u32[]{:S(2)}) copy-start(s32[1,32,4]{1,2,0:T(4,128)} %param.16) | copy-start | bytes 1540
  38.6 9.5 %copy-start.4 = (f32[32,16,128]{2,1,0:T(8,128)}, f32[32,16,128]{2,1,0:T(8,128)S(1)}, u32[]{:S(2)}) copy-start(f32[32,16,128]{2,1,0:T(8,128)S(1)} %all-to-all-done.1.in_ref) | copy-start | bytes 786436
  38.6 63.6 %all-to-all-start = ((f32[32,144,128]{2,1,0:T(8,128)}), f32[32,144,128]{2,1,0:T(8,128)S(1)}, u32[]{:S(2)}, u32[]{:S(2)}) async-start(f32[32,144,128]{2,1,0:T(8,128)} %forward_y.1), calls=%async_computation | async-start | bytes 4718592 | tf_op jit(solution)/shard_map/all_to_all | solution.py:322
  47.9 30.4 %all-gather.3.cloned.1.call-start = ((), (), s32[]{:S(2)}) async-start(), calls=%async_computation.5 | async-start | bytes 1327104 | tf_op jit(solution)/shard_map/all_gather | solution.py:319
  116.8 8.5 %copy-start.7 = (f32[8,128]{1,0:T(8,128)S(1)}, f32[8,128]{1,0:T(8,128)}, u32[]{:S(2)}) copy-start(f32[8,128]{1,0:T(8,128)} %get-tuple-element.5) | copy-start | bytes 12292
  116.8 60.8 %all-to-all-start.2 = ((f32[32,144,128]{2,1,0:T(8,128)}), f32[32,144,128]{2,1,0:T(8,128)S(1)}, u32[]{:S(2)}, u32[]{:S(2)}) async-start(f32[32,144,128]{2,1,0:T(8,128)} %get-tuple-element.6), calls=%async_computation.2 | async-start | bytes 4718592 | tf_op jit(solution)/shard_map/all_to_all | solution.py:327
  193.5 46.9 %copy-start.2 = (f32[12,384,32]{1,2,0:T(8,128)S(1)}, f32[12,384,32]{1,2,0:T(8,128)}, u32[]{:S(2)}) copy-start(f32[12,384,32]{1,2,0:T(8,128)} %param.13) | copy-start | bytes 1769476
  193.5 46.9 %copy-start.6 = (f32[12,384,32]{1,2,0:T(8,128)S(1)}, f32[12,384,32]{1,2,0:T(8,128)}, u32[]{:S(2)}) copy-start(f32[12,384,32]{1,2,0:T(8,128)} %param.11) | copy-start | bytes 1769476
  194.6 3.9 %collective-permute-start.8 = (f32[192,384]{1,0:T(8,128)S(1)}, f32[192,384]{1,0:T(8,128)S(1)}, u32[]{:S(2)}, u32[]{:S(2)}) collective-permute-start(f32[192,384]{1,0:T(8,128)S(1)} %dynamic-slice_bitcast_fusion), channel_id=1, source_target_pairs={{0,1},{1,0},{2,3},{3,2},{4,5},{5,4},{6,7},{7,6},{8,9},{9,8},{10,11... | collective-permute-start | bytes 884744 | tf_op jit(solution)/shard_map/ppermute | solution.py:336
  195.6 1.3 collective-permute-start
  197.0 7.2 %collective-permute-start.1 = (f32[8,128]{1,0:T(8,128)S(1)}, f32[8,128]{1,0:T(8,128)S(1)}, u32[]{:S(2)}, u32[]{:S(2)}) collective-permute-start(f32[8,128]{1,0:T(8,128)S(1)} %broadcast_add_fusion), channel_id=1, source_target_pairs={{0,2},{1,3},{2,0},{3,1},{4,6},{5,7},{6,4},{7,5},{8,10},{9,11},{10,... | collective-permute-start | bytes 12296 | tf_op jit(solution)/shard_map/ppermute | solution.py:302
  200.2 37.6 %all-to-all-start.3 = ((f32[4,48,384]{2,1,0:T(8,128)}), f32[4,48,384]{2,1,0:T(8,128)S(1)}, u32[]{:S(2)}, u32[]{:S(2)}) async-start(f32[4,48,384]{2,1,0:T(8,128)} %bitcast.15), calls=%async_computation.3 | async-start | bytes 589824 | tf_op jit(solution)/shard_map/all_to_all | solution.py:337
  204.3 7.3 %collective-permute-start.2 = (f32[8,128]{1,0:T(8,128)S(1)}, f32[8,128]{1,0:T(8,128)S(1)}, u32[]{:S(2)}, u32[]{:S(2)}) collective-permute-start(f32[8,128]{1,0:T(8,128)S(1)} %fusion.2), channel_id=1, source_target_pairs={{0,4},{1,5},{2,6},{3,7},{4,0},{5,1},{6,2},{7,3},{8,12},{9,13},{10,... | collective-permute-start | bytes 12296 | tf_op jit(solution)/shard_map/ppermute | solution.py:302
  211.6 3.6 %collective-permute-start.3 = (f32[8,128]{1,0:T(8,128)S(1)}, f32[8,128]{1,0:T(8,128)S(1)}, u32[]{:S(2)}, u32[]{:S(2)}) collective-permute-start(f32[8,128]{1,0:T(8,128)S(1)} %add.88), channel_id=1, source_target_pairs={{0,8},{8,0},{16,24},{24,16},{32,40},{40,32},{48,56},{56,48},{64,72... | collective-permute-start | bytes 12296 | tf_op jit(solution)/shard_map/ppermute | solution.py:302
  215.2 5.1 %collective-permute-start.4 = (f32[8,128]{1,0:T(8,128)S(1)}, f32[8,128]{1,0:T(8,128)S(1)}, u32[]{:S(2)}, u32[]{:S(2)}) collective-permute-start(f32[8,128]{1,0:T(8,128)S(1)} %add.89), channel_id=1, source_target_pairs={{0,16},{8,24},{16,0},{24,8},{32,48},{40,56},{48,32},{56,40},{64,80... | collective-permute-start | bytes 12296 | tf_op jit(solution)/shard_map/ppermute | solution.py:302
  220.3 3.6 %collective-permute-start.5 = (f32[8,128]{1,0:T(8,128)S(1)}, f32[8,128]{1,0:T(8,128)S(1)}, u32[]{:S(2)}, u32[]{:S(2)}) collective-permute-start(f32[8,128]{1,0:T(8,128)S(1)} %add.90), channel_id=1, source_target_pairs={{0,32},{8,40},{16,48},{24,56},{32,0},{40,8},{48,16},{56,24},{64,96... | collective-permute-start | bytes 12296 | tf_op jit(solution)/shard_map/ppermute | solution.py:302
  223.9 4.5 %collective-permute-start.6 = (f32[8,128]{1,0:T(8,128)S(1)}, f32[8,128]{1,0:T(8,128)S(1)}, u32[]{:S(2)}, u32[]{:S(2)}) collective-permute-start(f32[8,128]{1,0:T(8,128)S(1)} %add.91), channel_id=1, source_target_pairs={{0,64},{8,72},{16,80},{24,88},{32,96},{40,104},{48,112},{56,120},{... | collective-permute-start | bytes 12296 | tf_op jit(solution)/shard_map/ppermute | solution.py:302
  228.4 7.5 %collective-permute-start.7 = (f32[8,128]{1,0:T(8,128)S(1)}, f32[8,128]{1,0:T(8,128)S(1)}, u32[]{:S(2)}, u32[]{:S(2)}) collective-permute-start(f32[8,128]{1,0:T(8,128)S(1)} %add.92), channel_id=1, source_target_pairs={{0,128},{8,136},{16,144},{24,152},{32,160},{40,168},{48,176},{56,1... | collective-permute-start | bytes 12296 | tf_op jit(solution)/shard_map/ppermute | solution.py:302
  238.5 1.3 collective-permute-start.9
  239.8 16.2 %collective-permute-start.10 = (f32[2,48,384]{2,1,0:T(8,128)S(1)}, f32[2,48,384]{2,1,0:T(8,128)S(1)}, u32[]{:S(2)}, u32[]{:S(2)}) collective-permute-start(f32[2,48,384]{2,1,0:T(8,128)S(1)} %maximum_select_fusion.1), channel_id=1, source_target_pairs={{0,2},{2,4},{4,6},{6,0},{1,3},{3,5},{5,7},{7,1},{8,10},{10,12},{12... | collective-permute-start | bytes 442376 | tf_op jit(solution)/shard_map/ppermute | solution.py:348
  242.7 20.9 %all-to-all-start.4 = ((f32[256,1,128]{2,1,0:T(1,128)}), f32[256,1,128]{2,1,0:T(1,128)S(1)}, u32[]{:S(2)}, u32[]{:S(2)}) async-start(f32[256,1,128]{2,1,0:T(1,128)} %broadcast_in_dim.33), calls=%async_computation.4 | async-start | bytes 262144 | tf_op jit(solution)/shard_map/all_to_all | solution.py:342
  251.6 8.3 %collective-permute-start.11 = (f32[2,48,384]{2,1,0:T(8,128)S(1)}, f32[2,48,384]{2,1,0:T(8,128)S(1)}, u32[]{:S(2)}, u32[]{:S(2)}) collective-permute-start(f32[2,48,384]{2,1,0:T(8,128)S(1)} %maximum_select_fusion.1), channel_id=1, source_target_pairs={{0,4},{2,6},{4,0},{6,2},{1,5},{3,7},{5,1},{7,3},{8,12},{10,14},{12... | collective-permute-start | bytes 442376 | tf_op jit(solution)/shard_map/ppermute | solution.py:348
  254.7 8.5 %collective-permute-start.12 = (f32[2,48,384]{2,1,0:T(8,128)S(1)}, f32[2,48,384]{2,1,0:T(8,128)S(1)}, u32[]{:S(2)}, u32[]{:S(2)}) collective-permute-start(f32[2,48,384]{2,1,0:T(8,128)S(1)} %maximum_select_fusion.1), channel_id=1, source_target_pairs={{0,6},{2,0},{4,2},{6,4},{1,7},{3,1},{5,3},{7,5},{8,14},{10,8},{12,... | collective-permute-start | bytes 442376 | tf_op jit(solution)/shard_map/ppermute | solution.py:348
  (4 other events, 13.4 us)
Sparse Core Ops, SparseCore 0:
  51.2 27.0 all-gather.2

commit v2 on v1

v2 whole, which is shorter than its diff:
```python
import jax
import jax.numpy as jnp
import ml_dtypes
import numpy as np
from jax import lax
from jax.experimental import pallas as pl
from jax.experimental.pallas import tpu as pltpu
from jax.sharding import Mesh
from jax.sharding import PartitionSpec as P

N = 384
SLABS = 32
ROWS = 12
PAIRS = ROWS // 2
LANES = 128
PLANES = 16
TX = 16
TY = 4
CELLS = TX * TY
TILES = 72
CAP = 4
SB = 128
SLAB = ("z", "y")
COIL = ("x", "core")
ALL = ("z", "y", "x", "core")
HALF_ROWS = PAIRS * 2 * PLANES
BLOCK = 24 * PAIRS
HALF = LANES // 2
COILS = HALF // PLANES
VMEM_LIMIT = 56 * 1024 * 1024
F32 = jnp.float32
BF16 = jnp.bfloat16
NT = (((1,), (1,)), ((), ()))


def split_table(table):
    table = table.astype(np.float32)
    high = table.astype(ml_dtypes.bfloat16)
    low = (table - high.astype(np.float32)).astype(ml_dtypes.bfloat16)
    return high, low


def dft_tables():
    pos = np.arange(N)
    phase = (pos[:, None] * pos[None, :] % N) * (2.0 * np.pi / N)
    real = np.cos(phase) / np.sqrt(N)
    imag = -np.sin(phase) / np.sqrt(N)
    base = ROWS * np.arange(SLABS)[:, None]
    rows = np.concatenate([(base + np.arange(8)).reshape(-1), (base + np.arange(8, ROWS)).reshape(-1)])
    cols = np.concatenate([base.reshape(-1) + 2 * p + i for i in range(2) for p in range(PAIRS)])
    sending = [split_table(np.concatenate([real[rows], sign * imag[rows]], axis=1)) for sign in (1, -1)]
    arrival = [split_table(np.concatenate([real[:, cols], sign * imag[:, cols]], axis=1)) for sign in (1, -1)]
    return sending, arrival


def selections():
    place = np.arange(LANES)
    part, coil, plane = place // HALF, place // PLANES % COILS, place % PLANES
    group, src_part, src_plane = place // (2 * PLANES), place // PLANES % 2, place % PLANES
    same = (group[:, None] == coil) & (src_plane[:, None] == plane)
    maps = np.concatenate([same & (src_part[:, None] == 0), same & (src_part[:, None] == 1)], axis=1)
    spread, gather = [], []
    for r in range(4):
        hit = (group[:, None] == r) & (src_plane[:, None] == plane)
        from_real = hit & (src_part[:, None] == 0)
        from_imag = hit & (src_part[:, None] == 1)
        spread.append((from_real & (part == 0)) + (from_imag & (part == 1)) + 0.0)
        spread.append((from_real & (part == 1)) + 0.0 - (from_imag & (part == 0)))
        gather.append((group == r) & (src_plane == plane[:, None]) & (src_part == part[:, None]))
    spread = np.concatenate([np.concatenate(spread, axis=1)] * 2, axis=0)
    gather = np.concatenate(gather * 2, axis=0)
    return tuple(a.astype(ml_dtypes.bfloat16) for a in (maps, spread, gather))


def split(value):
    high = value.astype(BF16)
    return high, (value - high.astype(F32)).astype(BF16)


def dot(a, b):
    return jnp.dot(a, b, preferred_element_type=F32)


def dot_nt(a, b):
    return lax.dot_general(a, b, NT, preferred_element_type=F32)


def whole(array):
    return pl.BlockSpec(array.shape, lambda i: (0,) * array.ndim)


def times_i(value):
    rolled = pltpu.roll(value, HALF, 1)
    return jnp.where(lax.broadcasted_iota(jnp.int32, value.shape, 1) < HALF, -rolled, rolled)


def transform(high_ref, low_ref, pieces, turned):
    highs, lows = [], []
    for piece, turn in zip(pieces, turned):
        piece_high, piece_low = split(piece)
        turn_high, turn_low = split(turn)
        highs.append(jnp.concatenate([piece_high, turn_high], axis=0))
        lows.append(jnp.concatenate([piece_low, turn_low], axis=0))
    high = jnp.concatenate(highs, axis=1)
    low = jnp.concatenate(lows, axis=1)
    return dot(high_ref[...], high) + (dot(high_ref[...], low) + dot(low_ref[...], high))


def store_outgoing(out_ref, start, even, odd):
    out_ref[:, start:start + 8, :] = even[:256].reshape(SLABS, 8, LANES)
    out_ref[:, start + 8:start + 16, :] = odd[:256].reshape(SLABS, 8, LANES)
    lower = lax.broadcasted_iota(jnp.int32, (8, LANES), 0) < 4
    for m in range(SLABS // 2):
        first = even[256 + 8 * m:264 + 8 * m]
        second = odd[256 + 8 * m:264 + 8 * m]
        out_ref[2 * m, start + 16:start + 24, :] = jnp.where(lower, first, pltpu.roll(second, 4, 0))
        out_ref[2 * m + 1, start + 16:start + 24, :] = jnp.where(lower, pltpu.roll(first, 4, 0), second)


def gram_sum_kernel(tiles_ref, in_ref, out_ref, total):
    total[...] = jnp.zeros_like(total)
    lane = lax.broadcasted_iota(jnp.int32, (8, LANES), 1)

    def add(r, carry):
        for j in range(CAP):
            tile = tiles_ref[j, r]
            piece = in_ref[r, 8 * (j // 2):8 * (j // 2) + 8, :]
            keep = lane < CELLS if j % 2 == 0 else lane >= CELLS
            total[tile] = total[tile] + jnp.where(keep, piece, 0.0)
        return carry

    lax.fori_loop(0, SLABS, add, 0)
    groups = N // TX // 2
    for b in range(ROWS // TY):
        for m in range(groups):
            first = total[2 * m * 3 + b]
            second = total[(2 * m + 1) * 3 + b]
            first = first + pltpu.roll(first, CELLS, 1)
            second = second + pltpu.roll(second, CELLS, 1)
            at = (b * groups + m) * 8
            out_ref[at:at + 8, :] = jnp.where(lane < CELLS, first, second)


def gram_sum(arrived, tiles):
    return pl.pallas_call(
        gram_sum_kernel,
        in_specs=[pl.BlockSpec(memory_space=pltpu.SMEM), pl.BlockSpec(memory_space=pltpu.VMEM)],
        out_specs=pl.BlockSpec(memory_space=pltpu.VMEM),
        out_shape=jax.ShapeDtypeStruct((TILES // 2 * 8, LANES), F32),
        scratch_shapes=[pltpu.VMEM((TILES, 8, LANES), F32)],
        compiler_params=pltpu.CompilerParams(vmem_limit_bytes=VMEM_LIMIT),
        name="gram_sum",
    )(tiles, arrived)


def forward_y_kernel(d_ref, s_ref, maps_ref, spread_ref, high_ref, low_ref, out_ref):
    flipped = d_ref[...].reshape(LANES, N).T
    wide = dot(jnp.concatenate(split(flipped), axis=1), spread_ref[...])
    for p in range(2):
        images, turned = [], []
        for r in (2 * p, 2 * p + 1):
            maps = dot(s_ref[r], maps_ref[...])
            real_map, imag_map = maps[:, :LANES], maps[:, LANES:]
            d = wide[:, 2 * r * LANES:(2 * r + 1) * LANES]
            turned_d = wide[:, (2 * r + 1) * LANES:(2 * r + 2) * LANES]
            images.append(real_map * d + imag_map * turned_d)
            turned.append(real_map * turned_d - imag_map * d)
        done = transform(high_ref, low_ref, images, turned)
        store_outgoing(out_ref, 24 * p, done[:, :LANES], done[:, LANES:])


def forward_y(direction, maps, sel_maps, sel_spread, table):
    return pl.pallas_call(
        forward_y_kernel,
        grid=(ROWS // 4,),
        in_specs=[
            pl.BlockSpec((4, 2 * PLANES, N), lambda i: (i, 0, 0)),
            pl.BlockSpec((4, N, LANES), lambda i: (i, 0, 0)),
            whole(sel_maps),
            whole(sel_spread),
            whole(table[0]),
            whole(table[1]),
        ],
        out_specs=pl.BlockSpec((SLABS, 48, LANES), lambda i: (0, i, 0)),
        out_shape=jax.ShapeDtypeStruct((SLABS, 24 * PAIRS, LANES), F32),
        compiler_params=pltpu.CompilerParams(vmem_limit_bytes=VMEM_LIMIT),
        name="forward_y",
    )(direction, maps, sel_maps, sel_spread, *table)


def arrived_rows(ref, index, block):
    parts = []
    for i in range(2):
        start = i * 8 + index if index < 8 else 16 + 4 * i + index - 8
        parts += [ref[pl.ds(start + 24 * p, SLABS, stride=block), :] for p in range(PAIRS)]
    return jnp.concatenate(parts, axis=0)


def middle_kernel(norm_ref, in_ref, *rest):
    g_refs = rest[:8]
    fh_ref, fl_ref, bh_ref, bl_ref, out_ref, grid_ref, g_ref = rest[8:]
    xpos, core = lax.axis_index("x"), lax.axis_index("core")
    for d in range(4):
        x = lax.rem(xpos + 4 - d, 4)
        for k in range(2):
            g_ref[2 * x + lax.rem(core + k, 2)] = g_refs[4 * k + d][...]
    for p in range(PAIRS):
        pieces = [arrived_rows(in_ref, 2 * p + i, BLOCK) for i in range(2)]
        done = transform(fh_ref, fl_ref, pieces, [times_i(x) for x in pieces])
        for i in range(2):
            b = 2 * p + i
            grid_ref[b // TY, pl.ds(b % TY, N, stride=TY), :] = done[:, LANES * i:LANES * (i + 1)]
    left = lax.broadcasted_iota(jnp.int32, (CELLS, LANES), 1) < CELLS
    curve = jnp.zeros((8, LANES), F32)
    groups = N // TX // 2
    for b in range(ROWS // TY):
        for m in range(groups):
            at = (b * groups + m) * 8
            packed = jnp.concatenate([g_ref[c, at:at + 8, :] for c in range(8)], axis=0)
            weights = jnp.concatenate([jnp.where(left, packed, 0.0), jnp.where(left, 0.0, packed)], axis=0)
            cells = slice(2 * m * CELLS, (2 * m + 2) * CELLS)
            tile = grid_ref[b, cells, :]
            w_high, w_low = split(weights)
            t_high, t_low = split(tile)
            applied = dot(jnp.concatenate([w_high, w_low], axis=1), jnp.concatenate([t_high, t_high], axis=0))
            applied = applied + dot(w_high, t_low)
            curve = curve + jnp.sum((tile * applied).reshape(2 * CELLS // 8, 8, LANES), axis=0)
            grid_ref[b, cells, :] = applied
    norm = jnp.broadcast_to(norm_ref[...], (8, LANES)) / (8 * LANES)
    sums = jnp.where(lax.broadcasted_iota(jnp.int32, (8, LANES), 0) == 0, jnp.sum(curve, axis=0, keepdims=True), norm)
    out_ref[:, BLOCK:, :] = jnp.broadcast_to(sums[None], (SLABS, 8, LANES))
    for p in range(PAIRS):
        pieces = [grid_ref[b // TY, pl.ds(b % TY, N, stride=TY), :] for b in (2 * p, 2 * p + 1)]
        done = transform(bh_ref, bl_ref, pieces, [times_i(x) for x in pieces])
        store_outgoing(out_ref, 24 * p, done[:, :LANES], done[:, LANES:])


def middle(norm, arrived, grams, table_in, table_out):
    vmem = pl.BlockSpec(memory_space=pltpu.VMEM)
    return pl.pallas_call(
        middle_kernel,
        in_specs=[vmem] * 14,
        out_specs=vmem,
        out_shape=jax.ShapeDtypeStruct((SLABS, BLOCK + 8, LANES), F32),
        scratch_shapes=[
            pltpu.VMEM((ROWS // TY, N * TY, LANES), F32),
            pltpu.VMEM((8, TILES // 2 * 8, LANES), F32),
        ],
        compiler_params=pltpu.CompilerParams(vmem_limit_bytes=VMEM_LIMIT),
        name="middle",
    )(norm, arrived, *grams, *table_in, *table_out)


def backward_y_kernel(in_ref, s_ref, maps_ref, gather_ref, high_ref, low_ref, kept_ref, sent_ref):
    core = lax.axis_index("core")
    block = BLOCK + 8
    curve = jnp.sum(in_ref[pl.ds(BLOCK, SLABS, stride=block), :], axis=0, keepdims=True)
    norm = jnp.sum(in_ref[pl.ds(BLOCK + 1, SLABS, stride=block), :], axis=0, keepdims=True)
    sums = jnp.where(lax.broadcasted_iota(jnp.int32, (8, LANES), 0) == 0, curve, norm)
    sums = jnp.concatenate([sums] + [jnp.zeros_like(sums)] * (N // LANES - 1), axis=1)
    kept_ref[HALF_ROWS:, :] = sums
    sent_ref[HALF_ROWS:, :] = sums
    for g in range(ROWS // 4):
        highs, lows = [], []
        for p in range(2):
            rows = [4 * g + 2 * p + i for i in range(2)]
            pieces = [arrived_rows(in_ref, r, block) for r in rows]
            done = transform(high_ref, low_ref, pieces, [times_i(x) for x in pieces])
            for i in range(2):
                back = done[:, LANES * i:LANES * (i + 1)]
                maps = dot(s_ref[rows[i]], maps_ref[...])
                high, low = split(maps[:, :LANES] * back - maps[:, LANES:] * times_i(back))
                highs.append(high)
                lows.append(low)
        total = dot(jnp.concatenate(highs + lows, axis=1), gather_ref[...]).T
        for r in range(4):
            a = 4 * g + r
            at = a % PAIRS * 2 * PLANES
            rows = total[2 * PLANES * r:2 * PLANES * (r + 1), :]

            @pl.when(core == a // PAIRS)
            def _():
                kept_ref[at:at + 2 * PLANES, :] = rows

            @pl.when(core != a // PAIRS)
            def _():
                sent_ref[at:at + 2 * PLANES, :] = rows


def backward_y(arrived, maps, sel_maps, sel_gather, table):
    vmem = pl.BlockSpec(memory_space=pltpu.VMEM)
    half = jax.ShapeDtypeStruct((HALF_ROWS + 8, N), F32)
    return pl.pallas_call(
        backward_y_kernel,
        in_specs=[vmem] * 6,
        out_specs=[vmem, vmem],
        out_shape=[half, half],
        compiler_params=pltpu.CompilerParams(vmem_limit_bytes=VMEM_LIMIT),
        name="backward_y",
    )(arrived, maps, sel_maps, sel_gather, *table)


def gram_kernel(counts_ref, w_ref, out_ref):
    step = pl.program_id(0)
    owners = w_ref.shape[0]
    at = pl.multiple_of((lax.axis_index("x") * 2 + lax.axis_index("core")) * 8, 8)
    lane = lax.broadcasted_iota(jnp.int32, (8, SB), 1)
    for o in range(owners):
        rows = []
        for j in range(CAP):
            live = counts_ref[j, step * owners + o]
            rows.append(jnp.where(lane < live, w_ref[o, j, pl.ds(at, 8), :], 0.0))
        l_high, l_low = split(jnp.concatenate(rows, axis=0))
        r_high, r_low = split(w_ref[o].reshape(CAP * CELLS, SB))
        gram = dot_nt(jnp.concatenate([l_high, l_low], axis=1), jnp.concatenate([r_high, r_high], axis=1))
        gram = gram + dot_nt(l_high, r_low)
        for m in range(CAP // 2):
            first = gram[16 * m:16 * m + 8, LANES * m:LANES * (m + 1)]
            second = gram[16 * m + 8:16 * m + 16, LANES * m:LANES * (m + 1)]
            out_ref[o, 8 * m:8 * m + 8, :] = jnp.where(lane < CELLS, first, second)


def gram_rows(interp, counts):
    owners = 8
    return pl.pallas_call(
        gram_kernel,
        grid=(SLABS // owners,),
        in_specs=[pl.BlockSpec(memory_space=pltpu.SMEM), pl.BlockSpec((owners, CAP, CELLS, SB), lambda i: (i, 0, 0, 0))],
        out_specs=pl.BlockSpec((owners, 16, LANES), lambda i: (i, 0, 0)),
        out_shape=jax.ShapeDtypeStruct((SLABS, 16, LANES), F32),
        compiler_params=pltpu.CompilerParams(vmem_limit_bytes=VMEM_LIMIT),
        name="gram_rows",
    )(counts, interp)


def share_kernel(own_ref, a_ref, b_ref, c_ref, residual_ref, out_ref, part_ref, sums_ref):
    total = (own_ref[...] + a_ref[...]) + (b_ref[...] + c_ref[...])
    curvature = jnp.sum(total[HALF_ROWS:HALF_ROWS + 1, :LANES], axis=1, keepdims=True)
    norm_now = jnp.sum(total[HALF_ROWS + 1:HALF_ROWS + 2, :LANES], axis=1, keepdims=True)
    step = norm_now / curvature
    half = residual_ref[lax.axis_index("core")] - step * total[:HALF_ROWS]
    out_ref[...] = half
    square = jnp.sum((half * half).reshape(HALF_ROWS // 8, 8, N), axis=0)
    part = jnp.sum(square[:, :LANES] + square[:, LANES:2 * LANES] + square[:, 2 * LANES:], axis=0, keepdims=True)
    part_ref[...] = jnp.broadcast_to(part[None], part_ref.shape)
    sums_ref[...] = jnp.where(lax.broadcasted_iota(jnp.int32, (8, LANES), 0) == 0, step, norm_now)


def residual_share(own, others, residual):
    vmem = pl.BlockSpec(memory_space=pltpu.VMEM)
    return pl.pallas_call(
        share_kernel,
        in_specs=[vmem] * 5,
        out_specs=[vmem] * 3,
        out_shape=[
            jax.ShapeDtypeStruct((HALF_ROWS, N), F32),
            jax.ShapeDtypeStruct((2 * SLABS, 1, LANES), F32),
            jax.ShapeDtypeStruct((8, LANES), F32),
        ],
        compiler_params=pltpu.CompilerParams(vmem_limit_bytes=VMEM_LIMIT),
        name="residual_share",
    )(own, *others, residual)


def image_kernel(sums_ref, image_ref, direction_ref, out_ref):
    out_ref[...] = image_ref[...] + sums_ref[0:1, 0:1] * direction_ref[...]


def image_update(sums, image, direction):
    vmem = pl.BlockSpec(memory_space=pltpu.VMEM)
    return pl.pallas_call(
        image_kernel,
        in_specs=[vmem] * 3,
        out_specs=vmem,
        out_shape=jax.ShapeDtypeStruct(image.shape, F32),
        name="image_update",
    )(sums, image, direction)


def finish_kernel(sums_ref, parts_ref, direction_ref, own_ref, other_ref, residual_ref, next_ref):
    ratio = jnp.sum(jnp.sum(parts_ref[...], axis=0), axis=1, keepdims=True) / sums_ref[1:2, 0:1]
    core = lax.axis_index("core")
    for half, ref in ((core, own_ref), (1 - core, other_ref)):
        residual_ref[half] = ref[...]
        next_ref[half] = ref[...] + ratio * direction_ref[half]


def finish(sums, parts, direction, own, other):
    vmem = pl.BlockSpec(memory_space=pltpu.VMEM)
    full = jax.ShapeDtypeStruct(direction.shape, F32)
    return pl.pallas_call(
        finish_kernel,
        in_specs=[vmem] * 5,
        out_specs=[vmem, vmem],
        out_shape=[full, full],
        compiler_params=pltpu.CompilerParams(vmem_limit_bytes=VMEM_LIMIT),
        name="finish",
    )(sums, parts, direction, own, other)


def swap_core(value):
    return lax.ppermute(value, "core", [(0, 1), (1, 0)])


def from_x(value):
    return [lax.ppermute(value, "x", [(i, (i + d) % 4) for i in range(4)]) for d in range(1, 4)]


def body(image_x, residual, direction, sensitivity, interp, slot_tile, counts):
    sending, arrival = ([tuple(jnp.asarray(t) for t in pair) for pair in pairs] for pairs in dft_tables())
    sel_maps, sel_spread, sel_gather = (jnp.asarray(t) for t in selections())
    image_t, residual_t, direction_t = (jnp.transpose(a, (0, 2, 1)) for a in (image_x, residual, direction))

    grams = gram_rows(interp[0], counts[0].T)
    grams = lax.all_to_all(grams, SLAB, split_axis=0, concat_axis=0, tiled=True)
    grams = gram_sum(grams, slot_tile[0].T)
    grams = [grams] + from_x(grams)
    grams = grams + [swap_core(g) for g in grams]

    outgoing = forward_y(direction_t, sensitivity, sel_maps, sel_spread, sending[0])
    pencils = lax.all_to_all(outgoing, SLAB, split_axis=0, concat_axis=0, tiled=True)
    norm = jnp.sum(residual_t * residual_t).reshape(1, 1)
    outgoing = middle(norm, pencils.reshape(-1, LANES), grams, arrival[0], sending[1])
    slab_rows = lax.all_to_all(outgoing, SLAB, split_axis=0, concat_axis=0, tiled=True)
    kept, sent = backward_y(slab_rows.reshape(-1, LANES), sensitivity, sel_maps, sel_gather, arrival[1])

    kept = kept + swap_core(sent)
    halves = (2, HALF_ROWS, N)
    half, parts, sums = residual_share(kept, from_x(kept), residual_t.reshape(halves))
    parts = lax.all_to_all(parts, SLAB + ("core",), split_axis=0, concat_axis=0, tiled=True)
    next_image = image_update(sums, image_t.reshape(halves), direction_t.reshape(halves))
    next_residual, next_direction = finish(sums, parts, direction_t.reshape(halves), half, swap_core(half))
    return tuple(
        jnp.transpose(a.reshape(direction_t.shape), (0, 2, 1)) for a in (next_image, next_residual, next_direction)
    )


def solution(mesh):
    fine = Mesh(mesh.devices.reshape(8, 4, 4, 2), ALL)
    rows = P(SLAB, None, None)
    return jax.shard_map(
        body,
        mesh=fine,
        in_specs=(
            rows,
            rows,
            rows,
            P(SLAB, None, COIL),
            P(SLAB, None, None, None, None),
            rows,
            rows,
        ),
        out_specs=(rows, rows, rows),
        check_vma=False,
    )
```

time: 276 us -> 223 us (0.81)
  blocking collectives: 0 us -> 64.4 us
  waiting for transfers between devices: 134 us -> 72.6 us
  starting transfers between devices: 58.9 us -> 33.3 us
  between operations: 17.5 us -> 0.73 us
  other arithmetic: 7.29 us -> 1.75 us
  Pallas kernels: 47.7 us -> 42.7 us
  local copies, waits for them, and re-layouts: 8.34 us -> 4.82 us
    all_to_all x0 -> x1, blocking collectives: none -> 64.4 us  [body(): lax.all_to_all(outgoing, SLAB, split_axis=0, concat_axis=0, tiled=True)]
    all_to_all x2 -> x1, waiting for transfers between devices: 75.6 us -> 38 us  [body(): lax.all_to_all(outgoing, SLAB, split_axis=0, concat_axis=0, tiled=True)]
    all_gather x1 -> x0, waiting for transfers between devices: 27.4 us -> none  [body(): grams = lax.all_gather(grams, COIL, axis=0, tiled=False)]
    all_to_all x2 -> x1, starting transfers between devices: 16.4 us -> 6.36 us  [body(): lax.all_to_all(outgoing, SLAB, split_axis=0, concat_axis=0, tiled=True)]
    ppermute x13 -> x12, starting transfers between devices: 17.8 us -> 9.22 us  [the longest x6 9.19 us: from_x(): lax.ppermute(value, 'x', [(i, (i + d) % 4) for i in range(4)])]
    all_to_all x2 -> x1, starting transfers between devices: 12.9 us -> 6.07 us  [body(): lax.all_to_all(parts, SLAB + ('core',), split_axis=0, concat_axis=0, tile...]
    all_to_all x2 -> x1, waiting for transfers between devices: 0.33 us -> 6.38 us  [body(): lax.all_to_all(parts, SLAB + ('core',), split_axis=0, concat_axis=0, tile...]
    ppermute x13 -> x12, waiting for transfers between devices: 30.1 us -> 24.6 us  [the longest x6 22.8 us: from_x(): lax.ppermute(value, 'x', [(i, (i + d) % 4) for i in range(4)])]
  transfers between devices with their start and end apart: 19 -> 15, of which waited for: 15 -> 9; matrix products, arithmetic and copies ran while one was open for 3% -> 0% of each run, Pallas kernels for 5% -> 5%
where the time goes in v2:
time: 223 us; the launch traced here: 220 us
  waiting for transfers between devices  72.6 us (33%)
  blocking collectives  64.4 us (29%)
  Pallas kernels  42.7 us (19%)
  starting transfers between devices  33.3 us (15%)
  local copies, waits for them, and re-layouts  4.82 us (2%)
    all_to_all x1, blocking collectives, body(): lax.all_to_all(outgoing, SLAB, split_axis=0, concat_axis=0, tiled=True)  64.4 us
    all_to_all x1, waiting for transfers between devices, body(): lax.all_to_all(outgoing, SLAB, split_axis=0, concat_axis=0, tiled=True)  38 us
    ppermute x6, waiting for transfers between devices, from_x(): lax.ppermute(value, 'x', [(i, (i + d) % 4) for i in range(4)])  22.8 us
    pallas_call x1, Pallas kernels, middle(): pl.pallas_call(middle_kernel, in_specs=[vmem] * 14, out_specs=vmem, out_s...  12.2 us
    all_to_all x1, starting transfers between devices, body(): grams = lax.all_to_all(grams, SLAB, split_axis=0, concat_axis=0, tiled=True)  11.7 us
    ppermute x6, starting transfers between devices, from_x(): lax.ppermute(value, 'x', [(i, (i + d) % 4) for i in range(4)])  9.19 us
    pallas_call x1, Pallas kernels, backward_y(): pl.pallas_call(backward_y_kernel, in_specs=[vmem] * 6, out_specs=[vmem, v...  8.59 us
    pallas_call x1, Pallas kernels, forward_y(): pl.pallas_call(forward_y_kernel, grid=(ROWS // 4,), in_specs=[pl.BlockSpe...  7.62 us
  transfers between devices with their start and end apart: 15, of which 9 were waited for; matrix products, arithmetic and copies ran while one was open for 0% of the time, Pallas kernels for 5%

profile of v2, /device:TPU:8, one launch (start us, length us, event | category | flops | bytes accessed | tf_op | source)
XLA Modules:
  0.0 220.3 jit_solution(17771756059553329978)
XLA Ops:
  0.6 5.0 %gram_rows.1 = f32[32,16,128]{2,1,0:T(8,128)} custom-call(s32[4,32]{1,0:T(4,128)} %bitcast.40, f32[32,4,64,128]{3,2,1,0:T(8,128)} %bitcast.36), custom_call_target="tpu_custom_call" | custom-call | tf_op jit(solution)/shard_map/gram_rows/pallas_call | solution.py:325
  5.7 11.7 %all-to-all-start.1 = ((f32[32,16,128]{2,1,0:T(8,128)}), f32[32,16,128]{2,1,0:T(8,128)S(1)}, u32[]{:S(2)}, u32[]{:S(2)}) async-start(f32[32,16,128]{2,1,0:T(8,128)} %gram_rows.1), calls=%async_computation.1 | async-start | bytes 524288 | tf_op jit(solution)/shard_map/all_to_all | solution.py:415
  17.4 7.6 %forward_y.1 = f32[32,144,128]{2,1,0:T(8,128)} custom-call(f32[12,32,384]{2,1,0:T(8,128)} %bitcast.33, bf16[12,384,128]{2,1,0:T(8,128)(2,1)} %s_ref.3, bf16[128,256]{1,0:T(8,128)(2,1)} %constant.32.clone.maps_ref, bf16[256,1024]{1,0:T(8,128)(2,1)} %constant.33.clone.spread_ref, bf16[384,768]{1,0:T(8,128)(2,1)} %constant.24.clone.high_ref, ...), custom_call_target="tpu_custom_call" | custom-call | tf_op jit(solution)/shard_map/forward_y/pallas_call | solution.py:173
  25.0 3.6 %all-to-all-done.1.in_ref = f32[32,16,128]{2,1,0:T(8,128)S(1)} async-done(((f32[32,16,128]{2,1,0:T(8,128)}), f32[32,16,128]{2,1,0:T(8,128)S(1)}, u32[]{:S(2)}, u32[]{:S(2)}) %all-to-all-start.1) | async-done | bytes 262176 | tf_op jit(solution)/shard_map/all_to_all | solution.py:415
  28.6 6.4 %all-to-all-start = ((f32[32,144,128]{2,1,0:T(8,128)}), f32[32,144,128]{2,1,0:T(8,128)S(1)}, u32[]{:S(2)}, u32[]{:S(2)}) async-start(f32[32,144,128]{2,1,0:T(8,128)} %forward_y.1), calls=%async_computation | async-start | bytes 4718592 | tf_op jit(solution)/shard_map/all_to_all | solution.py:421
  35.0 2.3 %gram_sum.1.rest_0_ = f32[288,128]{1,0:T(8,128)} custom-call(s32[4,32]{1,0:T(4,128)} %bitcast.41, f32[32,16,128]{2,1,0:T(8,128)} %copy-done.3), custom_call_target="tpu_custom_call" | custom-call | tf_op jit(solution)/shard_map/gram_sum/pallas_call | solution.py:145
  37.3 2.8 %collective-permute-start.2 = (f32[288,128]{1,0:T(8,128)}, f32[288,128]{1,0:T(8,128)S(1)}, u32[]{:S(2)}, u32[]{:S(2)}) collective-permute-start(f32[288,128]{1,0:T(8,128)} %gram_sum.1.rest_0_), channel_id=1, source_target_pairs={{0,6},{2,0},{4,2},{6,4},{1,7},{3,1},{5,3},{7,5},{8,14},{10,8},{12,... | collective-permute-start | bytes 442376 | tf_op jit(solution)/shard_map/ppermute | solution.py:406
  41.7 3.8 %collective-permute-done.2.rest_3_ = f32[288,128]{1,0:T(8,128)S(1)} collective-permute-done((f32[288,128]{1,0:T(8,128)}, f32[288,128]{1,0:T(8,128)S(1)}, u32[]{:S(2)}, u32[]{:S(2)}) %collective-permute-start.2) | collective-permute-done | bytes 147488 | tf_op jit(solution)/shard_map/ppermute | solution.py:406
  45.5 2.0 collective-permute-done.1.rest_2_
  47.6 1.5 collective-permute-done.rest_1_
  51.2 38.0 %all-to-all-done = f32[32,144,128]{2,1,0:T(8,128)S(1)} async-done(((f32[32,144,128]{2,1,0:T(8,128)}), f32[32,144,128]{2,1,0:T(8,128)S(1)}, u32[]{:S(2)}, u32[]{:S(2)}) %all-to-all-start) | async-done | bytes 2359328 | tf_op jit(solution)/shard_map/all_to_all | solution.py:421
  89.2 1.4 copy-done
  90.6 12.2 %middle.1 = f32[32,152,128]{2,1,0:T(8,128)} custom-call(f32[1,1]{1,0:T(1,128)} %bitcast.1.norm_ref, f32[4608,128]{1,0:T(8,128)} %bitcast.32, f32[288,128]{1,0:T(8,128)} %gram_sum.1.rest_0_, f32[288,128]{1,0:T(8,128)} %copy-done.10, f32[288,128]{1,0:T(8,128)} %copy-done.9, f32[288,128]{1,0:T(8,128)} %copy-done.8, f32[288,128]{1,0:T(8,128)} %copy-done.11, ...), custom_call_target="tpu_custom_call" | custom-call | tf_op jit(solution)/shard_map/middle/pallas_call | solution.py:240
  102.8 64.4 %all_to_all.20 = f32[32,152,128]{2,1,0:T(8,128)} all-to-all(f32[32,152,128]{2,1,0:T(8,128)} %middle.1), channel_id=1, replica_groups=mesh['z'=8,'y'=4,'x'=4,'core'=2] {'z','y'}, dimensions={0} | all-to-all | bytes 4980736 | tf_op jit(solution)/shard_map/all_to_all | solution.py:424
  167.2 8.6 %backward_y.1 = (f32[200,384]{1,0:T(8,128)}, f32[200,384]{1,0:T(8,128)}) custom-call(f32[4864,128]{1,0:T(8,128)} %bitcast.31, bf16[12,384,128]{2,1,0:T(8,128)(2,1)} %s_ref.3, bf16[128,256]{1,0:T(8,128)(2,1)} %constant.32.clone.maps_ref, bf16[1024,128]{1,0:T(8,128)(2,1)} %constant.34.clone.gather_ref, bf16[384,768]{1,0:T(8,128)(2,1)} %constant.30.clone.high_ref, ...), custom_call_target="tpu_custom_call" | custom-call | tf_op jit(solution)/shard_map/backward_y/pallas_call | solution.py:293
  175.8 1.8 collective-permute-done.7
  178.7 3.1 %collective-permute-start.10 = (f32[200,384]{1,0:T(8,128)S(1)}, f32[200,384]{1,0:T(8,128)S(1)}, u32[]{:S(2)}, u32[]{:S(2)}) collective-permute-start(f32[200,384]{1,0:T(8,128)S(1)} %add.3.own_ref), channel_id=1, source_target_pairs={{0,6},{2,0},{4,2},{6,4},{1,7},{3,1},{5,3},{7,5},{8,14},{10,8},{12,... | collective-permute-start | bytes 921608 | tf_op jit(solution)/shard_map/ppermute | solution.py:406
  183.4 11.8 %collective-permute-done.10.c_ref = f32[200,384]{1,0:T(8,128)S(1)} collective-permute-done((f32[200,384]{1,0:T(8,128)S(1)}, f32[200,384]{1,0:T(8,128)S(1)}, u32[]{:S(2)}, u32[]{:S(2)}) %collective-permute-start.10) | collective-permute-done | bytes 307232 | tf_op jit(solution)/shard_map/ppermute | solution.py:406
  195.2 3.7 %collective-permute-done.8.a_ref = f32[200,384]{1,0:T(8,128)S(1)} collective-permute-done((f32[200,384]{1,0:T(8,128)S(1)}, f32[200,384]{1,0:T(8,128)S(1)}, u32[]{:S(2)}, u32[]{:S(2)}) %collective-permute-start.8) | collective-permute-done | bytes 307232 | tf_op jit(solution)/shard_map/ppermute | solution.py:406
  199.6 2.3 %residual_share.1 = (f32[192,384]{1,0:T(8,128)}, f32[64,1,128]{2,1,0:T(1,128)}, f32[8,128]{1,0:T(8,128)}) custom-call(f32[200,384]{1,0:T(8,128)} %copy-done.2, f32[200,384]{1,0:T(8,128)} %copy-done.6, f32[200,384]{1,0:T(8,128)} %copy-done.5, f32[200,384]{1,0:T(8,128)} %copy-done.4, f32[2,192,384]{2,1,0:T(8,128)} %bitcast.37), custom_call_target="tpu_custom_call" | custom-call | tf_op jit(solution)/shard_map/residual_share/pallas_call | solution.py:351
  201.9 6.1 %all-to-all-start.3 = ((f32[64,1,128]{2,1,0:T(1,128)}), f32[64,1,128]{2,1,0:T(1,128)S(1)}, u32[]{:S(2)}, u32[]{:S(2)}) async-start(f32[64,1,128]{2,1,0:T(1,128)} %get-tuple-element.13), calls=%async_computation.3 | async-start | bytes 65536 | tf_op jit(solution)/shard_map/all_to_all | solution.py:430
  208.0 2.2 image_update.1
  210.2 6.4 %all-to-all-done.3.parts_ref = f32[64,1,128]{2,1,0:T(1,128)S(1)} async-done(((f32[64,1,128]{2,1,0:T(1,128)}), f32[64,1,128]{2,1,0:T(1,128)S(1)}, u32[]{:S(2)}, u32[]{:S(2)}) %all-to-all-start.3) | async-done | bytes 32800 | tf_op jit(solution)/shard_map/all_to_all | solution.py:430
  217.9 2.4 %finish.1 = (f32[2,192,384]{2,1,0:T(8,128)}, f32[2,192,384]{2,1,0:T(8,128)}) custom-call(f32[8,128]{1,0:T(8,128)} %get-tuple-element.12.sums_ref, f32[64,1,128]{2,1,0:T(1,128)} %copy-done.14, f32[2,192,384]{2,1,0:T(8,128)} %bitcast.35, f32[192,384]{1,0:T(8,128)} %get-tuple-element.14.own_ref, f32[192,384]{1,0:T(8,128)} %copy-done.7), custom_call_target="tpu_custom_call" | custom-call | tf_op jit(solution)/shard_map/finish/pallas_call | solution.py:391
  (47 shorter events, 8.6 us)
Async XLA Ops:
  5.7 22.9 %all-to-all-start.1 = ((f32[32,16,128]{2,1,0:T(8,128)}), f32[32,16,128]{2,1,0:T(8,128)S(1)}, u32[]{:S(2)}, u32[]{:S(2)}) async-start(f32[32,16,128]{2,1,0:T(8,128)} %gram_rows.1), calls=%async_computation.1 | async-start | bytes 524288 | tf_op jit(solution)/shard_map/all_to_all | solution.py:415
  25.0 24.1 %copy-start.1 = (f32[12,384,32]{1,2,0:T(8,128)S(1)}, f32[12,384,32]{1,2,0:T(8,128)}, u32[]{:S(2)}) copy-start(f32[12,384,32]{1,2,0:T(8,128)} %param.19) | copy-start | bytes 1769476
  28.6 6.4 %copy-start.3 = (f32[32,16,128]{2,1,0:T(8,128)}, f32[32,16,128]{2,1,0:T(8,128)S(1)}, u32[]{:S(2)}) copy-start(f32[32,16,128]{2,1,0:T(8,128)S(1)} %all-to-all-done.1.in_ref) | copy-start | bytes 786436
  28.6 60.6 %all-to-all-start = ((f32[32,144,128]{2,1,0:T(8,128)}), f32[32,144,128]{2,1,0:T(8,128)S(1)}, u32[]{:S(2)}, u32[]{:S(2)}) async-start(f32[32,144,128]{2,1,0:T(8,128)} %forward_y.1), calls=%async_computation | async-start | bytes 4718592 | tf_op jit(solution)/shard_map/all_to_all | solution.py:421
  37.3 8.3 %collective-permute-start.2 = (f32[288,128]{1,0:T(8,128)}, f32[288,128]{1,0:T(8,128)S(1)}, u32[]{:S(2)}, u32[]{:S(2)}) collective-permute-start(f32[288,128]{1,0:T(8,128)} %gram_sum.1.rest_0_), channel_id=1, source_target_pairs={{0,6},{2,0},{4,2},{6,4},{1,7},{3,1},{5,3},{7,5},{8,14},{10,8},{12,... | collective-permute-start | bytes 442376 | tf_op jit(solution)/shard_map/ppermute | solution.py:406
  40.0 7.5 %collective-permute-start.1 = (f32[288,128]{1,0:T(8,128)}, f32[288,128]{1,0:T(8,128)S(1)}, u32[]{:S(2)}, u32[]{:S(2)}) collective-permute-start(f32[288,128]{1,0:T(8,128)} %gram_sum.1.rest_0_), channel_id=1, source_target_pairs={{0,4},{2,6},{4,0},{6,2},{1,5},{3,7},{5,1},{7,3},{8,12},{10,14},{12... | collective-permute-start | bytes 442376 | tf_op jit(solution)/shard_map/ppermute | solution.py:406
  40.8 8.3 %collective-permute-start = (f32[288,128]{1,0:T(8,128)}, f32[288,128]{1,0:T(8,128)S(1)}, u32[]{:S(2)}, u32[]{:S(2)}) collective-permute-start(f32[288,128]{1,0:T(8,128)} %gram_sum.1.rest_0_), channel_id=1, source_target_pairs={{0,2},{2,4},{4,6},{6,0},{1,3},{3,5},{5,7},{7,1},{8,10},{10,12},{12... | collective-permute-start | bytes 442376 | tf_op jit(solution)/shard_map/ppermute | solution.py:406
  41.7 8.2 %collective-permute-start.3 = (f32[288,128]{1,0:T(8,128)}, f32[288,128]{1,0:T(8,128)S(1)}, u32[]{:S(2)}, u32[]{:S(2)}) collective-permute-start(f32[288,128]{1,0:T(8,128)} %gram_sum.1.rest_0_), channel_id=1, source_target_pairs={{0,1},{1,0},{2,3},{3,2},{4,5},{5,4},{6,7},{7,6},{8,9},{9,8},{10,11... | collective-permute-start | bytes 442376 | tf_op jit(solution)/shard_map/ppermute | solution.py:402
  45.5 43.7 %copy-start.8 = (f32[288,128]{1,0:T(8,128)}, f32[288,128]{1,0:T(8,128)S(1)}, u32[]{:S(2)}) copy-start(f32[288,128]{1,0:T(8,128)S(1)} %collective-permute-done.2.rest_3_) | copy-start | bytes 442372
  45.5 4.3 %collective-permute-start.6 = (f32[288,128]{1,0:T(8,128)S(1)}, f32[288,128]{1,0:T(8,128)S(1)}, u32[]{:S(2)}, u32[]{:S(2)}) collective-permute-start(f32[288,128]{1,0:T(8,128)S(1)} %collective-permute-done.2.rest_3_), channel_id=1, source_target_pairs={{0,1},{1,0},{2,3},{3,2},{4,5},{5,4},{6,7},{7,6},{8,9},{9,8},{10,11... | collective-permute-start | bytes 442376 | tf_op jit(solution)/shard_map/ppermute | solution.py:402
  47.6 41.6 %copy-start.9 = (f32[288,128]{1,0:T(8,128)}, f32[288,128]{1,0:T(8,128)S(1)}, u32[]{:S(2)}) copy-start(f32[288,128]{1,0:T(8,128)S(1)} %collective-permute-done.1.rest_2_) | copy-start | bytes 442372
  47.6 2.3 %collective-permute-start.5 = (f32[288,128]{1,0:T(8,128)S(1)}, f32[288,128]{1,0:T(8,128)S(1)}, u32[]{:S(2)}, u32[]{:S(2)}) collective-permute-start(f32[288,128]{1,0:T(8,128)S(1)} %collective-permute-done.1.rest_2_), channel_id=1, source_target_pairs={{0,1},{1,0},{2,3},{3,2},{4,5},{5,4},{6,7},{7,6},{8,9},{9,8},{10,11... | collective-permute-start | bytes 442376 | tf_op jit(solution)/shard_map/ppermute | solution.py:402
  49.1 40.1 %copy-start.10 = (f32[288,128]{1,0:T(8,128)}, f32[288,128]{1,0:T(8,128)S(1)}, u32[]{:S(2)}) copy-start(f32[288,128]{1,0:T(8,128)S(1)} %collective-permute-done.rest_1_) | copy-start | bytes 442372
  49.1 2.1 collective-permute-start.4
  49.9 39.4 %copy-start.11 = (f32[288,128]{1,0:T(8,128)}, f32[288,128]{1,0:T(8,128)S(1)}, u32[]{:S(2)}) copy-start(f32[288,128]{1,0:T(8,128)S(1)} %collective-permute-done.3.rest_4_) | copy-start | bytes 442372
  175.8 1.8 collective-permute-start.7
  178.6 20.2 %copy-start.2 = (f32[200,384]{1,0:T(8,128)}, f32[200,384]{1,0:T(8,128)S(1)}, u32[]{:S(2)}) copy-start(f32[200,384]{1,0:T(8,128)S(1)} %add.3.own_ref) | copy-start | bytes 921604
  178.7 16.5 %collective-permute-start.10 = (f32[200,384]{1,0:T(8,128)S(1)}, f32[200,384]{1,0:T(8,128)S(1)}, u32[]{:S(2)}, u32[]{:S(2)}) collective-permute-start(f32[200,384]{1,0:T(8,128)S(1)} %add.3.own_ref), channel_id=1, source_target_pairs={{0,6},{2,0},{4,2},{6,4},{1,7},{3,1},{5,3},{7,5},{8,14},{10,8},{12,... | collective-permute-start | bytes 921608 | tf_op jit(solution)/shard_map/ppermute | solution.py:406
  181.7 13.5 %collective-permute-start.9 = (f32[200,384]{1,0:T(8,128)S(1)}, f32[200,384]{1,0:T(8,128)S(1)}, u32[]{:S(2)}, u32[]{:S(2)}) collective-permute-start(f32[200,384]{1,0:T(8,128)S(1)} %add.3.own_ref), channel_id=1, source_target_pairs={{0,4},{2,6},{4,0},{6,2},{1,5},{3,7},{5,1},{7,3},{8,12},{10,14},{12... | collective-permute-start | bytes 921608 | tf_op jit(solution)/shard_map/ppermute | solution.py:406
  182.5 16.3 %collective-permute-start.8 = (f32[200,384]{1,0:T(8,128)S(1)}, f32[200,384]{1,0:T(8,128)S(1)}, u32[]{:S(2)}, u32[]{:S(2)}) collective-permute-start(f32[200,384]{1,0:T(8,128)S(1)} %add.3.own_ref), channel_id=1, source_target_pairs={{0,2},{2,4},{4,6},{6,0},{1,3},{3,5},{5,7},{7,1},{8,10},{10,12},{12... | collective-permute-start | bytes 921608 | tf_op jit(solution)/shard_map/ppermute | solution.py:406
  195.2 3.7 %copy-start.4 = (f32[200,384]{1,0:T(8,128)}, f32[200,384]{1,0:T(8,128)S(1)}, u32[]{:S(2)}) copy-start(f32[200,384]{1,0:T(8,128)S(1)} %collective-permute-done.10.c_ref) | copy-start | bytes 921604
  195.2 3.7 %copy-start.5 = (f32[200,384]{1,0:T(8,128)}, f32[200,384]{1,0:T(8,128)S(1)}, u32[]{:S(2)}) copy-start(f32[200,384]{1,0:T(8,128)S(1)} %collective-permute-done.9.b_ref) | copy-start | bytes 921604
  201.9 14.7 %collective-permute-start.11 = (f32[192,384]{1,0:T(8,128)}, f32[192,384]{1,0:T(8,128)S(1)}, u32[]{:S(2)}, u32[]{:S(2)}) collective-permute-start(f32[192,384]{1,0:T(8,128)} %get-tuple-element.14.own_ref), channel_id=1, source_target_pairs={{0,1},{1,0},{2,3},{3,2},{4,5},{5,4},{6,7},{7,6},{8,9},{9,8},{10,11... | collective-permute-start | bytes 884744 | tf_op jit(solution)/shard_map/ppermute | solution.py:402
  201.9 14.6 %all-to-all-start.3 = ((f32[64,1,128]{2,1,0:T(1,128)}), f32[64,1,128]{2,1,0:T(1,128)S(1)}, u32[]{:S(2)}, u32[]{:S(2)}) async-start(f32[64,1,128]{2,1,0:T(1,128)} %get-tuple-element.13), calls=%async_computation.3 | async-start | bytes 65536 | tf_op jit(solution)/shard_map/all_to_all | solution.py:430
  (6 other events, 4.8 us)

commit v3 on v2

--- a/solution.py
+++ b/solution.py
@@ -24,6 +24,7 @@
 COIL = ("x", "core")
 ALL = ("z", "y", "x", "core")
 HALF_ROWS = PAIRS * 2 * PLANES
+QUARTER = HALF_ROWS // 2
 BLOCK = 24 * PAIRS
 HALF = LANES // 2
 COILS = HALF // PLANES
@@ -196,20 +197,30 @@
     return jnp.concatenate(parts, axis=0)
 
 
-def middle_kernel(norm_ref, in_ref, *rest):
-    g_refs = rest[:8]
-    fh_ref, fl_ref, bh_ref, bl_ref, out_ref, grid_ref, g_ref = rest[8:]
+def middle_kernel(norm_ref, in_hbm, *rest):
+    g_hbm, tables_hbm = rest[:8], rest[8:12]
+    out_hbm, in_ref, table_ref, g_ref, grid_ref, out_ref, in_sem, table_sem, g_sem, out_sem = rest[12:]
+    fh_ref, fl_ref, bh_ref, bl_ref = (table_ref.at[i] for i in range(4))
     xpos, core = lax.axis_index("x"), lax.axis_index("core")
+    load_in = pltpu.make_async_copy(in_hbm, in_ref, in_sem)
+    load_tables = [pltpu.make_async_copy(tables_hbm[i], table_ref.at[i], table_sem.at[i]) for i in range(4)]
+    load_g = []
     for d in range(4):
-        x = lax.rem(xpos + 4 - d, 4)
         for k in range(2):
-            g_ref[2 * x + lax.rem(core + k, 2)] = g_refs[4 * k + d][...]
+            c = 2 * lax.rem(xpos + 4 - d, 4) + lax.rem(core + k, 2)
+            load_g.append(pltpu.make_async_copy(g_hbm[4 * k + d], g_ref.at[c], g_sem.at[4 * k + d]))
+    for copy in [load_in] + load_tables[:2] + load_g + load_tables[2:]:
+        copy.start()
+    for copy in [load_in] + load_tables[:2]:
+        copy.wait()
     for p in range(PAIRS):
         pieces = [arrived_rows(in_ref, 2 * p + i, BLOCK) for i in range(2)]
         done = transform(fh_ref, fl_ref, pieces, [times_i(x) for x in pieces])
         for i in range(2):
             b = 2 * p + i
             grid_ref[b // TY, pl.ds(b % TY, N, stride=TY), :] = done[:, LANES * i:LANES * (i + 1)]
+    for copy in load_g + load_tables[2:]:
+        copy.wait()
     left = lax.broadcasted_iota(jnp.int32, (CELLS, LANES), 1) < CELLS
     curve = jnp.zeros((8, LANES), F32)
     groups = N // TX // 2
@@ -229,37 +240,52 @@
     norm = jnp.broadcast_to(norm_ref[...], (8, LANES)) / (8 * LANES)
     sums = jnp.where(lax.broadcasted_iota(jnp.int32, (8, LANES), 0) == 0, jnp.sum(curve, axis=0, keepdims=True), norm)
     out_ref[:, BLOCK:, :] = jnp.broadcast_to(sums[None], (SLABS, 8, LANES))
+    stores = [pltpu.make_async_copy(out_ref.at[:, BLOCK:, :], out_hbm.at[:, BLOCK:, :], out_sem.at[PAIRS])]
+    stores[0].start()
     for p in range(PAIRS):
         pieces = [grid_ref[b // TY, pl.ds(b % TY, N, stride=TY), :] for b in (2 * p, 2 * p + 1)]
         done = transform(bh_ref, bl_ref, pieces, [times_i(x) for x in pieces])
         store_outgoing(out_ref, 24 * p, done[:, :LANES], done[:, LANES:])
+        rows = pl.ds(24 * p, 24)
+        stores.append(pltpu.make_async_copy(out_ref.at[:, rows, :], out_hbm.at[:, rows, :], out_sem.at[p]))
+        stores[-1].start()
+    for copy in stores:
+        copy.wait()
 
 
 def middle(norm, arrived, grams, table_in, table_out):
-    vmem = pl.BlockSpec(memory_space=pltpu.VMEM)
+    hbm = pl.BlockSpec(memory_space=pltpu.HBM)
     return pl.pallas_call(
         middle_kernel,
-        in_specs=[vmem] * 14,
-        out_specs=vmem,
+        in_specs=[pl.BlockSpec(memory_space=pltpu.VMEM)] + [hbm] * 13,
+        out_specs=hbm,
         out_shape=jax.ShapeDtypeStruct((SLABS, BLOCK + 8, LANES), F32),
         scratch_shapes=[
+            pltpu.VMEM((SLABS * BLOCK, LANES), F32),
+            pltpu.VMEM((4, N, 2 * N), BF16),
+            pltpu.VMEM((8, TILES // 2 * 8, LANES), F32),
             pltpu.VMEM((ROWS // TY, N * TY, LANES), F32),
-            pltpu.VMEM((8, TILES // 2 * 8, LANES), F32),
+            pltpu.VMEM((SLABS, BLOCK + 8, LANES), F32),
+            pltpu.SemaphoreType.DMA,
+            pltpu.SemaphoreType.DMA((4,)),
+            pltpu.SemaphoreType.DMA((8,)),
+            pltpu.SemaphoreType.DMA((PAIRS + 1,)),
         ],
         compiler_params=pltpu.CompilerParams(vmem_limit_bytes=VMEM_LIMIT),
         name="middle",
     )(norm, arrived, *grams, *table_in, *table_out)
 
 
-def backward_y_kernel(in_ref, s_ref, maps_ref, gather_ref, high_ref, low_ref, kept_ref, sent_ref):
+def backward_y_kernel(in_ref, s_ref, maps_ref, gather_ref, high_ref, low_ref, *rest):
+    kept_refs, sent_refs = rest[:2], rest[2:]
     core = lax.axis_index("core")
     block = BLOCK + 8
     curve = jnp.sum(in_ref[pl.ds(BLOCK, SLABS, stride=block), :], axis=0, keepdims=True)
     norm = jnp.sum(in_ref[pl.ds(BLOCK + 1, SLABS, stride=block), :], axis=0, keepdims=True)
     sums = jnp.where(lax.broadcasted_iota(jnp.int32, (8, LANES), 0) == 0, curve, norm)
     sums = jnp.concatenate([sums] + [jnp.zeros_like(sums)] * (N // LANES - 1), axis=1)
-    kept_ref[HALF_ROWS:, :] = sums
-    sent_ref[HALF_ROWS:, :] = sums
+    kept_refs[0][QUARTER:, :] = sums
+    sent_refs[0][QUARTER:, :] = sums
     for g in range(ROWS // 4):
         highs, lows = [], []
         for p in range(2):
@@ -275,26 +301,27 @@
         total = dot(jnp.concatenate(highs + lows, axis=1), gather_ref[...]).T
         for r in range(4):
             a = 4 * g + r
-            at = a % PAIRS * 2 * PLANES
+            at = a % (PAIRS // 2) * 2 * PLANES
+            quarter = a // (PAIRS // 2) % 2
             rows = total[2 * PLANES * r:2 * PLANES * (r + 1), :]
 
             @pl.when(core == a // PAIRS)
             def _():
-                kept_ref[at:at + 2 * PLANES, :] = rows
+                kept_refs[quarter][at:at + 2 * PLANES, :] = rows
 
             @pl.when(core != a // PAIRS)
             def _():
-                sent_ref[at:at + 2 * PLANES, :] = rows
+                sent_refs[quarter][at:at + 2 * PLANES, :] = rows
 
 
 def backward_y(arrived, maps, sel_maps, sel_gather, table):
     vmem = pl.BlockSpec(memory_space=pltpu.VMEM)
-    half = jax.ShapeDtypeStruct((HALF_ROWS + 8, N), F32)
+    quarters = [jax.ShapeDtypeStruct((QUARTER + 8, N), F32), jax.ShapeDtypeStruct((QUARTER, N), F32)]
     return pl.pallas_call(
         backward_y_kernel,
         in_specs=[vmem] * 6,
-        out_specs=[vmem, vmem],
-        out_shape=[half, half],
+        out_specs=[vmem] * 4,
+        out_shape=quarters * 2,
         compiler_params=pltpu.CompilerParams(vmem_limit_bytes=VMEM_LIMIT),
         name="backward_y",
     )(arrived, maps, sel_maps, sel_gather, *table)
@@ -321,7 +348,7 @@
 
 
 def gram_rows(interp, counts):
-    owners = 8
+    owners = 16
     return pl.pallas_call(
         gram_kernel,
         grid=(SLABS // owners,),
@@ -333,20 +360,24 @@
     )(counts, interp)
 
 
-def share_kernel(own_ref, a_ref, b_ref, c_ref, residual_ref, out_ref, part_ref, sums_ref):
-    total = (own_ref[...] + a_ref[...]) + (b_ref[...] + c_ref[...])
-    curvature = jnp.sum(total[HALF_ROWS:HALF_ROWS + 1, :LANES], axis=1, keepdims=True)
-    norm_now = jnp.sum(total[HALF_ROWS + 1:HALF_ROWS + 2, :LANES], axis=1, keepdims=True)
+def share_kernel(a_ref, more_a_ref, b_ref, more_b_ref, residual_ref, out_ref, part_ref, sums_ref):
+    first = a_ref[...] + more_a_ref[...]
+    curvature = jnp.sum(first[QUARTER:QUARTER + 1, :LANES], axis=1, keepdims=True)
+    norm_now = jnp.sum(first[QUARTER + 1:QUARTER + 2, :LANES], axis=1, keepdims=True)
     step = norm_now / curvature
-    half = residual_ref[lax.axis_index("core")] - step * total[:HALF_ROWS]
-    out_ref[...] = half
-    square = jnp.sum((half * half).reshape(HALF_ROWS // 8, 8, N), axis=0)
+    core = lax.axis_index("core")
+    square = jnp.zeros((8, N), F32)
+    for i, applied in enumerate((first[:QUARTER], b_ref[...] + more_b_ref[...])):
+        rows = pl.ds(i * QUARTER, QUARTER)
+        part = residual_ref[core, rows, :] - step * applied
+        out_ref[rows, :] = part
+        square = square + jnp.sum((part * part).reshape(QUARTER // 8, 8, N), axis=0)
     part = jnp.sum(square[:, :LANES] + square[:, LANES:2 * LANES] + square[:, 2 * LANES:], axis=0, keepdims=True)
     part_ref[...] = jnp.broadcast_to(part[None], part_ref.shape)
     sums_ref[...] = jnp.where(lax.broadcasted_iota(jnp.int32, (8, LANES), 0) == 0, step, norm_now)
 
 
-def residual_share(own, others, residual):
+def residual_share(first, second, residual):
     vmem = pl.BlockSpec(memory_space=pltpu.VMEM)
     return pl.pallas_call(
         share_kernel,
@@ -359,7 +390,7 @@
         ],
         compiler_params=pltpu.CompilerParams(vmem_limit_bytes=VMEM_LIMIT),
         name="residual_share",
-    )(own, *others, residual)
+    )(*first, *second, residual)
 
 
 def image_kernel(sums_ref, image_ref, direction_ref, out_ref):
@@ -402,6 +433,10 @@
     return lax.ppermute(value, "core", [(0, 1), (1, 0)])
 
 
+def swap_x(value, mask):
+    return lax.ppermute(value, "x", [(i, i ^ mask) for i in range(4)])
+
+
 def from_x(value):
     return [lax.ppermute(value, "x", [(i, (i + d) % 4) for i in range(4)]) for d in range(1, 4)]
 
@@ -422,11 +457,18 @@
     norm = jnp.sum(residual_t * residual_t).reshape(1, 1)
     outgoing = middle(norm, pencils.reshape(-1, LANES), grams, arrival[0], sending[1])
     slab_rows = lax.all_to_all(outgoing, SLAB, split_axis=0, concat_axis=0, tiled=True)
-    kept, sent = backward_y(slab_rows.reshape(-1, LANES), sensitivity, sel_maps, sel_gather, arrival[1])
-
-    kept = kept + swap_core(sent)
+    kept_a, kept_b, sent_a, sent_b = backward_y(
+        slab_rows.reshape(-1, LANES), sensitivity, sel_maps, sel_gather, arrival[1]
+    )
+
+    kept_a = kept_a + swap_core(sent_a)
+    kept_b = kept_b + swap_core(sent_b)
+    kept_a = kept_a + swap_x(kept_a, 1)
+    kept_b = kept_b + swap_x(kept_b, 3)
     halves = (2, HALF_ROWS, N)
-    half, parts, sums = residual_share(kept, from_x(kept), residual_t.reshape(halves))
+    half, parts, sums = residual_share(
+        (kept_a, swap_x(kept_a, 3)), (kept_b, swap_x(kept_b, 1)), residual_t.reshape(halves)
+    )
     parts = lax.all_to_all(parts, SLAB + ("core",), split_axis=0, concat_axis=0, tiled=True)
     next_image = image_update(sums, image_t.reshape(halves), direction_t.reshape(halves))
     next_residual, next_direction = finish(sums, parts, direction_t.reshape(halves), half, swap_core(half))

time: 223 us -> 216 us (0.969)
  waiting for transfers between devices: 72.6 us -> 63.4 us
  starting transfers between devices: 33.3 us -> 35.8 us
    ppermute x6 -> x3, waiting for transfers between devices: 22.8 us -> 7.37 us  [from_x(): lax.ppermute(value, 'x', [(i, (i + d) % 4) for i in range(4)])]
    ppermute x0 -> x4, waiting for transfers between devices: none -> 6.98 us  [swap_x(): return lax.ppermute(value, 'x', [(i, i ^ mask) for i in range(4)])]
    ppermute x0 -> x4, starting transfers between devices: none -> 6.69 us  [swap_x(): return lax.ppermute(value, 'x', [(i, i ^ mask) for i in range(4)])]
    ppermute x6 -> x3, starting transfers between devices: 9.19 us -> 4.44 us  [from_x(): lax.ppermute(value, 'x', [(i, (i + d) % 4) for i in range(4)])]
  transfers between devices with their start and end apart: 15 -> 17, of which waited for: 9 -> 10; matrix products, arithmetic and copies ran while one was open for 0% -> 1% of each run, Pallas kernels for 5% -> 6%
where the time goes in v3:
time: 216 us; the launch traced here: 214 us
  blocking collectives  64.4 us (30%)
  waiting for transfers between devices  63.4 us (29%)
  Pallas kernels  41.8 us (19%)
  starting transfers between devices  35.8 us (17%)
  local copies, waits for them, and re-layouts  4.77 us (2%)
  other arithmetic  2.68 us (1%)
    all_to_all x1, blocking collectives, body(): lax.all_to_all(outgoing, SLAB, split_axis=0, concat_axis=0, tiled=True)  64.4 us
    all_to_all x1, waiting for transfers between devices, body(): lax.all_to_all(outgoing, SLAB, split_axis=0, concat_axis=0, tiled=True)  38 us
    pallas_call x1, Pallas kernels, middle(): pl.pallas_call(middle_kernel, in_specs=[pl.BlockSpec(memory_space=pltpu.V...  12 us
    all_to_all x1, starting transfers between devices, body(): grams = lax.all_to_all(grams, SLAB, split_axis=0, concat_axis=0, tiled=True)  11.7 us
    pallas_call x1, Pallas kernels, backward_y(): pl.pallas_call(backward_y_kernel, in_specs=[vmem] * 6, out_specs=[vmem] *...  8.58 us
    pallas_call x1, Pallas kernels, forward_y(): pl.pallas_call(forward_y_kernel, grid=(ROWS // 4,), in_specs=[pl.BlockSpe...  7.64 us
    ppermute x3, waiting for transfers between devices, from_x(): lax.ppermute(value, 'x', [(i, (i + d) % 4) for i in range(4)])  7.37 us
    ppermute x4, waiting for transfers between devices, swap_x(): return lax.ppermute(value, 'x', [(i, i ^ mask) for i in range(4)])  6.98 us
  transfers between devices with their start and end apart: 17, of which 10 were waited for; matrix products, arithmetic and copies ran while one was open for 1% of the time, Pallas kernels for 6%

profile of v3, /device:TPU:8, one launch (start us, length us, event | category | flops | bytes accessed | tf_op | source)
XLA Modules:
  0.0 213.6 jit_solution(7616033691665173430)
XLA Ops:
  0.6 4.5 %gram_rows.1 = f32[32,16,128]{2,1,0:T(8,128)} custom-call(s32[4,32]{1,0:T(4,128)} %bitcast.40, f32[32,4,64,128]{3,2,1,0:T(8,128)} %bitcast.36), custom_call_target="tpu_custom_call" | custom-call | tf_op jit(solution)/shard_map/gram_rows/pallas_call | solution.py:352
  5.1 11.7 %all-to-all-start.1 = ((f32[32,16,128]{2,1,0:T(8,128)}), f32[32,16,128]{2,1,0:T(8,128)S(1)}, u32[]{:S(2)}, u32[]{:S(2)}) async-start(f32[32,16,128]{2,1,0:T(8,128)} %gram_rows.1), calls=%async_computation.1 | async-start | bytes 524288 | tf_op jit(solution)/shard_map/all_to_all | solution.py:450
  16.8 7.6 %forward_y.1 = f32[32,144,128]{2,1,0:T(8,128)} custom-call(f32[12,32,384]{2,1,0:T(8,128)} %bitcast.33, bf16[12,384,128]{2,1,0:T(8,128)(2,1)} %s_ref.3, bf16[128,256]{1,0:T(8,128)(2,1)} %constant.32.clone.maps_ref, bf16[256,1024]{1,0:T(8,128)(2,1)} %constant.33.clone.spread_ref, bf16[384,768]{1,0:T(8,128)(2,1)} %constant.24.clone.high_ref, ...), custom_call_target="tpu_custom_call" | custom-call | tf_op jit(solution)/shard_map/forward_y/pallas_call | solution.py:174
  24.4 3.6 %all-to-all-done.1.in_ref = f32[32,16,128]{2,1,0:T(8,128)S(1)} async-done(((f32[32,16,128]{2,1,0:T(8,128)}), f32[32,16,128]{2,1,0:T(8,128)S(1)}, u32[]{:S(2)}, u32[]{:S(2)}) %all-to-all-start.1) | async-done | bytes 262176 | tf_op jit(solution)/shard_map/all_to_all | solution.py:450
  28.0 6.4 %all-to-all-start = ((f32[32,144,128]{2,1,0:T(8,128)}), f32[32,144,128]{2,1,0:T(8,128)S(1)}, u32[]{:S(2)}, u32[]{:S(2)}) async-start(f32[32,144,128]{2,1,0:T(8,128)} %forward_y.1), calls=%async_computation | async-start | bytes 4718592 | tf_op jit(solution)/shard_map/all_to_all | solution.py:456
  34.4 2.3 %gram_sum.1.rest_0_ = f32[288,128]{1,0:T(8,128)} custom-call(s32[4,32]{1,0:T(4,128)} %bitcast.41, f32[32,16,128]{2,1,0:T(8,128)} %copy-done.2), custom_call_target="tpu_custom_call" | custom-call | tf_op jit(solution)/shard_map/gram_sum/pallas_call | solution.py:146
  36.7 2.8 %collective-permute-start.2 = (f32[288,128]{1,0:T(8,128)}, f32[288,128]{1,0:T(8,128)S(1)}, u32[]{:S(2)}, u32[]{:S(2)}) collective-permute-start(f32[288,128]{1,0:T(8,128)} %gram_sum.1.rest_0_), channel_id=1, source_target_pairs={{0,6},{2,0},{4,2},{6,4},{1,7},{3,1},{5,3},{7,5},{8,14},{10,8},{12,... | collective-permute-start | bytes 442376 | tf_op jit(solution)/shard_map/ppermute | solution.py:441
  41.1 3.8 %collective-permute-done.2.rest_3_ = f32[288,128]{1,0:T(8,128)S(1)} collective-permute-done((f32[288,128]{1,0:T(8,128)}, f32[288,128]{1,0:T(8,128)S(1)}, u32[]{:S(2)}, u32[]{:S(2)}) %collective-permute-start.2) | collective-permute-done | bytes 147488 | tf_op jit(solution)/shard_map/ppermute | solution.py:441
  45.0 2.0 collective-permute-done.1.rest_2_
  47.0 1.5 collective-permute-done.rest_1_
  50.7 38.0 %all-to-all-done = f32[32,144,128]{2,1,0:T(8,128)S(1)} async-done(((f32[32,144,128]{2,1,0:T(8,128)}), f32[32,144,128]{2,1,0:T(8,128)S(1)}, u32[]{:S(2)}, u32[]{:S(2)}) %all-to-all-start) | async-done | bytes 2359328 | tf_op jit(solution)/shard_map/all_to_all | solution.py:456
  90.1 12.0 %middle.1 = f32[32,152,128]{2,1,0:T(8,128)} custom-call(f32[1,1]{1,0:T(1,128)} %bitcast.1.norm_ref, f32[4608,128]{1,0:T(8,128)} %bitcast.32, f32[288,128]{1,0:T(8,128)} %gram_sum.1.rest_0_, f32[288,128]{1,0:T(8,128)} %copy-done.10, f32[288,128]{1,0:T(8,128)} %copy-done.9, f32[288,128]{1,0:T(8,128)} %copy-done.8, f32[288,128]{1,0:T(8,128)} %copy-done.11, ...), custom_call_target="tpu_custom_call" | custom-call | tf_op jit(solution)/shard_map/middle/pallas_call | solution.py:258
  102.1 64.4 %all_to_all.20 = f32[32,152,128]{2,1,0:T(8,128)} all-to-all(f32[32,152,128]{2,1,0:T(8,128)} %middle.1), channel_id=1, replica_groups=mesh['z'=8,'y'=4,'x'=4,'core'=2] {'z','y'}, dimensions={0} | all-to-all | bytes 4980736 | tf_op jit(solution)/shard_map/all_to_all | solution.py:459
  166.5 8.6 %backward_y.1 = (f32[104,384]{1,0:T(8,128)}, f32[96,384]{1,0:T(8,128)}, f32[104,384]{1,0:T(8,128)}, f32[96,384]{1,0:T(8,128)}) custom-call(f32[4864,128]{1,0:T(8,128)} %bitcast.31, bf16[12,384,128]{2,1,0:T(8,128)(2,1)} %s_ref.3, bf16[128,256]{1,0:T(8,128)(2,1)} %constant.32.clone.maps_ref, bf16[1024,128]{1,0:T(8,128)(2,1)} %constant.34.clone.gather_ref, ...), custom_call_target="tpu_custom_call" | custom-call | tf_op jit(solution)/shard_map/backward_y/pallas_call | solution.py:320
  177.6 1.6 collective-permute-start.8
  180.1 2.2 %collective-permute-start.11 = (f32[96,384]{1,0:T(8,128)S(1)}, f32[96,384]{1,0:T(8,128)S(1)}, u32[]{:S(2)}, u32[]{:S(2)}) collective-permute-start(f32[96,384]{1,0:T(8,128)S(1)} %add.14), channel_id=1, source_target_pairs={{0,6},{2,4},{4,2},{6,0},{1,7},{3,5},{5,3},{7,1},{8,14},{10,12},{12... | collective-permute-start | bytes 442376 | tf_op jit(solution)/shard_map/ppermute | solution.py:437
  182.3 1.6 collective-permute-done.8
  183.9 2.8 %collective-permute-start.9 = (f32[104,384]{1,0:T(8,128)S(1)}, f32[104,384]{1,0:T(8,128)S(1)}, u32[]{:S(2)}, u32[]{:S(2)}) collective-permute-start(f32[104,384]{1,0:T(8,128)S(1)} %add.13.a_ref), channel_id=1, source_target_pairs={{0,6},{2,4},{4,2},{6,0},{1,7},{3,5},{5,3},{7,1},{8,14},{10,12},{12... | collective-permute-start | bytes 479240 | tf_op jit(solution)/shard_map/ppermute | solution.py:437
  187.2 5.1 %collective-permute-done.12.more_b_ref = f32[96,384]{1,0:T(8,128)S(1)} collective-permute-done((f32[96,384]{1,0:T(8,128)S(1)}, f32[96,384]{1,0:T(8,128)S(1)}, u32[]{:S(2)}, u32[]{:S(2)}) %collective-permute-start.12) | collective-permute-done | bytes 147488 | tf_op jit(solution)/shard_map/ppermute | solution.py:437
  193.0 2.3 %residual_share.1 = (f32[192,384]{1,0:T(8,128)}, f32[64,1,128]{2,1,0:T(1,128)}, f32[8,128]{1,0:T(8,128)}) custom-call(f32[104,384]{1,0:T(8,128)} %copy-done.3, f32[104,384]{1,0:T(8,128)} %copy-done.6, f32[96,384]{1,0:T(8,128)} %copy-done.4, f32[96,384]{1,0:T(8,128)} %copy-done.7, f32[2,192,384]{2,1,0:T(8,128)} %bitcast.37), custom_call_target="tpu_custom_call" | custom-call | tf_op jit(solution)/shard_map/residual_share/pallas_call | solution.py:382
  195.3 6.1 %all-to-all-start.3 = ((f32[64,1,128]{2,1,0:T(1,128)}), f32[64,1,128]{2,1,0:T(1,128)S(1)}, u32[]{:S(2)}, u32[]{:S(2)}) async-start(f32[64,1,128]{2,1,0:T(1,128)} %get-tuple-element.17), calls=%async_computation.3 | async-start | bytes 65536 | tf_op jit(solution)/shard_map/all_to_all | solution.py:472
  201.4 2.2 %image_update.1 = f32[2,192,384]{2,1,0:T(8,128)} custom-call(f32[8,128]{1,0:T(8,128)} %get-tuple-element.16.sums_ref, f32[2,192,384]{2,1,0:T(8,128)} %bitcast.38, f32[2,192,384]{2,1,0:T(8,128)} %bitcast.34), custom_call_target="tpu_custom_call" | custom-call | tf_op jit(solution)/shard_map/image_update/pallas_call | solution.py:402
  203.6 6.4 %all-to-all-done.3.parts_ref = f32[64,1,128]{2,1,0:T(1,128)S(1)} async-done(((f32[64,1,128]{2,1,0:T(1,128)}), f32[64,1,128]{2,1,0:T(1,128)S(1)}, u32[]{:S(2)}, u32[]{:S(2)}) %all-to-all-start.3) | async-done | bytes 32800 | tf_op jit(solution)/shard_map/all_to_all | solution.py:472
  211.3 2.4 %finish.1 = (f32[2,192,384]{2,1,0:T(8,128)}, f32[2,192,384]{2,1,0:T(8,128)}) custom-call(f32[8,128]{1,0:T(8,128)} %get-tuple-element.16.sums_ref, f32[64,1,128]{2,1,0:T(1,128)} %copy-done.14, f32[2,192,384]{2,1,0:T(8,128)} %bitcast.35, f32[192,384]{1,0:T(8,128)} %get-tuple-element.18.own_ref, f32[192,384]{1,0:T(8,128)} %copy-done.5), custom_call_target="tpu_custom_call" | custom-call | tf_op jit(solution)/shard_map/finish/pallas_call | solution.py:422
  (54 shorter events, 11.2 us)
Async XLA Ops:
  5.1 22.9 %all-to-all-start.1 = ((f32[32,16,128]{2,1,0:T(8,128)}), f32[32,16,128]{2,1,0:T(8,128)S(1)}, u32[]{:S(2)}, u32[]{:S(2)}) async-start(f32[32,16,128]{2,1,0:T(8,128)} %gram_rows.1), calls=%async_computation.1 | async-start | bytes 524288 | tf_op jit(solution)/shard_map/all_to_all | solution.py:450
  24.4 24.1 %copy-start.1 = (f32[12,384,32]{1,2,0:T(8,128)S(1)}, f32[12,384,32]{1,2,0:T(8,128)}, u32[]{:S(2)}) copy-start(f32[12,384,32]{1,2,0:T(8,128)} %param.19) | copy-start | bytes 1769476
  28.0 6.4 %copy-start.2 = (f32[32,16,128]{2,1,0:T(8,128)}, f32[32,16,128]{2,1,0:T(8,128)S(1)}, u32[]{:S(2)}) copy-start(f32[32,16,128]{2,1,0:T(8,128)S(1)} %all-to-all-done.1.in_ref) | copy-start | bytes 786436
  28.0 60.6 %all-to-all-start = ((f32[32,144,128]{2,1,0:T(8,128)}), f32[32,144,128]{2,1,0:T(8,128)S(1)}, u32[]{:S(2)}, u32[]{:S(2)}) async-start(f32[32,144,128]{2,1,0:T(8,128)} %forward_y.1), calls=%async_computation | async-start | bytes 4718592 | tf_op jit(solution)/shard_map/all_to_all | solution.py:456
  36.7 8.3 %collective-permute-start.2 = (f32[288,128]{1,0:T(8,128)}, f32[288,128]{1,0:T(8,128)S(1)}, u32[]{:S(2)}, u32[]{:S(2)}) collective-permute-start(f32[288,128]{1,0:T(8,128)} %gram_sum.1.rest_0_), channel_id=1, source_target_pairs={{0,6},{2,0},{4,2},{6,4},{1,7},{3,1},{5,3},{7,5},{8,14},{10,8},{12,... | collective-permute-start | bytes 442376 | tf_op jit(solution)/shard_map/ppermute | solution.py:441
  39.4 7.5 %collective-permute-start.1 = (f32[288,128]{1,0:T(8,128)}, f32[288,128]{1,0:T(8,128)S(1)}, u32[]{:S(2)}, u32[]{:S(2)}) collective-permute-start(f32[288,128]{1,0:T(8,128)} %gram_sum.1.rest_0_), channel_id=1, source_target_pairs={{0,4},{2,6},{4,0},{6,2},{1,5},{3,7},{5,1},{7,3},{8,12},{10,14},{12... | collective-permute-start | bytes 442376 | tf_op jit(solution)/shard_map/ppermute | solution.py:441
  40.2 8.3 %collective-permute-start = (f32[288,128]{1,0:T(8,128)}, f32[288,128]{1,0:T(8,128)S(1)}, u32[]{:S(2)}, u32[]{:S(2)}) collective-permute-start(f32[288,128]{1,0:T(8,128)} %gram_sum.1.rest_0_), channel_id=1, source_target_pairs={{0,2},{2,4},{4,6},{6,0},{1,3},{3,5},{5,7},{7,1},{8,10},{10,12},{12... | collective-permute-start | bytes 442376 | tf_op jit(solution)/shard_map/ppermute | solution.py:441
  41.1 8.2 %collective-permute-start.3 = (f32[288,128]{1,0:T(8,128)}, f32[288,128]{1,0:T(8,128)S(1)}, u32[]{:S(2)}, u32[]{:S(2)}) collective-permute-start(f32[288,128]{1,0:T(8,128)} %gram_sum.1.rest_0_), channel_id=1, source_target_pairs={{0,1},{1,0},{2,3},{3,2},{4,5},{5,4},{6,7},{7,6},{8,9},{9,8},{10,11... | collective-permute-start | bytes 442376 | tf_op jit(solution)/shard_map/ppermute | solution.py:433
  44.9 43.7 %copy-start.8 = (f32[288,128]{1,0:T(8,128)}, f32[288,128]{1,0:T(8,128)S(1)}, u32[]{:S(2)}) copy-start(f32[288,128]{1,0:T(8,128)S(1)} %collective-permute-done.2.rest_3_) | copy-start | bytes 442372
  45.0 4.3 %collective-permute-start.6 = (f32[288,128]{1,0:T(8,128)S(1)}, f32[288,128]{1,0:T(8,128)S(1)}, u32[]{:S(2)}, u32[]{:S(2)}) collective-permute-start(f32[288,128]{1,0:T(8,128)S(1)} %collective-permute-done.2.rest_3_), channel_id=1, source_target_pairs={{0,1},{1,0},{2,3},{3,2},{4,5},{5,4},{6,7},{7,6},{8,9},{9,8},{10,11... | collective-permute-start | bytes 442376 | tf_op jit(solution)/shard_map/ppermute | solution.py:433
  47.0 41.7 %copy-start.9 = (f32[288,128]{1,0:T(8,128)}, f32[288,128]{1,0:T(8,128)S(1)}, u32[]{:S(2)}) copy-start(f32[288,128]{1,0:T(8,128)S(1)} %collective-permute-done.1.rest_2_) | copy-start | bytes 442372
  47.0 2.3 %collective-permute-start.5 = (f32[288,128]{1,0:T(8,128)S(1)}, f32[288,128]{1,0:T(8,128)S(1)}, u32[]{:S(2)}, u32[]{:S(2)}) collective-permute-start(f32[288,128]{1,0:T(8,128)S(1)} %collective-permute-done.1.rest_2_), channel_id=1, source_target_pairs={{0,1},{1,0},{2,3},{3,2},{4,5},{5,4},{6,7},{7,6},{8,9},{9,8},{10,11... | collective-permute-start | bytes 442376 | tf_op jit(solution)/shard_map/ppermute | solution.py:433
  48.5 40.1 %copy-start.10 = (f32[288,128]{1,0:T(8,128)}, f32[288,128]{1,0:T(8,128)S(1)}, u32[]{:S(2)}) copy-start(f32[288,128]{1,0:T(8,128)S(1)} %collective-permute-done.rest_1_) | copy-start | bytes 442372
  48.5 2.1 %collective-permute-start.4 = (f32[288,128]{1,0:T(8,128)S(1)}, f32[288,128]{1,0:T(8,128)}, u32[]{:S(2)}, u32[]{:S(2)}) collective-permute-start(f32[288,128]{1,0:T(8,128)S(1)} %collective-permute-done.rest_1_), channel_id=1, source_target_pairs={{0,1},{1,0},{2,3},{3,2},{4,5},{5,4},{6,7},{7,6},{8,9},{9,8},{10,11... | collective-permute-start | bytes 442376 | tf_op jit(solution)/shard_map/ppermute | solution.py:433
  49.3 39.4 %copy-start.11 = (f32[288,128]{1,0:T(8,128)}, f32[288,128]{1,0:T(8,128)S(1)}, u32[]{:S(2)}) copy-start(f32[288,128]{1,0:T(8,128)S(1)} %collective-permute-done.3.rest_4_) | copy-start | bytes 442372
  175.1 1.6 collective-permute-start.7
  175.1 4.1 %collective-permute-start.10 = (f32[96,384]{1,0:T(8,128)}, f32[96,384]{1,0:T(8,128)S(1)}, u32[]{:S(2)}, u32[]{:S(2)}) collective-permute-start(f32[96,384]{1,0:T(8,128)} %get-tuple-element.15), channel_id=1, source_target_pairs={{0,1},{1,0},{2,3},{3,2},{4,5},{5,4},{6,7},{7,6},{8,9},{9,8},{10,11... | collective-permute-start | bytes 442376 | tf_op jit(solution)/shard_map/ppermute | solution.py:433
  177.6 6.2 %collective-permute-start.8 = (f32[104,384]{1,0:T(8,128)S(1)}, f32[104,384]{1,0:T(8,128)S(1)}, u32[]{:S(2)}, u32[]{:S(2)}) collective-permute-start(f32[104,384]{1,0:T(8,128)S(1)} %add.12), channel_id=1, source_target_pairs={{0,2},{2,0},{4,6},{6,4},{1,3},{3,1},{5,7},{7,5},{8,10},{10,8},{12,... | collective-permute-start | bytes 479240 | tf_op jit(solution)/shard_map/ppermute | solution.py:437
  180.1 6.9 %collective-permute-start.11 = (f32[96,384]{1,0:T(8,128)S(1)}, f32[96,384]{1,0:T(8,128)S(1)}, u32[]{:S(2)}, u32[]{:S(2)}) collective-permute-start(f32[96,384]{1,0:T(8,128)S(1)} %add.14), channel_id=1, source_target_pairs={{0,6},{2,4},{4,2},{6,0},{1,7},{3,5},{5,3},{7,1},{8,14},{10,12},{12... | collective-permute-start | bytes 442376 | tf_op jit(solution)/shard_map/ppermute | solution.py:437
  183.9 8.4 %copy-start.3 = (f32[104,384]{1,0:T(8,128)}, f32[104,384]{1,0:T(8,128)S(1)}, u32[]{:S(2)}) copy-start(f32[104,384]{1,0:T(8,128)S(1)} %add.13.a_ref) | copy-start | bytes 479236
  183.9 8.4 %collective-permute-start.9 = (f32[104,384]{1,0:T(8,128)S(1)}, f32[104,384]{1,0:T(8,128)S(1)}, u32[]{:S(2)}, u32[]{:S(2)}) collective-permute-start(f32[104,384]{1,0:T(8,128)S(1)} %add.13.a_ref), channel_id=1, source_target_pairs={{0,6},{2,4},{4,2},{6,0},{1,7},{3,5},{5,3},{7,1},{8,14},{10,12},{12... | collective-permute-start | bytes 479240 | tf_op jit(solution)/shard_map/ppermute | solution.py:437
  187.1 5.2 %collective-permute-start.12 = (f32[96,384]{1,0:T(8,128)S(1)}, f32[96,384]{1,0:T(8,128)S(1)}, u32[]{:S(2)}, u32[]{:S(2)}) collective-permute-start(f32[96,384]{1,0:T(8,128)S(1)} %add.15.b_ref), channel_id=1, source_target_pairs={{0,2},{2,0},{4,6},{6,4},{1,3},{3,1},{5,7},{7,5},{8,10},{10,8},{12,... | collective-permute-start | bytes 442376 | tf_op jit(solution)/shard_map/ppermute | solution.py:437
  195.3 14.7 %collective-permute-start.13 = (f32[192,384]{1,0:T(8,128)}, f32[192,384]{1,0:T(8,128)S(1)}, u32[]{:S(2)}, u32[]{:S(2)}) collective-permute-start(f32[192,384]{1,0:T(8,128)} %get-tuple-element.18.own_ref), channel_id=1, source_target_pairs={{0,1},{1,0},{2,3},{3,2},{4,5},{5,4},{6,7},{7,6},{8,9},{9,8},{10,11... | collective-permute-start | bytes 884744 | tf_op jit(solution)/shard_map/ppermute | solution.py:433
  195.3 14.7 %all-to-all-start.3 = ((f32[64,1,128]{2,1,0:T(1,128)}), f32[64,1,128]{2,1,0:T(1,128)S(1)}, u32[]{:S(2)}, u32[]{:S(2)}) async-start(f32[64,1,128]{2,1,0:T(1,128)} %get-tuple-element.17), calls=%async_computation.3 | async-start | bytes 65536 | tf_op jit(solution)/shard_map/all_to_all | solution.py:472
  (8 other events, 10.7 us)

commit v4 on v3

--- a/solution.py
+++ b/solution.py
@@ -28,7 +28,8 @@
 BLOCK = 24 * PAIRS
 HALF = LANES // 2
 COILS = HALF // PLANES
-VMEM_LIMIT = 56 * 1024 * 1024
+VMEM_LIMIT = 32 * 1024 * 1024
+VMEM_ALL = 56 * 1024 * 1024
 F32 = jnp.float32
 BF16 = jnp.bfloat16
 NT = (((1,), (1,)), ((), ()))
@@ -86,6 +87,18 @@
     return lax.dot_general(a, b, NT, preferred_element_type=F32)
 
 
+def near(*arrays):
+    return [pltpu.with_memory_space_constraint(a, pltpu.VMEM) for a in arrays]
+
+
+def far(*arrays):
+    return [pltpu.with_memory_space_constraint(a, pltpu.HBM) for a in arrays]
+
+
+def near_out(*shape):
+    return pltpu.VMEM(shape, F32)
+
+
 def whole(array):
     return pl.BlockSpec(array.shape, lambda i: (0,) * array.ndim)
 
@@ -197,21 +210,20 @@
     return jnp.concatenate(parts, axis=0)
 
 
-def middle_kernel(norm_ref, in_hbm, *rest):
+def middle_kernel(norm_ref, in_ref, *rest):
     g_hbm, tables_hbm = rest[:8], rest[8:12]
-    out_hbm, in_ref, table_ref, g_ref, grid_ref, out_ref, in_sem, table_sem, g_sem, out_sem = rest[12:]
+    out_ref, table_ref, g_ref, grid_ref, table_sem, g_sem = rest[12:]
     fh_ref, fl_ref, bh_ref, bl_ref = (table_ref.at[i] for i in range(4))
     xpos, core = lax.axis_index("x"), lax.axis_index("core")
-    load_in = pltpu.make_async_copy(in_hbm, in_ref, in_sem)
     load_tables = [pltpu.make_async_copy(tables_hbm[i], table_ref.at[i], table_sem.at[i]) for i in range(4)]
     load_g = []
     for d in range(4):
         for k in range(2):
             c = 2 * lax.rem(xpos + 4 - d, 4) + lax.rem(core + k, 2)
             load_g.append(pltpu.make_async_copy(g_hbm[4 * k + d], g_ref.at[c], g_sem.at[4 * k + d]))
-    for copy in [load_in] + load_tables[:2] + load_g + load_tables[2:]:
+    for copy in load_tables[:2] + load_g + load_tables[2:]:
         copy.start()
-    for copy in [load_in] + load_tables[:2]:
+    for copy in load_tables[:2]:
         copy.wait()
     for p in range(PAIRS):
         pieces = [arrived_rows(in_ref, 2 * p + i, BLOCK) for i in range(2)]
@@ -240,40 +252,30 @@
     norm = jnp.broadcast_to(norm_ref[...], (8, LANES)) / (8 * LANES)
     sums = jnp.where(lax.broadcasted_iota(jnp.int32, (8, LANES), 0) == 0, jnp.sum(curve, axis=0, keepdims=True), norm)
     out_ref[:, BLOCK:, :] = jnp.broadcast_to(sums[None], (SLABS, 8, LANES))
-    stores = [pltpu.make_async_copy(out_ref.at[:, BLOCK:, :], out_hbm.at[:, BLOCK:, :], out_sem.at[PAIRS])]
-    stores[0].start()
     for p in range(PAIRS):
         pieces = [grid_ref[b // TY, pl.ds(b % TY, N, stride=TY), :] for b in (2 * p, 2 * p + 1)]
         done = transform(bh_ref, bl_ref, pieces, [times_i(x) for x in pieces])
         store_outgoing(out_ref, 24 * p, done[:, :LANES], done[:, LANES:])
-        rows = pl.ds(24 * p, 24)
-        stores.append(pltpu.make_async_copy(out_ref.at[:, rows, :], out_hbm.at[:, rows, :], out_sem.at[p]))
-        stores[-1].start()
-    for copy in stores:
-        copy.wait()
 
 
 def middle(norm, arrived, grams, table_in, table_out):
+    vmem = pl.BlockSpec(memory_space=pltpu.VMEM)
     hbm = pl.BlockSpec(memory_space=pltpu.HBM)
     return pl.pallas_call(
         middle_kernel,
-        in_specs=[pl.BlockSpec(memory_space=pltpu.VMEM)] + [hbm] * 13,
-        out_specs=hbm,
-        out_shape=jax.ShapeDtypeStruct((SLABS, BLOCK + 8, LANES), F32),
+        in_specs=[vmem] * 2 + [hbm] * 12,
+        out_specs=vmem,
+        out_shape=near_out(SLABS, BLOCK + 8, LANES),
         scratch_shapes=[
-            pltpu.VMEM((SLABS * BLOCK, LANES), F32),
             pltpu.VMEM((4, N, 2 * N), BF16),
             pltpu.VMEM((8, TILES // 2 * 8, LANES), F32),
             pltpu.VMEM((ROWS // TY, N * TY, LANES), F32),
-            pltpu.VMEM((SLABS, BLOCK + 8, LANES), F32),
-            pltpu.SemaphoreType.DMA,
             pltpu.SemaphoreType.DMA((4,)),
             pltpu.SemaphoreType.DMA((8,)),
-            pltpu.SemaphoreType.DMA((PAIRS + 1,)),
         ],
         compiler_params=pltpu.CompilerParams(vmem_limit_bytes=VMEM_LIMIT),
         name="middle",
-    )(norm, arrived, *grams, *table_in, *table_out)
+    )(norm, *near(arrived), *far(*grams, *table_in, *table_out))
 
 
 def backward_y_kernel(in_ref, s_ref, maps_ref, gather_ref, high_ref, low_ref, *rest):
@@ -316,7 +318,7 @@
 
 def backward_y(arrived, maps, sel_maps, sel_gather, table):
     vmem = pl.BlockSpec(memory_space=pltpu.VMEM)
-    quarters = [jax.ShapeDtypeStruct((QUARTER + 8, N), F32), jax.ShapeDtypeStruct((QUARTER, N), F32)]
+    quarters = [near_out(QUARTER + 8, N), near_out(QUARTER, N)]
     return pl.pallas_call(
         backward_y_kernel,
         in_specs=[vmem] * 6,
@@ -324,7 +326,7 @@
         out_shape=quarters * 2,
         compiler_params=pltpu.CompilerParams(vmem_limit_bytes=VMEM_LIMIT),
         name="backward_y",
-    )(arrived, maps, sel_maps, sel_gather, *table)
+    )(*near(arrived, maps, sel_maps, sel_gather, *table))
 
 
 def gram_kernel(counts_ref, w_ref, out_ref):
@@ -355,9 +357,9 @@
         in_specs=[pl.BlockSpec(memory_space=pltpu.SMEM), pl.BlockSpec((owners, CAP, CELLS, SB), lambda i: (i, 0, 0, 0))],
         out_specs=pl.BlockSpec((owners, 16, LANES), lambda i: (i, 0, 0)),
         out_shape=jax.ShapeDtypeStruct((SLABS, 16, LANES), F32),
-        compiler_params=pltpu.CompilerParams(vmem_limit_bytes=VMEM_LIMIT),
+        compiler_params=pltpu.CompilerParams(vmem_limit_bytes=VMEM_ALL),
         name="gram_rows",
-    )(counts, interp)
+    )(counts, *far(interp))
 
 
 def share_kernel(a_ref, more_a_ref, b_ref, more_b_ref, residual_ref, out_ref, part_ref, sums_ref):
@@ -384,13 +386,13 @@
         in_specs=[vmem] * 5,
         out_specs=[vmem] * 3,
         out_shape=[
-            jax.ShapeDtypeStruct((HALF_ROWS, N), F32),
-            jax.ShapeDtypeStruct((2 * SLABS, 1, LANES), F32),
-            jax.ShapeDtypeStruct((8, LANES), F32),
+            near_out(HALF_ROWS, N),
+            near_out(2 * SLABS, 1, LANES),
+            near_out(8, LANES),
         ],
         compiler_params=pltpu.CompilerParams(vmem_limit_bytes=VMEM_LIMIT),
         name="residual_share",
-    )(*first, *second, residual)
+    )(*near(*first, *second, residual))
 
 
 def image_kernel(sums_ref, image_ref, direction_ref, out_ref):
@@ -405,7 +407,7 @@
         out_specs=vmem,
         out_shape=jax.ShapeDtypeStruct(image.shape, F32),
         name="image_update",
-    )(sums, image, direction)
+    )(*near(sums, image, direction))
 
 
 def finish_kernel(sums_ref, parts_ref, direction_ref, own_ref, other_ref, residual_ref, next_ref):
@@ -426,7 +428,7 @@
         out_shape=[full, full],
         compiler_params=pltpu.CompilerParams(vmem_limit_bytes=VMEM_LIMIT),
         name="finish",
-    )(sums, parts, direction, own, other)
+    )(*near(sums, parts, direction, own, other))
 
 
 def swap_core(value):

time: 216 us -> 204 us (0.944)
  Pallas kernels: 41.8 us -> 29.1 us
    pallas_call x1, Pallas kernels: 8.58 us -> 5.54 us  [backward_y(): pl.pallas_call(backward_y_kernel, in_specs=[vmem] * 6, out_specs=[vmem] *...]
    pallas_call x1, Pallas kernels: 7.64 us -> 5.12 us  [forward_y(): pl.pallas_call(forward_y_kernel, grid=(ROWS // 4,), in_specs=[pl.BlockSpe...]
    pallas_call x1, Pallas kernels: 12 us -> 9.76 us  [middle(): pl.pallas_call(middle_kernel, in_specs=[vmem] * 2 + [hbm] * 12, out_specs...]
    unnamed x30 -> x48, local copies, waits for them, and re-layouts: 4.77 us -> 5.5 us
  transfers between devices with their start and end apart: 17 -> 17, of which waited for: 10 -> 9; matrix products, arithmetic and copies ran while one was open for 1% -> 0% of each run, Pallas kernels for 6% -> 4%
where the time goes in v4:
time: 204 us; the launch traced here: 202 us
  waiting for transfers between devices  64.7 us (32%)
  blocking collectives  64.2 us (31%)
  starting transfers between devices  36.3 us (18%)
  Pallas kernels  29.1 us (14%)
  local copies, waits for them, and re-layouts  5.5 us (3%)
    all_to_all x1, blocking collectives, body(): lax.all_to_all(outgoing, SLAB, split_axis=0, concat_axis=0, tiled=True)  64.2 us
    all_to_all x1, waiting for transfers between devices, body(): lax.all_to_all(outgoing, SLAB, split_axis=0, concat_axis=0, tiled=True)  38.1 us
    all_to_all x1, starting transfers between devices, body(): grams = lax.all_to_all(grams, SLAB, split_axis=0, concat_axis=0, tiled=True)  11.7 us
    pallas_call x1, Pallas kernels, middle(): pl.pallas_call(middle_kernel, in_specs=[vmem] * 2 + [hbm] * 12, out_specs...  9.76 us
    all_to_all x1, waiting for transfers between devices, body(): lax.all_to_all(parts, SLAB + ('core',), split_axis=0, concat_axis=0, tile...  7.58 us
    ppermute x4, waiting for transfers between devices, swap_x(): return lax.ppermute(value, 'x', [(i, i ^ mask) for i in range(4)])  7.4 us
    ppermute x3, waiting for transfers between devices, from_x(): lax.ppermute(value, 'x', [(i, (i + d) % 4) for i in range(4)])  7.16 us
    ppermute x4, starting transfers between devices, swap_x(): return lax.ppermute(value, 'x', [(i, i ^ mask) for i in range(4)])  6.91 us
  transfers between devices with their start and end apart: 17, of which 9 were waited for; matrix products, arithmetic and copies ran while one was open for 0% of the time, Pallas kernels for 4%

profile of v4, /device:TPU:8, one launch (start us, length us, event | category | flops | bytes accessed | tf_op | source)
XLA Modules:
  0.0 201.7 jit_solution(13446092953164996915)
XLA Ops:
  0.7 4.6 %gram_rows.1 = f32[32,16,128]{2,1,0:T(8,128)} custom-call(s32[4,32]{1,0:T(4,128)} %bitcast.41, f32[32,4,64,128]{3,2,1,0:T(8,128)} %bitcast.39), custom_call_target="tpu_custom_call" | custom-call | tf_op jit(solution)/shard_map/gram_rows/pallas_call | solution.py:354
  5.3 11.7 %all-to-all-start.1 = ((f32[32,16,128]{2,1,0:T(8,128)}), f32[32,16,128]{2,1,0:T(8,128)S(1)}, u32[]{:S(2)}, u32[]{:S(2)}) async-start(f32[32,16,128]{2,1,0:T(8,128)} %gram_rows.1), calls=%async_computation.1 | async-start | bytes 524288 | tf_op jit(solution)/shard_map/all_to_all | solution.py:452
  17.1 1.0 copy-done.13
  18.1 5.1 %forward_y.1 = f32[32,144,128]{2,1,0:T(8,128)S(1)} custom-call(f32[12,32,384]{2,1,0:T(8,128)S(1)} %bitcast.33, bf16[12,384,128]{2,1,0:T(8,128)(2,1)S(1)} %copy-done.2, bf16[128,256]{1,0:T(8,128)(2,1)S(1)} %copy-done.14, bf16[256,1024]{1,0:T(8,128)(2,1)S(1)} %copy-done.13, bf16[384,768]{1,0:T(8,128)(2,1)S(1)} %copy-done.10, bf16[384,768]{1,0:T(8,128)(2,1)S(1)} %copy-done.9), custom_call_target="tpu_custom_call" | custom-call | tf_op jit(solution)/shard_map/forward_y/pallas_call | solution.py:187
  23.2 1.4 copy-done
  24.7 3.6 %all-to-all-done.1.in_ref = f32[32,16,128]{2,1,0:T(8,128)S(1)} async-done(((f32[32,16,128]{2,1,0:T(8,128)}), f32[32,16,128]{2,1,0:T(8,128)S(1)}, u32[]{:S(2)}, u32[]{:S(2)}) %all-to-all-start.1) | async-done | bytes 262176 | tf_op jit(solution)/shard_map/all_to_all | solution.py:452
  28.9 6.2 %all-to-all-start = ((f32[32,144,128]{2,1,0:T(8,128)}), f32[32,144,128]{2,1,0:T(8,128)S(1)}, u32[]{:S(2)}, u32[]{:S(2)}) async-start(f32[32,144,128]{2,1,0:T(8,128)} %copy-done), calls=%async_computation | async-start | bytes 4718592 | tf_op jit(solution)/shard_map/all_to_all | solution.py:458
  36.1 1.2 gram_sum.1.rest_0_
  37.4 2.8 %collective-permute-start.2 = (f32[288,128]{1,0:T(8,128)S(1)}, f32[288,128]{1,0:T(8,128)S(1)}, u32[]{:S(2)}, u32[]{:S(2)}) collective-permute-start(f32[288,128]{1,0:T(8,128)S(1)} %gram_sum.1.rest_0_), channel_id=1, source_target_pairs={{0,6},{2,0},{4,2},{6,4},{1,7},{3,1},{5,3},{7,5},{8,14},{10,8},{12,... | collective-permute-start | bytes 442376 | tf_op jit(solution)/shard_map/ppermute | solution.py:443
  41.9 3.5 %collective-permute-done.2.rest_3_ = f32[288,128]{1,0:T(8,128)S(1)} collective-permute-done((f32[288,128]{1,0:T(8,128)S(1)}, f32[288,128]{1,0:T(8,128)S(1)}, u32[]{:S(2)}, u32[]{:S(2)}) %collective-permute-start.2) | collective-permute-done | bytes 147488 | tf_op jit(solution)/shard_map/ppermute | solution.py:443
  45.4 2.1 %collective-permute-done.1.rest_2_ = f32[288,128]{1,0:T(8,128)S(1)} collective-permute-done((f32[288,128]{1,0:T(8,128)S(1)}, f32[288,128]{1,0:T(8,128)S(1)}, u32[]{:S(2)}, u32[]{:S(2)}) %collective-permute-start.1) | collective-permute-done | bytes 147488 | tf_op jit(solution)/shard_map/ppermute | solution.py:443
  47.6 1.5 collective-permute-done.rest_1_
  51.3 38.1 %all-to-all-done = f32[32,144,128]{2,1,0:T(8,128)S(1)} async-done(((f32[32,144,128]{2,1,0:T(8,128)}), f32[32,144,128]{2,1,0:T(8,128)S(1)}, u32[]{:S(2)}, u32[]{:S(2)}) %all-to-all-start) | async-done | bytes 2359328 | tf_op jit(solution)/shard_map/all_to_all | solution.py:458
  89.4 9.8 %middle.1 = f32[32,152,128]{2,1,0:T(8,128)S(1)} custom-call(f32[1,1]{1,0:T(1,128)} %bitcast.1.norm_ref, f32[4608,128]{1,0:T(8,128)S(1)} %bitcast.32, f32[288,128]{1,0:T(8,128)} %copy-done.12, f32[288,128]{1,0:T(8,128)} %copy-done.20, f32[288,128]{1,0:T(8,128)} %copy-done.19, f32[288,128]{1,0:T(8,128)} %copy-done.18, f32[288,128]{1,0:T(8,128)} %copy-done.21, ...), custom_call_target="tpu_custom_call" | custom-call | tf_op jit(solution)/shard_map/middle/pallas_call | solution.py:264
  99.2 64.2 %all_to_all.20 = f32[32,152,128]{2,1,0:T(8,128)S(1)} all-to-all(f32[32,152,128]{2,1,0:T(8,128)S(1)} %middle.1), channel_id=1, replica_groups=mesh['z'=8,'y'=4,'x'=4,'core'=2] {'z','y'}, dimensions={0} | all-to-all | bytes 4980736 | tf_op jit(solution)/shard_map/all_to_all | solution.py:461
  163.5 5.5 %backward_y.1 = (f32[104,384]{1,0:T(8,128)S(1)}, f32[96,384]{1,0:T(8,128)S(1)}, f32[104,384]{1,0:T(8,128)S(1)}, f32[96,384]{1,0:T(8,128)S(1)}) custom-call(f32[4864,128]{1,0:T(8,128)S(1)} %bitcast.31, bf16[12,384,128]{2,1,0:T(8,128)(2,1)S(1)} %copy-done.3, bf16[128,256]{1,0:T(8,128)(2,1)S(1)} %copy-done.15, bf16[1024,128]{1,0:T(8,128)(2,1)S(1)} %copy-done.16, ...), custom_call_target="tpu_custom_call" | custom-call | tf_op jit(solution)/shard_map/backward_y/pallas_call | solution.py:322
  170.8 1.6 collective-permute-start.8
  172.4 2.2 %collective-permute-start.11 = (f32[96,384]{1,0:T(8,128)S(1)}, f32[96,384]{1,0:T(8,128)S(1)}, u32[]{:S(2)}, u32[]{:S(2)}) collective-permute-start(f32[96,384]{1,0:T(8,128)S(1)} %add.14), channel_id=1, source_target_pairs={{0,6},{2,4},{4,2},{6,0},{1,7},{3,5},{5,3},{7,1},{8,14},{10,12},{12... | collective-permute-start | bytes 442376 | tf_op jit(solution)/shard_map/ppermute | solution.py:439
  174.6 2.5 %collective-permute-done.8 = f32[104,384]{1,0:T(8,128)S(1)} collective-permute-done((f32[104,384]{1,0:T(8,128)S(1)}, f32[104,384]{1,0:T(8,128)S(1)}, u32[]{:S(2)}, u32[]{:S(2)}) %collective-permute-start.8) | collective-permute-done | bytes 159776 | tf_op jit(solution)/shard_map/ppermute | solution.py:439
  177.0 2.9 %collective-permute-start.9 = (f32[104,384]{1,0:T(8,128)S(1)}, f32[104,384]{1,0:T(8,128)S(1)}, u32[]{:S(2)}, u32[]{:S(2)}) collective-permute-start(f32[104,384]{1,0:T(8,128)S(1)} %add.13.a_ref), channel_id=1, source_target_pairs={{0,6},{2,4},{4,2},{6,0},{1,7},{3,5},{5,3},{7,1},{8,14},{10,12},{12... | collective-permute-start | bytes 479240 | tf_op jit(solution)/shard_map/ppermute | solution.py:439
  180.2 4.9 %collective-permute-done.12.more_b_ref = f32[96,384]{1,0:T(8,128)S(1)} collective-permute-done((f32[96,384]{1,0:T(8,128)S(1)}, f32[96,384]{1,0:T(8,128)S(1)}, u32[]{:S(2)}, u32[]{:S(2)}) %collective-permute-start.12) | collective-permute-done | bytes 147488 | tf_op jit(solution)/shard_map/ppermute | solution.py:439
  186.0 6.1 %all-to-all-start.3 = ((f32[64,1,128]{2,1,0:T(1,128)}), f32[64,1,128]{2,1,0:T(1,128)S(1)}, u32[]{:S(2)}, u32[]{:S(2)}) async-start(f32[64,1,128]{2,1,0:T(1,128)} %get-tuple-element.17), calls=%async_computation.3 | async-start | bytes 65536 | tf_op jit(solution)/shard_map/all_to_all | solution.py:474
  193.0 7.6 %all-to-all-done.3.parts_ref = f32[64,1,128]{2,1,0:T(1,128)S(1)} async-done(((f32[64,1,128]{2,1,0:T(1,128)}), f32[64,1,128]{2,1,0:T(1,128)S(1)}, u32[]{:S(2)}, u32[]{:S(2)}) %all-to-all-start.3) | async-done | bytes 32800 | tf_op jit(solution)/shard_map/all_to_all | solution.py:474
  200.6 1.1 finish.1
  (72 shorter events, 9.4 us)
Async XLA Ops:
  5.3 22.9 %all-to-all-start.1 = ((f32[32,16,128]{2,1,0:T(8,128)}), f32[32,16,128]{2,1,0:T(8,128)S(1)}, u32[]{:S(2)}, u32[]{:S(2)}) async-start(f32[32,16,128]{2,1,0:T(8,128)} %gram_rows.1), calls=%async_computation.1 | async-start | bytes 524288 | tf_op jit(solution)/shard_map/all_to_all | solution.py:452
  24.7 24.4 %copy-start.4 = (f32[12,384,32]{1,2,0:T(8,128)S(1)}, f32[12,384,32]{1,2,0:T(8,128)}, u32[]{:S(2)}) copy-start(f32[12,384,32]{1,2,0:T(8,128)} %param.19) | copy-start | bytes 1769476
  28.9 60.5 %all-to-all-start = ((f32[32,144,128]{2,1,0:T(8,128)}), f32[32,144,128]{2,1,0:T(8,128)S(1)}, u32[]{:S(2)}, u32[]{:S(2)}) async-start(f32[32,144,128]{2,1,0:T(8,128)} %copy-done), calls=%async_computation | async-start | bytes 4718592 | tf_op jit(solution)/shard_map/all_to_all | solution.py:458
  37.4 8.0 %collective-permute-start.2 = (f32[288,128]{1,0:T(8,128)S(1)}, f32[288,128]{1,0:T(8,128)S(1)}, u32[]{:S(2)}, u32[]{:S(2)}) collective-permute-start(f32[288,128]{1,0:T(8,128)S(1)} %gram_sum.1.rest_0_), channel_id=1, source_target_pairs={{0,6},{2,0},{4,2},{6,4},{1,7},{3,1},{5,3},{7,5},{8,14},{10,8},{12,... | collective-permute-start | bytes 442376 | tf_op jit(solution)/shard_map/ppermute | solution.py:443
  40.2 7.3 %collective-permute-start.1 = (f32[288,128]{1,0:T(8,128)S(1)}, f32[288,128]{1,0:T(8,128)S(1)}, u32[]{:S(2)}, u32[]{:S(2)}) collective-permute-start(f32[288,128]{1,0:T(8,128)S(1)} %gram_sum.1.rest_0_), channel_id=1, source_target_pairs={{0,4},{2,6},{4,0},{6,2},{1,5},{3,7},{5,1},{7,3},{8,12},{10,14},{12... | collective-permute-start | bytes 442376 | tf_op jit(solution)/shard_map/ppermute | solution.py:443
  41.0 8.1 %collective-permute-start = (f32[288,128]{1,0:T(8,128)S(1)}, f32[288,128]{1,0:T(8,128)S(1)}, u32[]{:S(2)}, u32[]{:S(2)}) collective-permute-start(f32[288,128]{1,0:T(8,128)S(1)} %gram_sum.1.rest_0_), channel_id=1, source_target_pairs={{0,2},{2,4},{4,6},{6,0},{1,3},{3,5},{5,7},{7,1},{8,10},{10,12},{12... | collective-permute-start | bytes 442376 | tf_op jit(solution)/shard_map/ppermute | solution.py:443
  41.9 8.0 %collective-permute-start.3 = (f32[288,128]{1,0:T(8,128)S(1)}, f32[288,128]{1,0:T(8,128)S(1)}, u32[]{:S(2)}, u32[]{:S(2)}) collective-permute-start(f32[288,128]{1,0:T(8,128)S(1)} %gram_sum.1.rest_0_), channel_id=1, source_target_pairs={{0,1},{1,0},{2,3},{3,2},{4,5},{5,4},{6,7},{7,6},{8,9},{9,8},{10,11... | collective-permute-start | bytes 442376 | tf_op jit(solution)/shard_map/ppermute | solution.py:435
  45.4 4.5 %collective-permute-start.6 = (f32[288,128]{1,0:T(8,128)S(1)}, f32[288,128]{1,0:T(8,128)S(1)}, u32[]{:S(2)}, u32[]{:S(2)}) collective-permute-start(f32[288,128]{1,0:T(8,128)S(1)} %collective-permute-done.2.rest_3_), channel_id=1, source_target_pairs={{0,1},{1,0},{2,3},{3,2},{4,5},{5,4},{6,7},{7,6},{8,9},{9,8},{10,11... | collective-permute-start | bytes 442376 | tf_op jit(solution)/shard_map/ppermute | solution.py:435
  47.5 2.4 %collective-permute-start.5 = (f32[288,128]{1,0:T(8,128)S(1)}, f32[288,128]{1,0:T(8,128)S(1)}, u32[]{:S(2)}, u32[]{:S(2)}) collective-permute-start(f32[288,128]{1,0:T(8,128)S(1)} %collective-permute-done.1.rest_2_), channel_id=1, source_target_pairs={{0,1},{1,0},{2,3},{3,2},{4,5},{5,4},{6,7},{7,6},{8,9},{9,8},{10,11... | collective-permute-start | bytes 442376 | tf_op jit(solution)/shard_map/ppermute | solution.py:435
  49.1 2.2 %collective-permute-start.4 = (f32[288,128]{1,0:T(8,128)S(1)}, f32[288,128]{1,0:T(8,128)}, u32[]{:S(2)}, u32[]{:S(2)}) collective-permute-start(f32[288,128]{1,0:T(8,128)S(1)} %collective-permute-done.rest_1_), channel_id=1, source_target_pairs={{0,1},{1,0},{2,3},{3,2},{4,5},{5,4},{6,7},{7,6},{8,9},{9,8},{10,11... | collective-permute-start | bytes 442376 | tf_op jit(solution)/shard_map/ppermute | solution.py:435
  99.2 64.3 %copy-start.3 = (bf16[12,384,128]{2,1,0:T(8,128)(2,1)S(1)}, bf16[12,384,128]{2,1,0:T(8,128)(2,1)}, u32[]{:S(2)}) copy-start(bf16[12,384,128]{2,1,0:T(8,128)(2,1)} %s_ref.3) | copy-start | bytes 3538948
  99.2 64.3 %copy-start.7 = (bf16[384,768]{1,0:T(8,128)(2,1)S(1)}, bf16[384,768]{1,0:T(8,128)(2,1)}, u32[]{:S(2)}) copy-start(bf16[384,768]{1,0:T(8,128)(2,1)} %constant.31.clone.low_ref) | copy-start | bytes 1769476
  99.2 64.3 %copy-start.8 = (bf16[384,768]{1,0:T(8,128)(2,1)S(1)}, bf16[384,768]{1,0:T(8,128)(2,1)}, u32[]{:S(2)}) copy-start(bf16[384,768]{1,0:T(8,128)(2,1)} %constant.30.clone.high_ref) | copy-start | bytes 1769476
  99.2 64.3 %copy-start.15 = (bf16[128,256]{1,0:T(8,128)(2,1)S(1)}, bf16[128,256]{1,0:T(8,128)(2,1)}, u32[]{:S(2)}) copy-start(bf16[128,256]{1,0:T(8,128)(2,1)} %constant.32.clone.maps_ref) | copy-start | bytes 196612
  99.2 64.3 %copy-start.16 = (bf16[1024,128]{1,0:T(8,128)(2,1)S(1)}, bf16[1024,128]{1,0:T(8,128)(2,1)}, u32[]{:S(2)}) copy-start(bf16[1024,128]{1,0:T(8,128)(2,1)} %constant.34.clone.gather_ref) | copy-start | bytes 786436
  169.0 23.0 %copy-start.11 = (f32[12,384,32]{1,2,0:T(8,128)S(1)}, f32[12,384,32]{1,2,0:T(8,128)}, u32[]{:S(2)}) copy-start(f32[12,384,32]{1,2,0:T(8,128)} %param.18) | copy-start | bytes 1769476
  169.0 1.7 collective-permute-start.7
  169.4 3.0 %collective-permute-start.10 = (f32[96,384]{1,0:T(8,128)S(1)}, f32[96,384]{1,0:T(8,128)S(1)}, u32[]{:S(2)}, u32[]{:S(2)}) collective-permute-start(f32[96,384]{1,0:T(8,128)S(1)} %get-tuple-element.15), channel_id=1, source_target_pairs={{0,1},{1,0},{2,3},{3,2},{4,5},{5,4},{6,7},{7,6},{8,9},{9,8},{10,11... | collective-permute-start | bytes 442376 | tf_op jit(solution)/shard_map/ppermute | solution.py:435
  170.8 6.2 %collective-permute-start.8 = (f32[104,384]{1,0:T(8,128)S(1)}, f32[104,384]{1,0:T(8,128)S(1)}, u32[]{:S(2)}, u32[]{:S(2)}) collective-permute-start(f32[104,384]{1,0:T(8,128)S(1)} %add.12), channel_id=1, source_target_pairs={{0,2},{2,0},{4,6},{6,4},{1,3},{3,1},{5,7},{7,5},{8,10},{10,8},{12,... | collective-permute-start | bytes 479240 | tf_op jit(solution)/shard_map/ppermute | solution.py:439
  172.4 7.5 %collective-permute-start.11 = (f32[96,384]{1,0:T(8,128)S(1)}, f32[96,384]{1,0:T(8,128)S(1)}, u32[]{:S(2)}, u32[]{:S(2)}) collective-permute-start(f32[96,384]{1,0:T(8,128)S(1)} %add.14), channel_id=1, source_target_pairs={{0,6},{2,4},{4,2},{6,0},{1,7},{3,5},{5,3},{7,1},{8,14},{10,12},{12... | collective-permute-start | bytes 442376 | tf_op jit(solution)/shard_map/ppermute | solution.py:439
  177.0 8.1 %collective-permute-start.9 = (f32[104,384]{1,0:T(8,128)S(1)}, f32[104,384]{1,0:T(8,128)S(1)}, u32[]{:S(2)}, u32[]{:S(2)}) collective-permute-start(f32[104,384]{1,0:T(8,128)S(1)} %add.13.a_ref), channel_id=1, source_target_pairs={{0,6},{2,4},{4,2},{6,0},{1,7},{3,5},{5,3},{7,1},{8,14},{10,12},{12... | collective-permute-start | bytes 479240 | tf_op jit(solution)/shard_map/ppermute | solution.py:439
  179.9 5.2 %collective-permute-start.12 = (f32[96,384]{1,0:T(8,128)S(1)}, f32[96,384]{1,0:T(8,128)S(1)}, u32[]{:S(2)}, u32[]{:S(2)}) collective-permute-start(f32[96,384]{1,0:T(8,128)S(1)} %add.15.b_ref), channel_id=1, source_target_pairs={{0,2},{2,0},{4,6},{6,4},{1,3},{3,1},{5,7},{7,5},{8,10},{10,8},{12,... | collective-permute-start | bytes 442376 | tf_op jit(solution)/shard_map/ppermute | solution.py:439
  186.0 14.6 %collective-permute-start.13 = (f32[192,384]{1,0:T(8,128)S(1)}, f32[192,384]{1,0:T(8,128)S(1)}, u32[]{:S(2)}, u32[]{:S(2)}) collective-permute-start(f32[192,384]{1,0:T(8,128)S(1)} %get-tuple-element.18.own_ref), channel_id=1, source_target_pairs={{0,1},{1,0},{2,3},{3,2},{4,5},{5,4},{6,7},{7,6},{8,9},{9,8},{10,11... | collective-permute-start | bytes 884744 | tf_op jit(solution)/shard_map/ppermute | solution.py:435
  186.0 14.6 %all-to-all-start.3 = ((f32[64,1,128]{2,1,0:T(1,128)}), f32[64,1,128]{2,1,0:T(1,128)S(1)}, u32[]{:S(2)}, u32[]{:S(2)}) async-start(f32[64,1,128]{2,1,0:T(1,128)} %get-tuple-element.17), calls=%async_computation.3 | async-start | bytes 65536 | tf_op jit(solution)/shard_map/all_to_all | solution.py:474
  (17 other events, 119.0 us)

commit v5 on v4

--- a/solution.py
+++ b/solution.py
@@ -24,6 +24,8 @@
 COIL = ("x", "core")
 ALL = ("z", "y", "x", "core")
 HALF_ROWS = PAIRS * 2 * PLANES
+ZS = 8
+YS = 4
 QUARTER = HALF_ROWS // 2
 BLOCK = 24 * PAIRS
 HALF = LANES // 2
@@ -131,19 +133,42 @@
         out_ref[2 * m + 1, start + 16:start + 24, :] = jnp.where(lower, pltpu.roll(first, 4, 0), second)
 
 
-def gram_sum_kernel(tiles_ref, in_ref, out_ref, total):
+def regroup_kernel(in_ref, *out_refs):
+    ypos = lax.axis_index("y")
+    for e in range(YS):
+        for z in range(ZS):
+            out_refs[e][z] = in_ref[z, lax.rem(ypos + e, YS)]
+
+
+def regroup(arrived):
+    vmem = pl.BlockSpec(memory_space=pltpu.VMEM)
+    return pl.pallas_call(
+        regroup_kernel,
+        in_specs=[vmem],
+        out_specs=[vmem] * YS,
+        out_shape=[jax.ShapeDtypeStruct((ZS, 16, LANES), F32)] * YS,
+        compiler_params=pltpu.CompilerParams(vmem_limit_bytes=VMEM_ALL),
+        name="regroup",
+    )(arrived)
+
+
+def gram_sum_kernel(tiles_ref, *rest):
+    in_refs, out_ref, total = rest[:YS], rest[YS], rest[YS + 1]
+    ypos = lax.axis_index("y")
     total[...] = jnp.zeros_like(total)
     lane = lax.broadcasted_iota(jnp.int32, (8, LANES), 1)
 
-    def add(r, carry):
-        for j in range(CAP):
-            tile = tiles_ref[j, r]
-            piece = in_ref[r, 8 * (j // 2):8 * (j // 2) + 8, :]
-            keep = lane < CELLS if j % 2 == 0 else lane >= CELLS
-            total[tile] = total[tile] + jnp.where(keep, piece, 0.0)
+    def add(z, carry):
+        for e in range(YS):
+            holder = z * YS + lax.rem(ypos - e + YS, YS)
+            for j in range(CAP):
+                tile = tiles_ref[j, holder]
+                piece = in_refs[e][z, 8 * (j // 2):8 * (j // 2) + 8, :]
+                keep = lane < CELLS if j % 2 == 0 else lane >= CELLS
+                total[tile] = total[tile] + jnp.where(keep, piece, 0.0)
         return carry
 
-    lax.fori_loop(0, SLABS, add, 0)
+    lax.fori_loop(0, ZS, add, 0)
     groups = N // TX // 2
     for b in range(ROWS // TY):
         for m in range(groups):
@@ -158,13 +183,13 @@
 def gram_sum(arrived, tiles):
     return pl.pallas_call(
         gram_sum_kernel,
-        in_specs=[pl.BlockSpec(memory_space=pltpu.SMEM), pl.BlockSpec(memory_space=pltpu.VMEM)],
+        in_specs=[pl.BlockSpec(memory_space=pltpu.SMEM)] + [pl.BlockSpec(memory_space=pltpu.VMEM)] * YS,
         out_specs=pl.BlockSpec(memory_space=pltpu.VMEM),
         out_shape=jax.ShapeDtypeStruct((TILES // 2 * 8, LANES), F32),
         scratch_shapes=[pltpu.VMEM((TILES, 8, LANES), F32)],
-        compiler_params=pltpu.CompilerParams(vmem_limit_bytes=VMEM_LIMIT),
+        compiler_params=pltpu.CompilerParams(vmem_limit_bytes=VMEM_ALL),
         name="gram_sum",
-    )(tiles, arrived)
+    )(tiles, *arrived)
 
 
 def forward_y_kernel(d_ref, s_ref, maps_ref, spread_ref, high_ref, low_ref, out_ref):
@@ -196,10 +221,10 @@
             whole(table[1]),
         ],
         out_specs=pl.BlockSpec((SLABS, 48, LANES), lambda i: (0, i, 0)),
-        out_shape=jax.ShapeDtypeStruct((SLABS, 24 * PAIRS, LANES), F32),
+        out_shape=pltpu.HBM((SLABS, 24 * PAIRS, LANES), F32),
         compiler_params=pltpu.CompilerParams(vmem_limit_bytes=VMEM_LIMIT),
         name="forward_y",
-    )(direction, maps, sel_maps, sel_spread, *table)
+    )(*near(direction, maps, sel_maps), *far(sel_spread), *near(*table))
 
 
 def arrived_rows(ref, index, block):
@@ -357,9 +382,9 @@
         in_specs=[pl.BlockSpec(memory_space=pltpu.SMEM), pl.BlockSpec((owners, CAP, CELLS, SB), lambda i: (i, 0, 0, 0))],
         out_specs=pl.BlockSpec((owners, 16, LANES), lambda i: (i, 0, 0)),
         out_shape=jax.ShapeDtypeStruct((SLABS, 16, LANES), F32),
-        compiler_params=pltpu.CompilerParams(vmem_limit_bytes=VMEM_ALL),
+        compiler_params=pltpu.CompilerParams(vmem_limit_bytes=VMEM_LIMIT),
         name="gram_rows",
-    )(counts, *far(interp))
+    )(*far(counts, interp))
 
 
 def share_kernel(a_ref, more_a_ref, b_ref, more_b_ref, residual_ref, out_ref, part_ref, sums_ref):
@@ -435,6 +460,12 @@
     return lax.ppermute(value, "core", [(0, 1), (1, 0)])
 
 
+def to_next(values, axis, count):
+    return list(values[:1]) + [
+        lax.ppermute(values[d], axis, [(i, (i + d) % count) for i in range(count)]) for d in range(1, count)
+    ]
+
+
 def swap_x(value, mask):
     return lax.ppermute(value, "x", [(i, i ^ mask) for i in range(4)])
 
@@ -449,12 +480,14 @@
     image_t, residual_t, direction_t = (jnp.transpose(a, (0, 2, 1)) for a in (image_x, residual, direction))
 
     grams = gram_rows(interp[0], counts[0].T)
-    grams = lax.all_to_all(grams, SLAB, split_axis=0, concat_axis=0, tiled=True)
-    grams = gram_sum(grams, slot_tile[0].T)
+    grams = lax.all_to_all(grams.reshape(ZS, YS, 16, LANES), "z", split_axis=0, concat_axis=0, tiled=True)
+    outgoing = forward_y(direction_t, sensitivity, sel_maps, sel_spread, sending[0])
+    outgoing, grams = lax.optimization_barrier((outgoing, grams))
+    grams = regroup(grams)
+    grams = gram_sum(to_next(grams, "y", YS), slot_tile[0].T)
     grams = [grams] + from_x(grams)
     grams = grams + [swap_core(g) for g in grams]
 
-    outgoing = forward_y(direction_t, sensitivity, sel_maps, sel_spread, sending[0])
     pencils = lax.all_to_all(outgoing, SLAB, split_axis=0, concat_axis=0, tiled=True)
     norm = jnp.sum(residual_t * residual_t).reshape(1, 1)
     outgoing = middle(norm, pencils.reshape(-1, LANES), grams, arrival[0], sending[1])

time: 204 us -> 201 us (0.985)
  waiting for transfers between devices: 64.7 us -> 59 us
  Pallas kernels: 29.1 us -> 33.7 us
  local copies, waits for them, and re-layouts: 5.5 us -> 2.74 us
    all_to_all x1, waiting for transfers between devices: 38.1 us -> 22.6 us  [body(): lax.all_to_all(outgoing, SLAB, split_axis=0, concat_axis=0, tiled=True)]
    ppermute x0 -> x3, waiting for transfers between devices: none -> 7.3 us  [to_next(): lax.ppermute(values[d], axis, [(i, (i + d) % count) for i in range(count)])]
    ppermute x0 -> x3, starting transfers between devices: none -> 4.7 us  [to_next(): lax.ppermute(values[d], axis, [(i, (i + d) % count) for i in range(count)])]
    all_to_all x1, starting transfers between devices: 11.7 us -> 8.47 us  [body(): lax.all_to_all(grams.reshape(ZS, YS, 16, LANES), 'z', split_axis=0, conca...]
    unnamed x48 -> x44, local copies, waits for them, and re-layouts: 5.5 us -> 2.74 us
  transfers between devices with their start and end apart: 17 -> 20, of which waited for: 9 -> 12; matrix products, arithmetic and copies ran while one was open for 0% -> 0% of each run, Pallas kernels for 4% -> 6%
where the time goes in v5:
time: 201 us; the launch traced here: 198 us
  blocking collectives  64.2 us (32%)
  waiting for transfers between devices  59 us (29%)
  starting transfers between devices  37 us (18%)
  Pallas kernels  33.7 us (17%)
  local copies, waits for them, and re-layouts  2.74 us (1%)
    all_to_all x1, blocking collectives, body(): lax.all_to_all(outgoing, SLAB, split_axis=0, concat_axis=0, tiled=True)  64.2 us
    all_to_all x1, waiting for transfers between devices, body(): lax.all_to_all(outgoing, SLAB, split_axis=0, concat_axis=0, tiled=True)  22.6 us
    pallas_call x1, Pallas kernels, middle(): pl.pallas_call(middle_kernel, in_specs=[vmem] * 2 + [hbm] * 12, out_specs...  9.7 us
    all_to_all x1, starting transfers between devices, body(): lax.all_to_all(grams.reshape(ZS, YS, 16, LANES), 'z', split_axis=0, conca...  8.47 us
    ppermute x3, waiting for transfers between devices, from_x(): lax.ppermute(value, 'x', [(i, (i + d) % 4) for i in range(4)])  8.46 us
    all_to_all x1, waiting for transfers between devices, body(): lax.all_to_all(parts, SLAB + ('core',), split_axis=0, concat_axis=0, tile...  7.58 us
    ppermute x4, waiting for transfers between devices, swap_x(): return lax.ppermute(value, 'x', [(i, i ^ mask) for i in range(4)])  7.39 us
    ppermute x3, waiting for transfers between devices, to_next(): lax.ppermute(values[d], axis, [(i, (i + d) % count) for i in range(count)])  7.3 us
  transfers between devices with their start and end apart: 20, of which 12 were waited for; matrix products, arithmetic and copies ran while one was open for 0% of the time, Pallas kernels for 6%

profile of v5, /device:TPU:8, one launch (start us, length us, event | category | flops | bytes accessed | tf_op | source)
XLA Modules:
  0.0 198.5 jit_solution(14043220460196347256)
XLA Ops:
  0.7 4.6 %gram_rows.1 = f32[32,16,128]{2,1,0:T(8,128)} custom-call(s32[4,32]{1,0:T(4,128)} %bitcast.41, f32[32,4,64,128]{3,2,1,0:T(8,128)} %bitcast.39), custom_call_target="tpu_custom_call" | custom-call | tf_op jit(solution)/shard_map/gram_rows/pallas_call | solution.py:379
  5.3 8.5 %all-to-all-start = ((f32[8,4,16,128]{3,2,1,0:T(8,128)}), f32[8,4,16,128]{3,2,1,0:T(8,128)S(1)}, u32[]{:S(2)}, u32[]{:S(2)}) async-start(f32[8,4,16,128]{3,2,1,0:T(8,128)} %bitcast.6), calls=%async_computation | async-start | bytes 524288 | tf_op jit(solution)/shard_map/all_to_all | solution.py:483
  13.8 7.0 %forward_y.1 = f32[32,144,128]{2,1,0:T(8,128)} custom-call(f32[12,32,384]{2,1,0:T(8,128)S(1)} %bitcast.34, bf16[12,384,128]{2,1,0:T(8,128)(2,1)S(1)} %copy-done.1, bf16[128,256]{1,0:T(8,128)(2,1)S(1)} %copy-done.9, bf16[256,1024]{1,0:T(8,128)(2,1)} %constant.33.clone.spread_ref, bf16[384,768]{1,0:T(8,128)(2,1)S(1)} %copy-done.7, bf16[384,768]{1,0:T(8,128)(2,1)S(1)} %copy-done.6), custom_call_target="tpu_custom_call" | custom-call | tf_op jit(solution)/shard_map/forward_y/pallas_call | solution.py:212
  20.8 4.8 %all-to-all-done.in_ref = f32[8,4,16,128]{3,2,1,0:T(8,128)S(1)} async-done(((f32[8,4,16,128]{3,2,1,0:T(8,128)}), f32[8,4,16,128]{3,2,1,0:T(8,128)S(1)}, u32[]{:S(2)}, u32[]{:S(2)}) %all-to-all-start) | async-done | bytes 262176 | tf_op jit(solution)/shard_map/all_to_all | solution.py:483
  26.4 5.6 %all-to-all-start.1 = ((f32[32,144,128]{2,1,0:T(8,128)}), f32[32,144,128]{2,1,0:T(8,128)S(1)}, u32[]{:S(2)}, u32[]{:S(2)}) async-start(f32[32,144,128]{2,1,0:T(8,128)} %forward_y.1), calls=%async_computation.1 | async-start | bytes 4718592 | tf_op jit(solution)/shard_map/all_to_all | solution.py:491
  32.0 1.7 regroup.1
  35.9 2.4 %collective-permute-start.2 = (f32[8,16,128]{2,1,0:T(8,128)}, f32[8,16,128]{2,1,0:T(8,128)S(1)}, u32[]{:S(2)}, u32[]{:S(2)}) collective-permute-start(f32[8,16,128]{2,1,0:T(8,128)} %get-tuple-element.23), channel_id=1, source_target_pairs={{0,24},{8,0},{16,8},{24,16},{1,25},{9,1},{17,9},{25,17},{2,26},{10... | collective-permute-start | bytes 196616 | tf_op jit(solution)/shard_map/ppermute | solution.py:465
  38.3 2.1 %collective-permute-done.rest_1_ = f32[8,16,128]{2,1,0:T(8,128)S(1)} collective-permute-done((f32[8,16,128]{2,1,0:T(8,128)}, f32[8,16,128]{2,1,0:T(8,128)S(1)}, u32[]{:S(2)}, u32[]{:S(2)}) %collective-permute-start) | collective-permute-done | bytes 65568 | tf_op jit(solution)/shard_map/ppermute | solution.py:465
  40.4 2.8 %collective-permute-done.1.rest_2_ = f32[8,16,128]{2,1,0:T(8,128)S(1)} collective-permute-done((f32[8,16,128]{2,1,0:T(8,128)}, f32[8,16,128]{2,1,0:T(8,128)S(1)}, u32[]{:S(2)}, u32[]{:S(2)}) %collective-permute-start.1) | collective-permute-done | bytes 65568 | tf_op jit(solution)/shard_map/ppermute | solution.py:465
  43.2 2.4 %collective-permute-done.2.rest_3_ = f32[8,16,128]{2,1,0:T(8,128)S(1)} collective-permute-done((f32[8,16,128]{2,1,0:T(8,128)}, f32[8,16,128]{2,1,0:T(8,128)S(1)}, u32[]{:S(2)}, u32[]{:S(2)}) %collective-permute-start.2) | collective-permute-done | bytes 65568 | tf_op jit(solution)/shard_map/ppermute | solution.py:465
  46.3 2.3 %gram_sum.1.rest_0_ = f32[288,128]{1,0:T(8,128)} custom-call(s32[4,32]{1,0:T(4,128)} %bitcast.42, f32[8,16,128]{2,1,0:T(8,128)} %get-tuple-element.20.rest_0_, f32[8,16,128]{2,1,0:T(8,128)} %copy-done.19, f32[8,16,128]{2,1,0:T(8,128)} %copy-done.20, f32[8,16,128]{2,1,0:T(8,128)} %copy-done.21), custom_call_target="tpu_custom_call" | custom-call | tf_op jit(solution)/shard_map/gram_sum/pallas_call | solution.py:184
  48.5 2.8 %collective-permute-start.5 = (f32[288,128]{1,0:T(8,128)}, f32[288,128]{1,0:T(8,128)S(1)}, u32[]{:S(2)}, u32[]{:S(2)}) collective-permute-start(f32[288,128]{1,0:T(8,128)} %gram_sum.1.rest_0_), channel_id=1, source_target_pairs={{0,6},{2,0},{4,2},{6,4},{1,7},{3,1},{5,3},{7,5},{8,14},{10,8},{12,... | collective-permute-start | bytes 442376 | tf_op jit(solution)/shard_map/ppermute | solution.py:474
  53.0 4.9 %collective-permute-done.5.rest_3_ = f32[288,128]{1,0:T(8,128)S(1)} collective-permute-done((f32[288,128]{1,0:T(8,128)}, f32[288,128]{1,0:T(8,128)S(1)}, u32[]{:S(2)}, u32[]{:S(2)}) %collective-permute-start.5) | collective-permute-done | bytes 147488 | tf_op jit(solution)/shard_map/ppermute | solution.py:474
  57.9 1.9 collective-permute-done.4.rest_2_
  63.6 22.6 %all-to-all-done.1 = f32[32,144,128]{2,1,0:T(8,128)S(1)} async-done(((f32[32,144,128]{2,1,0:T(8,128)}), f32[32,144,128]{2,1,0:T(8,128)S(1)}, u32[]{:S(2)}, u32[]{:S(2)}) %all-to-all-start.1) | async-done | bytes 2359328 | tf_op jit(solution)/shard_map/all_to_all | solution.py:491
  86.2 9.7 %middle.1 = f32[32,152,128]{2,1,0:T(8,128)S(1)} custom-call(f32[1,1]{1,0:T(1,128)} %bitcast.1.norm_ref, f32[4608,128]{1,0:T(8,128)S(1)} %bitcast.33, f32[288,128]{1,0:T(8,128)} %gram_sum.1.rest_0_, f32[288,128]{1,0:T(8,128)} %copy-done.15, f32[288,128]{1,0:T(8,128)} %copy-done.14, f32[288,128]{1,0:T(8,128)} %copy-done.13, f32[288,128]{1,0:T(8,128)} %copy-done.16, ...), custom_call_target="tpu_custom_call" | custom-call | tf_op jit(solution)/shard_map/middle/pallas_call | solution.py:289
  96.0 64.2 %all_to_all.20 = f32[32,152,128]{2,1,0:T(8,128)S(1)} all-to-all(f32[32,152,128]{2,1,0:T(8,128)S(1)} %middle.1), channel_id=1, replica_groups=mesh['z'=8,'y'=4,'x'=4,'core'=2] {'z','y'}, dimensions={0} | all-to-all | bytes 4980736 | tf_op jit(solution)/shard_map/all_to_all | solution.py:494
  160.3 5.5 %backward_y.1 = (f32[104,384]{1,0:T(8,128)S(1)}, f32[96,384]{1,0:T(8,128)S(1)}, f32[104,384]{1,0:T(8,128)S(1)}, f32[96,384]{1,0:T(8,128)S(1)}) custom-call(f32[4864,128]{1,0:T(8,128)S(1)} %bitcast.32, bf16[12,384,128]{2,1,0:T(8,128)(2,1)S(1)} %copy-done.2, bf16[128,256]{1,0:T(8,128)(2,1)S(1)} %copy-done.10, bf16[1024,128]{1,0:T(8,128)(2,1)S(1)} %copy-done.11, ...), custom_call_target="tpu_custom_call" | custom-call | tf_op jit(solution)/shard_map/backward_y/pallas_call | solution.py:347
  169.1 2.2 %collective-permute-start.14 = (f32[96,384]{1,0:T(8,128)S(1)}, f32[96,384]{1,0:T(8,128)S(1)}, u32[]{:S(2)}, u32[]{:S(2)}) collective-permute-start(f32[96,384]{1,0:T(8,128)S(1)} %add.14), channel_id=1, source_target_pairs={{0,6},{2,4},{4,2},{6,0},{1,7},{3,5},{5,3},{7,1},{8,14},{10,12},{12... | collective-permute-start | bytes 442376 | tf_op jit(solution)/shard_map/ppermute | solution.py:470
  171.3 2.5 %collective-permute-done.11 = f32[104,384]{1,0:T(8,128)S(1)} collective-permute-done((f32[104,384]{1,0:T(8,128)S(1)}, f32[104,384]{1,0:T(8,128)S(1)}, u32[]{:S(2)}, u32[]{:S(2)}) %collective-permute-start.11) | collective-permute-done | bytes 159776 | tf_op jit(solution)/shard_map/ppermute | solution.py:470
  173.8 2.8 %collective-permute-start.12 = (f32[104,384]{1,0:T(8,128)S(1)}, f32[104,384]{1,0:T(8,128)S(1)}, u32[]{:S(2)}, u32[]{:S(2)}) collective-permute-start(f32[104,384]{1,0:T(8,128)S(1)} %add.13.a_ref), channel_id=1, source_target_pairs={{0,6},{2,4},{4,2},{6,0},{1,7},{3,5},{5,3},{7,1},{8,14},{10,12},{12... | collective-permute-start | bytes 479240 | tf_op jit(solution)/shard_map/ppermute | solution.py:470
  177.0 4.9 %collective-permute-done.15.more_b_ref = f32[96,384]{1,0:T(8,128)S(1)} collective-permute-done((f32[96,384]{1,0:T(8,128)S(1)}, f32[96,384]{1,0:T(8,128)S(1)}, u32[]{:S(2)}, u32[]{:S(2)}) %collective-permute-start.15) | collective-permute-done | bytes 147488 | tf_op jit(solution)/shard_map/ppermute | solution.py:470
  182.7 6.1 %all-to-all-start.3 = ((f32[64,1,128]{2,1,0:T(1,128)}), f32[64,1,128]{2,1,0:T(1,128)S(1)}, u32[]{:S(2)}, u32[]{:S(2)}) async-start(f32[64,1,128]{2,1,0:T(1,128)} %get-tuple-element.29), calls=%async_computation.3 | async-start | bytes 65536 | tf_op jit(solution)/shard_map/all_to_all | solution.py:507
  189.8 7.6 %all-to-all-done.3.parts_ref = f32[64,1,128]{2,1,0:T(1,128)S(1)} async-done(((f32[64,1,128]{2,1,0:T(1,128)}), f32[64,1,128]{2,1,0:T(1,128)S(1)}, u32[]{:S(2)}, u32[]{:S(2)}) %all-to-all-start.3) | async-done | bytes 32800 | tf_op jit(solution)/shard_map/all_to_all | solution.py:507
  (75 shorter events, 15.7 us)
Async XLA Ops:
  5.3 20.4 %all-to-all-start = ((f32[8,4,16,128]{3,2,1,0:T(8,128)}), f32[8,4,16,128]{3,2,1,0:T(8,128)S(1)}, u32[]{:S(2)}, u32[]{:S(2)}) async-start(f32[8,4,16,128]{3,2,1,0:T(8,128)} %bitcast.6), calls=%async_computation | async-start | bytes 524288 | tf_op jit(solution)/shard_map/all_to_all | solution.py:483
  26.4 59.9 %all-to-all-start.1 = ((f32[32,144,128]{2,1,0:T(8,128)}), f32[32,144,128]{2,1,0:T(8,128)S(1)}, u32[]{:S(2)}, u32[]{:S(2)}) async-start(f32[32,144,128]{2,1,0:T(8,128)} %forward_y.1), calls=%async_computation.1 | async-start | bytes 4718592 | tf_op jit(solution)/shard_map/all_to_all | solution.py:491
  33.6 6.8 %collective-permute-start = (f32[8,16,128]{2,1,0:T(8,128)}, f32[8,16,128]{2,1,0:T(8,128)S(1)}, u32[]{:S(2)}, u32[]{:S(2)}) collective-permute-start(f32[8,16,128]{2,1,0:T(8,128)} %get-tuple-element.21), channel_id=1, source_target_pairs={{0,8},{8,16},{16,24},{24,0},{1,9},{9,17},{17,25},{25,1},{2,10},{10... | collective-permute-start | bytes 196616 | tf_op jit(solution)/shard_map/ppermute | solution.py:465
  35.1 8.1 %collective-permute-start.1 = (f32[8,16,128]{2,1,0:T(8,128)}, f32[8,16,128]{2,1,0:T(8,128)S(1)}, u32[]{:S(2)}, u32[]{:S(2)}) collective-permute-start(f32[8,16,128]{2,1,0:T(8,128)} %get-tuple-element.22), channel_id=1, source_target_pairs={{0,16},{8,24},{16,0},{24,8},{1,17},{9,25},{17,1},{25,9},{2,18},{10... | collective-permute-start | bytes 196616 | tf_op jit(solution)/shard_map/ppermute | solution.py:465
  35.9 9.7 %collective-permute-start.2 = (f32[8,16,128]{2,1,0:T(8,128)}, f32[8,16,128]{2,1,0:T(8,128)S(1)}, u32[]{:S(2)}, u32[]{:S(2)}) collective-permute-start(f32[8,16,128]{2,1,0:T(8,128)} %get-tuple-element.23), channel_id=1, source_target_pairs={{0,24},{8,0},{16,8},{24,16},{1,25},{9,1},{17,9},{25,17},{2,26},{10... | collective-permute-start | bytes 196616 | tf_op jit(solution)/shard_map/ppermute | solution.py:465
  48.5 9.3 %collective-permute-start.5 = (f32[288,128]{1,0:T(8,128)}, f32[288,128]{1,0:T(8,128)S(1)}, u32[]{:S(2)}, u32[]{:S(2)}) collective-permute-start(f32[288,128]{1,0:T(8,128)} %gram_sum.1.rest_0_), channel_id=1, source_target_pairs={{0,6},{2,0},{4,2},{6,4},{1,7},{3,1},{5,3},{7,5},{8,14},{10,8},{12,... | collective-permute-start | bytes 442376 | tf_op jit(solution)/shard_map/ppermute | solution.py:474
  51.3 8.5 %collective-permute-start.4 = (f32[288,128]{1,0:T(8,128)}, f32[288,128]{1,0:T(8,128)S(1)}, u32[]{:S(2)}, u32[]{:S(2)}) collective-permute-start(f32[288,128]{1,0:T(8,128)} %gram_sum.1.rest_0_), channel_id=1, source_target_pairs={{0,4},{2,6},{4,0},{6,2},{1,5},{3,7},{5,1},{7,3},{8,12},{10,14},{12... | collective-permute-start | bytes 442376 | tf_op jit(solution)/shard_map/ppermute | solution.py:474
  52.1 9.4 %collective-permute-start.3 = (f32[288,128]{1,0:T(8,128)}, f32[288,128]{1,0:T(8,128)S(1)}, u32[]{:S(2)}, u32[]{:S(2)}) collective-permute-start(f32[288,128]{1,0:T(8,128)} %gram_sum.1.rest_0_), channel_id=1, source_target_pairs={{0,2},{2,4},{4,6},{6,0},{1,3},{3,5},{5,7},{7,1},{8,10},{10,12},{12... | collective-permute-start | bytes 442376 | tf_op jit(solution)/shard_map/ppermute | solution.py:474
  53.0 9.3 %collective-permute-start.6 = (f32[288,128]{1,0:T(8,128)}, f32[288,128]{1,0:T(8,128)S(1)}, u32[]{:S(2)}, u32[]{:S(2)}) collective-permute-start(f32[288,128]{1,0:T(8,128)} %gram_sum.1.rest_0_), channel_id=1, source_target_pairs={{0,1},{1,0},{2,3},{3,2},{4,5},{5,4},{6,7},{7,6},{8,9},{9,8},{10,11... | collective-permute-start | bytes 442376 | tf_op jit(solution)/shard_map/ppermute | solution.py:460
  57.9 4.4 %collective-permute-start.9 = (f32[288,128]{1,0:T(8,128)S(1)}, f32[288,128]{1,0:T(8,128)S(1)}, u32[]{:S(2)}, u32[]{:S(2)}) collective-permute-start(f32[288,128]{1,0:T(8,128)S(1)} %collective-permute-done.5.rest_3_), channel_id=1, source_target_pairs={{0,1},{1,0},{2,3},{3,2},{4,5},{5,4},{6,7},{7,6},{8,9},{9,8},{10,11... | collective-permute-start | bytes 442376 | tf_op jit(solution)/shard_map/ppermute | solution.py:460
  59.8 2.5 %collective-permute-start.8 = (f32[288,128]{1,0:T(8,128)S(1)}, f32[288,128]{1,0:T(8,128)S(1)}, u32[]{:S(2)}, u32[]{:S(2)}) collective-permute-start(f32[288,128]{1,0:T(8,128)S(1)} %collective-permute-done.4.rest_2_), channel_id=1, source_target_pairs={{0,1},{1,0},{2,3},{3,2},{4,5},{5,4},{6,7},{7,6},{8,9},{9,8},{10,11... | collective-permute-start | bytes 442376 | tf_op jit(solution)/shard_map/ppermute | solution.py:460
  61.5 2.2 %collective-permute-start.7 = (f32[288,128]{1,0:T(8,128)S(1)}, f32[288,128]{1,0:T(8,128)}, u32[]{:S(2)}, u32[]{:S(2)}) collective-permute-start(f32[288,128]{1,0:T(8,128)S(1)} %collective-permute-done.3.rest_1_), channel_id=1, source_target_pairs={{0,1},{1,0},{2,3},{3,2},{4,5},{5,4},{6,7},{7,6},{8,9},{9,8},{10,11... | collective-permute-start | bytes 442376 | tf_op jit(solution)/shard_map/ppermute | solution.py:460
  95.9 64.3 %copy-start.2 = (bf16[12,384,128]{2,1,0:T(8,128)(2,1)S(1)}, bf16[12,384,128]{2,1,0:T(8,128)(2,1)}, u32[]{:S(2)}) copy-start(bf16[12,384,128]{2,1,0:T(8,128)(2,1)} %s_ref.3) | copy-start | bytes 3538948
  95.9 64.3 %copy-start.4 = (bf16[384,768]{1,0:T(8,128)(2,1)S(1)}, bf16[384,768]{1,0:T(8,128)(2,1)}, u32[]{:S(2)}) copy-start(bf16[384,768]{1,0:T(8,128)(2,1)} %constant.31.clone.low_ref) | copy-start | bytes 1769476
  96.0 64.3 %copy-start.5 = (bf16[384,768]{1,0:T(8,128)(2,1)S(1)}, bf16[384,768]{1,0:T(8,128)(2,1)}, u32[]{:S(2)}) copy-start(bf16[384,768]{1,0:T(8,128)(2,1)} %constant.30.clone.high_ref) | copy-start | bytes 1769476
  96.0 64.3 %copy-start.10 = (bf16[128,256]{1,0:T(8,128)(2,1)S(1)}, bf16[128,256]{1,0:T(8,128)(2,1)}, u32[]{:S(2)}) copy-start(bf16[128,256]{1,0:T(8,128)(2,1)} %constant.32.clone.maps_ref) | copy-start | bytes 196612
  165.8 1.7 collective-permute-start.10
  166.1 3.0 %collective-permute-start.13 = (f32[96,384]{1,0:T(8,128)S(1)}, f32[96,384]{1,0:T(8,128)S(1)}, u32[]{:S(2)}, u32[]{:S(2)}) collective-permute-start(f32[96,384]{1,0:T(8,128)S(1)} %get-tuple-element.27), channel_id=1, source_target_pairs={{0,1},{1,0},{2,3},{3,2},{4,5},{5,4},{6,7},{7,6},{8,9},{9,8},{10,11... | collective-permute-start | bytes 442376 | tf_op jit(solution)/shard_map/ppermute | solution.py:460
  167.5 6.2 %collective-permute-start.11 = (f32[104,384]{1,0:T(8,128)S(1)}, f32[104,384]{1,0:T(8,128)S(1)}, u32[]{:S(2)}, u32[]{:S(2)}) collective-permute-start(f32[104,384]{1,0:T(8,128)S(1)} %add.12), channel_id=1, source_target_pairs={{0,2},{2,0},{4,6},{6,4},{1,3},{3,1},{5,7},{7,5},{8,10},{10,8},{12,... | collective-permute-start | bytes 479240 | tf_op jit(solution)/shard_map/ppermute | solution.py:470
  169.1 7.5 %collective-permute-start.14 = (f32[96,384]{1,0:T(8,128)S(1)}, f32[96,384]{1,0:T(8,128)S(1)}, u32[]{:S(2)}, u32[]{:S(2)}) collective-permute-start(f32[96,384]{1,0:T(8,128)S(1)} %add.14), channel_id=1, source_target_pairs={{0,6},{2,4},{4,2},{6,0},{1,7},{3,5},{5,3},{7,1},{8,14},{10,12},{12... | collective-permute-start | bytes 442376 | tf_op jit(solution)/shard_map/ppermute | solution.py:470
  173.8 8.1 %collective-permute-start.12 = (f32[104,384]{1,0:T(8,128)S(1)}, f32[104,384]{1,0:T(8,128)S(1)}, u32[]{:S(2)}, u32[]{:S(2)}) collective-permute-start(f32[104,384]{1,0:T(8,128)S(1)} %add.13.a_ref), channel_id=1, source_target_pairs={{0,6},{2,4},{4,2},{6,0},{1,7},{3,5},{5,3},{7,1},{8,14},{10,12},{12... | collective-permute-start | bytes 479240 | tf_op jit(solution)/shard_map/ppermute | solution.py:470
  176.7 5.2 %collective-permute-start.15 = (f32[96,384]{1,0:T(8,128)S(1)}, f32[96,384]{1,0:T(8,128)S(1)}, u32[]{:S(2)}, u32[]{:S(2)}) collective-permute-start(f32[96,384]{1,0:T(8,128)S(1)} %add.15.b_ref), channel_id=1, source_target_pairs={{0,2},{2,0},{4,6},{6,4},{1,3},{3,1},{5,7},{7,5},{8,10},{10,8},{12,... | collective-permute-start | bytes 442376 | tf_op jit(solution)/shard_map/ppermute | solution.py:470
  182.7 14.6 %collective-permute-start.16 = (f32[192,384]{1,0:T(8,128)S(1)}, f32[192,384]{1,0:T(8,128)S(1)}, u32[]{:S(2)}, u32[]{:S(2)}) collective-permute-start(f32[192,384]{1,0:T(8,128)S(1)} %get-tuple-element.30.own_ref), channel_id=1, source_target_pairs={{0,1},{1,0},{2,3},{3,2},{4,5},{5,4},{6,7},{7,6},{8,9},{9,8},{10,11... | collective-permute-start | bytes 884744 | tf_op jit(solution)/shard_map/ppermute | solution.py:460
  182.7 14.6 %all-to-all-start.3 = ((f32[64,1,128]{2,1,0:T(1,128)}), f32[64,1,128]{2,1,0:T(1,128)S(1)}, u32[]{:S(2)}, u32[]{:S(2)}) async-start(f32[64,1,128]{2,1,0:T(1,128)} %get-tuple-element.29), calls=%async_computation.3 | async-start | bytes 65536 | tf_op jit(solution)/shard_map/all_to_all | solution.py:507
  (18 other events, 212.3 us)

commit v6 on v5

--- a/solution.py
+++ b/solution.py
@@ -114,7 +114,7 @@
     highs, lows = [], []
     for piece, turn in zip(pieces, turned):
         piece_high, piece_low = split(piece)
-        turn_high, turn_low = split(turn)
+        turn_high, turn_low = (times_i(piece_high), times_i(piece_low)) if turn is None else split(turn)
         highs.append(jnp.concatenate([piece_high, turn_high], axis=0))
         lows.append(jnp.concatenate([piece_low, turn_low], axis=0))
     high = jnp.concatenate(highs, axis=1)
@@ -248,11 +248,12 @@
             load_g.append(pltpu.make_async_copy(g_hbm[4 * k + d], g_ref.at[c], g_sem.at[4 * k + d]))
     for copy in load_tables[:2] + load_g + load_tables[2:]:
         copy.start()
-    for copy in load_tables[:2]:
-        copy.wait()
     for p in range(PAIRS):
         pieces = [arrived_rows(in_ref, 2 * p + i, BLOCK) for i in range(2)]
-        done = transform(fh_ref, fl_ref, pieces, [times_i(x) for x in pieces])
+        if p == 0:
+            for copy in load_tables[:2]:
+                copy.wait()
+        done = transform(fh_ref, fl_ref, pieces, [None, None])
         for i in range(2):
             b = 2 * p + i
             grid_ref[b // TY, pl.ds(b % TY, N, stride=TY), :] = done[:, LANES * i:LANES * (i + 1)]
@@ -279,7 +280,7 @@
     out_ref[:, BLOCK:, :] = jnp.broadcast_to(sums[None], (SLABS, 8, LANES))
     for p in range(PAIRS):
         pieces = [grid_ref[b // TY, pl.ds(b % TY, N, stride=TY), :] for b in (2 * p, 2 * p + 1)]
-        done = transform(bh_ref, bl_ref, pieces, [times_i(x) for x in pieces])
+        done = transform(bh_ref, bl_ref, pieces, [None, None])
         store_outgoing(out_ref, 24 * p, done[:, :LANES], done[:, LANES:])
 
 
@@ -318,7 +319,7 @@
         for p in range(2):
             rows = [4 * g + 2 * p + i for i in range(2)]
             pieces = [arrived_rows(in_ref, r, block) for r in rows]
-            done = transform(high_ref, low_ref, pieces, [times_i(x) for x in pieces])
+            done = transform(high_ref, low_ref, pieces, [None, None])
             for i in range(2):
                 back = done[:, LANES * i:LANES * (i + 1)]
                 maps = dot(s_ref[rows[i]], maps_ref[...])
@@ -366,8 +367,8 @@
             rows.append(jnp.where(lane < live, w_ref[o, j, pl.ds(at, 8), :], 0.0))
         l_high, l_low = split(jnp.concatenate(rows, axis=0))
         r_high, r_low = split(w_ref[o].reshape(CAP * CELLS, SB))
-        gram = dot_nt(jnp.concatenate([l_high, l_low], axis=1), jnp.concatenate([r_high, r_high], axis=1))
-        gram = gram + dot_nt(l_high, r_low)
+        both = dot_nt(jnp.concatenate([l_high, l_low], axis=0), r_high)
+        gram = both[:CAP * 8] + (both[CAP * 8:] + dot_nt(l_high, r_low))
         for m in range(CAP // 2):
             first = gram[16 * m:16 * m + 8, LANES * m:LANES * (m + 1)]
             second = gram[16 * m + 8:16 * m + 16, LANES * m:LANES * (m + 1)]

time: 201 us -> 200 us (level)
  no operation moved by 1% of the time
where the time goes in v6:
time: 200 us; the launch traced here: 197 us
  blocking collectives  64.2 us (32%)
  waiting for transfers between devices  59 us (30%)
  starting transfers between devices  36.8 us (18%)
  Pallas kernels  32.6 us (16%)
  local copies, waits for them, and re-layouts  2.74 us (1%)
    all_to_all x1, blocking collectives, body(): lax.all_to_all(outgoing, SLAB, split_axis=0, concat_axis=0, tiled=True)  64.2 us
    all_to_all x1, waiting for transfers between devices, body(): lax.all_to_all(outgoing, SLAB, split_axis=0, concat_axis=0, tiled=True)  22.6 us
    pallas_call x1, Pallas kernels, middle(): pl.pallas_call(middle_kernel, in_specs=[vmem] * 2 + [hbm] * 12, out_specs...  9.35 us
    all_to_all x1, starting transfers between devices, body(): lax.all_to_all(grams.reshape(ZS, YS, 16, LANES), 'z', split_axis=0, conca...  8.47 us
    ppermute x3, waiting for transfers between devices, from_x(): lax.ppermute(value, 'x', [(i, (i + d) % 4) for i in range(4)])  8.4 us
    all_to_all x1, waiting for transfers between devices, body(): lax.all_to_all(parts, SLAB + ('core',), split_axis=0, concat_axis=0, tile...  7.58 us
    ppermute x4, waiting for transfers between devices, swap_x(): return lax.ppermute(value, 'x', [(i, i ^ mask) for i in range(4)])  7.37 us
    ppermute x3, waiting for transfers between devices, to_next(): lax.ppermute(values[d], axis, [(i, (i + d) % count) for i in range(count)])  7.28 us
  transfers between devices with their start and end apart: 20, of which 12 were waited for; matrix products, arithmetic and copies ran while one was open for 0% of the time, Pallas kernels for 6%

profile of v6, /device:TPU:8, one launch (start us, length us, event | category | flops | bytes accessed | tf_op | source)
XLA Modules:
  0.0 197.2 jit_solution(16679904646890284814)
XLA Ops:
  0.7 4.0 %gram_rows.1 = f32[32,16,128]{2,1,0:T(8,128)} custom-call(s32[4,32]{1,0:T(4,128)} %bitcast.41, f32[32,4,64,128]{3,2,1,0:T(8,128)} %bitcast.39), custom_call_target="tpu_custom_call" | custom-call | tf_op jit(solution)/shard_map/gram_rows/pallas_call | solution.py:380
  4.7 8.5 %all-to-all-start = ((f32[8,4,16,128]{3,2,1,0:T(8,128)}), f32[8,4,16,128]{3,2,1,0:T(8,128)S(1)}, u32[]{:S(2)}, u32[]{:S(2)}) async-start(f32[8,4,16,128]{3,2,1,0:T(8,128)} %bitcast.6), calls=%async_computation | async-start | bytes 524288 | tf_op jit(solution)/shard_map/all_to_all | solution.py:484
  13.2 7.0 %forward_y.1 = f32[32,144,128]{2,1,0:T(8,128)} custom-call(f32[12,32,384]{2,1,0:T(8,128)S(1)} %bitcast.34, bf16[12,384,128]{2,1,0:T(8,128)(2,1)S(1)} %copy-done.1, bf16[128,256]{1,0:T(8,128)(2,1)S(1)} %copy-done.9, bf16[256,1024]{1,0:T(8,128)(2,1)} %constant.33.clone.spread_ref, bf16[384,768]{1,0:T(8,128)(2,1)S(1)} %copy-done.7, bf16[384,768]{1,0:T(8,128)(2,1)S(1)} %copy-done.6), custom_call_target="tpu_custom_call" | custom-call | tf_op jit(solution)/shard_map/forward_y/pallas_call | solution.py:212
  20.2 4.9 %all-to-all-done.in_ref = f32[8,4,16,128]{3,2,1,0:T(8,128)S(1)} async-done(((f32[8,4,16,128]{3,2,1,0:T(8,128)}), f32[8,4,16,128]{3,2,1,0:T(8,128)S(1)}, u32[]{:S(2)}, u32[]{:S(2)}) %all-to-all-start) | async-done | bytes 262176 | tf_op jit(solution)/shard_map/all_to_all | solution.py:484
  25.8 5.6 %all-to-all-start.1 = ((f32[32,144,128]{2,1,0:T(8,128)}), f32[32,144,128]{2,1,0:T(8,128)S(1)}, u32[]{:S(2)}, u32[]{:S(2)}) async-start(f32[32,144,128]{2,1,0:T(8,128)} %forward_y.1), calls=%async_computation.1 | async-start | bytes 4718592 | tf_op jit(solution)/shard_map/all_to_all | solution.py:492
  31.3 1.7 regroup.1
  35.3 2.4 %collective-permute-start.2 = (f32[8,16,128]{2,1,0:T(8,128)}, f32[8,16,128]{2,1,0:T(8,128)S(1)}, u32[]{:S(2)}, u32[]{:S(2)}) collective-permute-start(f32[8,16,128]{2,1,0:T(8,128)} %get-tuple-element.23), channel_id=1, source_target_pairs={{0,24},{8,0},{16,8},{24,16},{1,25},{9,1},{17,9},{25,17},{2,26},{10... | collective-permute-start | bytes 196616 | tf_op jit(solution)/shard_map/ppermute | solution.py:466
  37.7 2.1 %collective-permute-done.rest_1_ = f32[8,16,128]{2,1,0:T(8,128)S(1)} collective-permute-done((f32[8,16,128]{2,1,0:T(8,128)}, f32[8,16,128]{2,1,0:T(8,128)S(1)}, u32[]{:S(2)}, u32[]{:S(2)}) %collective-permute-start) | collective-permute-done | bytes 65568 | tf_op jit(solution)/shard_map/ppermute | solution.py:466
  39.8 2.8 %collective-permute-done.1.rest_2_ = f32[8,16,128]{2,1,0:T(8,128)S(1)} collective-permute-done((f32[8,16,128]{2,1,0:T(8,128)}, f32[8,16,128]{2,1,0:T(8,128)S(1)}, u32[]{:S(2)}, u32[]{:S(2)}) %collective-permute-start.1) | collective-permute-done | bytes 65568 | tf_op jit(solution)/shard_map/ppermute | solution.py:466
  42.6 2.4 %collective-permute-done.2.rest_3_ = f32[8,16,128]{2,1,0:T(8,128)S(1)} collective-permute-done((f32[8,16,128]{2,1,0:T(8,128)}, f32[8,16,128]{2,1,0:T(8,128)S(1)}, u32[]{:S(2)}, u32[]{:S(2)}) %collective-permute-start.2) | collective-permute-done | bytes 65568 | tf_op jit(solution)/shard_map/ppermute | solution.py:466
  45.6 2.3 %gram_sum.1.rest_0_ = f32[288,128]{1,0:T(8,128)} custom-call(s32[4,32]{1,0:T(4,128)} %bitcast.42, f32[8,16,128]{2,1,0:T(8,128)} %get-tuple-element.20.rest_0_, f32[8,16,128]{2,1,0:T(8,128)} %copy-done.19, f32[8,16,128]{2,1,0:T(8,128)} %copy-done.20, f32[8,16,128]{2,1,0:T(8,128)} %copy-done.21), custom_call_target="tpu_custom_call" | custom-call | tf_op jit(solution)/shard_map/gram_sum/pallas_call | solution.py:184
  47.9 2.7 %collective-permute-start.5 = (f32[288,128]{1,0:T(8,128)}, f32[288,128]{1,0:T(8,128)S(1)}, u32[]{:S(2)}, u32[]{:S(2)}) collective-permute-start(f32[288,128]{1,0:T(8,128)} %gram_sum.1.rest_0_), channel_id=1, source_target_pairs={{0,6},{2,0},{4,2},{6,4},{1,7},{3,1},{5,3},{7,5},{8,14},{10,8},{12,... | collective-permute-start | bytes 442376 | tf_op jit(solution)/shard_map/ppermute | solution.py:475
  52.4 4.8 %collective-permute-done.5.rest_3_ = f32[288,128]{1,0:T(8,128)S(1)} collective-permute-done((f32[288,128]{1,0:T(8,128)}, f32[288,128]{1,0:T(8,128)S(1)}, u32[]{:S(2)}, u32[]{:S(2)}) %collective-permute-start.5) | collective-permute-done | bytes 147488 | tf_op jit(solution)/shard_map/ppermute | solution.py:475
  57.2 1.9 collective-permute-done.4.rest_2_
  63.0 22.6 %all-to-all-done.1 = f32[32,144,128]{2,1,0:T(8,128)S(1)} async-done(((f32[32,144,128]{2,1,0:T(8,128)}), f32[32,144,128]{2,1,0:T(8,128)S(1)}, u32[]{:S(2)}, u32[]{:S(2)}) %all-to-all-start.1) | async-done | bytes 2359328 | tf_op jit(solution)/shard_map/all_to_all | solution.py:492
  85.6 9.3 %middle.1 = f32[32,152,128]{2,1,0:T(8,128)S(1)} custom-call(f32[1,1]{1,0:T(1,128)} %bitcast.1.norm_ref, f32[4608,128]{1,0:T(8,128)S(1)} %bitcast.33, f32[288,128]{1,0:T(8,128)} %gram_sum.1.rest_0_, f32[288,128]{1,0:T(8,128)} %copy-done.15, f32[288,128]{1,0:T(8,128)} %copy-done.14, f32[288,128]{1,0:T(8,128)} %copy-done.13, f32[288,128]{1,0:T(8,128)} %copy-done.16, ...), custom_call_target="tpu_custom_call" | custom-call | tf_op jit(solution)/shard_map/middle/pallas_call | solution.py:290
  95.0 64.2 %all_to_all.20 = f32[32,152,128]{2,1,0:T(8,128)S(1)} all-to-all(f32[32,152,128]{2,1,0:T(8,128)S(1)} %middle.1), channel_id=1, replica_groups=mesh['z'=8,'y'=4,'x'=4,'core'=2] {'z','y'}, dimensions={0} | all-to-all | bytes 4980736 | tf_op jit(solution)/shard_map/all_to_all | solution.py:495
  159.3 5.5 %backward_y.1 = (f32[104,384]{1,0:T(8,128)S(1)}, f32[96,384]{1,0:T(8,128)S(1)}, f32[104,384]{1,0:T(8,128)S(1)}, f32[96,384]{1,0:T(8,128)S(1)}) custom-call(f32[4864,128]{1,0:T(8,128)S(1)} %bitcast.32, bf16[12,384,128]{2,1,0:T(8,128)(2,1)S(1)} %copy-done.2, bf16[128,256]{1,0:T(8,128)(2,1)S(1)} %copy-done.10, bf16[1024,128]{1,0:T(8,128)(2,1)S(1)} %copy-done.11, ...), custom_call_target="tpu_custom_call" | custom-call | tf_op jit(solution)/shard_map/backward_y/pallas_call | solution.py:348
  167.9 2.2 %collective-permute-start.14 = (f32[96,384]{1,0:T(8,128)S(1)}, f32[96,384]{1,0:T(8,128)S(1)}, u32[]{:S(2)}, u32[]{:S(2)}) collective-permute-start(f32[96,384]{1,0:T(8,128)S(1)} %add.14), channel_id=1, source_target_pairs={{0,6},{2,4},{4,2},{6,0},{1,7},{3,5},{5,3},{7,1},{8,14},{10,12},{12... | collective-permute-start | bytes 442376 | tf_op jit(solution)/shard_map/ppermute | solution.py:471
  170.1 2.5 %collective-permute-done.11 = f32[104,384]{1,0:T(8,128)S(1)} collective-permute-done((f32[104,384]{1,0:T(8,128)S(1)}, f32[104,384]{1,0:T(8,128)S(1)}, u32[]{:S(2)}, u32[]{:S(2)}) %collective-permute-start.11) | collective-permute-done | bytes 159776 | tf_op jit(solution)/shard_map/ppermute | solution.py:471
  172.5 2.8 %collective-permute-start.12 = (f32[104,384]{1,0:T(8,128)S(1)}, f32[104,384]{1,0:T(8,128)S(1)}, u32[]{:S(2)}, u32[]{:S(2)}) collective-permute-start(f32[104,384]{1,0:T(8,128)S(1)} %add.13.a_ref), channel_id=1, source_target_pairs={{0,6},{2,4},{4,2},{6,0},{1,7},{3,5},{5,3},{7,1},{8,14},{10,12},{12... | collective-permute-start | bytes 479240 | tf_op jit(solution)/shard_map/ppermute | solution.py:471
  175.7 4.9 %collective-permute-done.15.more_b_ref = f32[96,384]{1,0:T(8,128)S(1)} collective-permute-done((f32[96,384]{1,0:T(8,128)S(1)}, f32[96,384]{1,0:T(8,128)S(1)}, u32[]{:S(2)}, u32[]{:S(2)}) %collective-permute-start.15) | collective-permute-done | bytes 147488 | tf_op jit(solution)/shard_map/ppermute | solution.py:471
  181.5 6.1 %all-to-all-start.3 = ((f32[64,1,128]{2,1,0:T(1,128)}), f32[64,1,128]{2,1,0:T(1,128)S(1)}, u32[]{:S(2)}, u32[]{:S(2)}) async-start(f32[64,1,128]{2,1,0:T(1,128)} %get-tuple-element.29), calls=%async_computation.3 | async-start | bytes 65536 | tf_op jit(solution)/shard_map/all_to_all | solution.py:508
  188.5 7.6 %all-to-all-done.3.parts_ref = f32[64,1,128]{2,1,0:T(1,128)S(1)} async-done(((f32[64,1,128]{2,1,0:T(1,128)}), f32[64,1,128]{2,1,0:T(1,128)S(1)}, u32[]{:S(2)}, u32[]{:S(2)}) %all-to-all-start.3) | async-done | bytes 32800 | tf_op jit(solution)/shard_map/all_to_all | solution.py:508
  (75 shorter events, 15.6 us)
Async XLA Ops:
  4.7 20.4 %all-to-all-start = ((f32[8,4,16,128]{3,2,1,0:T(8,128)}), f32[8,4,16,128]{3,2,1,0:T(8,128)S(1)}, u32[]{:S(2)}, u32[]{:S(2)}) async-start(f32[8,4,16,128]{3,2,1,0:T(8,128)} %bitcast.6), calls=%async_computation | async-start | bytes 524288 | tf_op jit(solution)/shard_map/all_to_all | solution.py:484
  25.8 59.8 %all-to-all-start.1 = ((f32[32,144,128]{2,1,0:T(8,128)}), f32[32,144,128]{2,1,0:T(8,128)S(1)}, u32[]{:S(2)}, u32[]{:S(2)}) async-start(f32[32,144,128]{2,1,0:T(8,128)} %forward_y.1), calls=%async_computation.1 | async-start | bytes 4718592 | tf_op jit(solution)/shard_map/all_to_all | solution.py:492
  33.0 6.8 %collective-permute-start = (f32[8,16,128]{2,1,0:T(8,128)}, f32[8,16,128]{2,1,0:T(8,128)S(1)}, u32[]{:S(2)}, u32[]{:S(2)}) collective-permute-start(f32[8,16,128]{2,1,0:T(8,128)} %get-tuple-element.21), channel_id=1, source_target_pairs={{0,8},{8,16},{16,24},{24,0},{1,9},{9,17},{17,25},{25,1},{2,10},{10... | collective-permute-start | bytes 196616 | tf_op jit(solution)/shard_map/ppermute | solution.py:466
  34.5 8.1 %collective-permute-start.1 = (f32[8,16,128]{2,1,0:T(8,128)}, f32[8,16,128]{2,1,0:T(8,128)S(1)}, u32[]{:S(2)}, u32[]{:S(2)}) collective-permute-start(f32[8,16,128]{2,1,0:T(8,128)} %get-tuple-element.22), channel_id=1, source_target_pairs={{0,16},{8,24},{16,0},{24,8},{1,17},{9,25},{17,1},{25,9},{2,18},{10... | collective-permute-start | bytes 196616 | tf_op jit(solution)/shard_map/ppermute | solution.py:466
  35.3 9.7 %collective-permute-start.2 = (f32[8,16,128]{2,1,0:T(8,128)}, f32[8,16,128]{2,1,0:T(8,128)S(1)}, u32[]{:S(2)}, u32[]{:S(2)}) collective-permute-start(f32[8,16,128]{2,1,0:T(8,128)} %get-tuple-element.23), channel_id=1, source_target_pairs={{0,24},{8,0},{16,8},{24,16},{1,25},{9,1},{17,9},{25,17},{2,26},{10... | collective-permute-start | bytes 196616 | tf_op jit(solution)/shard_map/ppermute | solution.py:466
  47.9 9.3 %collective-permute-start.5 = (f32[288,128]{1,0:T(8,128)}, f32[288,128]{1,0:T(8,128)S(1)}, u32[]{:S(2)}, u32[]{:S(2)}) collective-permute-start(f32[288,128]{1,0:T(8,128)} %gram_sum.1.rest_0_), channel_id=1, source_target_pairs={{0,6},{2,0},{4,2},{6,4},{1,7},{3,1},{5,3},{7,5},{8,14},{10,8},{12,... | collective-permute-start | bytes 442376 | tf_op jit(solution)/shard_map/ppermute | solution.py:475
  50.6 8.5 %collective-permute-start.4 = (f32[288,128]{1,0:T(8,128)}, f32[288,128]{1,0:T(8,128)S(1)}, u32[]{:S(2)}, u32[]{:S(2)}) collective-permute-start(f32[288,128]{1,0:T(8,128)} %gram_sum.1.rest_0_), channel_id=1, source_target_pairs={{0,4},{2,6},{4,0},{6,2},{1,5},{3,7},{5,1},{7,3},{8,12},{10,14},{12... | collective-permute-start | bytes 442376 | tf_op jit(solution)/shard_map/ppermute | solution.py:475
  51.5 9.3 %collective-permute-start.3 = (f32[288,128]{1,0:T(8,128)}, f32[288,128]{1,0:T(8,128)S(1)}, u32[]{:S(2)}, u32[]{:S(2)}) collective-permute-start(f32[288,128]{1,0:T(8,128)} %gram_sum.1.rest_0_), channel_id=1, source_target_pairs={{0,2},{2,4},{4,6},{6,0},{1,3},{3,5},{5,7},{7,1},{8,10},{10,12},{12... | collective-permute-start | bytes 442376 | tf_op jit(solution)/shard_map/ppermute | solution.py:475
  52.4 9.2 %collective-permute-start.6 = (f32[288,128]{1,0:T(8,128)}, f32[288,128]{1,0:T(8,128)S(1)}, u32[]{:S(2)}, u32[]{:S(2)}) collective-permute-start(f32[288,128]{1,0:T(8,128)} %gram_sum.1.rest_0_), channel_id=1, source_target_pairs={{0,1},{1,0},{2,3},{3,2},{4,5},{5,4},{6,7},{7,6},{8,9},{9,8},{10,11... | collective-permute-start | bytes 442376 | tf_op jit(solution)/shard_map/ppermute | solution.py:461
  57.2 4.4 %collective-permute-start.9 = (f32[288,128]{1,0:T(8,128)S(1)}, f32[288,128]{1,0:T(8,128)S(1)}, u32[]{:S(2)}, u32[]{:S(2)}) collective-permute-start(f32[288,128]{1,0:T(8,128)S(1)} %collective-permute-done.5.rest_3_), channel_id=1, source_target_pairs={{0,1},{1,0},{2,3},{3,2},{4,5},{5,4},{6,7},{7,6},{8,9},{9,8},{10,11... | collective-permute-start | bytes 442376 | tf_op jit(solution)/shard_map/ppermute | solution.py:461
  59.1 2.5 %collective-permute-start.8 = (f32[288,128]{1,0:T(8,128)S(1)}, f32[288,128]{1,0:T(8,128)S(1)}, u32[]{:S(2)}, u32[]{:S(2)}) collective-permute-start(f32[288,128]{1,0:T(8,128)S(1)} %collective-permute-done.4.rest_2_), channel_id=1, source_target_pairs={{0,1},{1,0},{2,3},{3,2},{4,5},{5,4},{6,7},{7,6},{8,9},{9,8},{10,11... | collective-permute-start | bytes 442376 | tf_op jit(solution)/shard_map/ppermute | solution.py:461
  60.8 2.2 %collective-permute-start.7 = (f32[288,128]{1,0:T(8,128)S(1)}, f32[288,128]{1,0:T(8,128)}, u32[]{:S(2)}, u32[]{:S(2)}) collective-permute-start(f32[288,128]{1,0:T(8,128)S(1)} %collective-permute-done.3.rest_1_), channel_id=1, source_target_pairs={{0,1},{1,0},{2,3},{3,2},{4,5},{5,4},{6,7},{7,6},{8,9},{9,8},{10,11... | collective-permute-start | bytes 442376 | tf_op jit(solution)/shard_map/ppermute | solution.py:461
  94.9 64.3 %copy-start.2 = (bf16[12,384,128]{2,1,0:T(8,128)(2,1)S(1)}, bf16[12,384,128]{2,1,0:T(8,128)(2,1)}, u32[]{:S(2)}) copy-start(bf16[12,384,128]{2,1,0:T(8,128)(2,1)} %s_ref.3) | copy-start | bytes 3538948
  95.0 64.3 %copy-start.4 = (bf16[384,768]{1,0:T(8,128)(2,1)S(1)}, bf16[384,768]{1,0:T(8,128)(2,1)}, u32[]{:S(2)}) copy-start(bf16[384,768]{1,0:T(8,128)(2,1)} %constant.31.clone.low_ref) | copy-start | bytes 1769476
  95.0 64.3 %copy-start.5 = (bf16[384,768]{1,0:T(8,128)(2,1)S(1)}, bf16[384,768]{1,0:T(8,128)(2,1)}, u32[]{:S(2)}) copy-start(bf16[384,768]{1,0:T(8,128)(2,1)} %constant.30.clone.high_ref) | copy-start | bytes 1769476
  95.0 64.3 %copy-start.10 = (bf16[128,256]{1,0:T(8,128)(2,1)S(1)}, bf16[128,256]{1,0:T(8,128)(2,1)}, u32[]{:S(2)}) copy-start(bf16[128,256]{1,0:T(8,128)(2,1)} %constant.32.clone.maps_ref) | copy-start | bytes 196612
  164.8 1.5 collective-permute-start.10
  164.9 3.0 %collective-permute-start.13 = (f32[96,384]{1,0:T(8,128)S(1)}, f32[96,384]{1,0:T(8,128)S(1)}, u32[]{:S(2)}, u32[]{:S(2)}) collective-permute-start(f32[96,384]{1,0:T(8,128)S(1)} %get-tuple-element.27), channel_id=1, source_target_pairs={{0,1},{1,0},{2,3},{3,2},{4,5},{5,4},{6,7},{7,6},{8,9},{9,8},{10,11... | collective-permute-start | bytes 442376 | tf_op jit(solution)/shard_map/ppermute | solution.py:461
  166.3 6.2 %collective-permute-start.11 = (f32[104,384]{1,0:T(8,128)S(1)}, f32[104,384]{1,0:T(8,128)S(1)}, u32[]{:S(2)}, u32[]{:S(2)}) collective-permute-start(f32[104,384]{1,0:T(8,128)S(1)} %add.12), channel_id=1, source_target_pairs={{0,2},{2,0},{4,6},{6,4},{1,3},{3,1},{5,7},{7,5},{8,10},{10,8},{12,... | collective-permute-start | bytes 479240 | tf_op jit(solution)/shard_map/ppermute | solution.py:471
  167.9 7.5 %collective-permute-start.14 = (f32[96,384]{1,0:T(8,128)S(1)}, f32[96,384]{1,0:T(8,128)S(1)}, u32[]{:S(2)}, u32[]{:S(2)}) collective-permute-start(f32[96,384]{1,0:T(8,128)S(1)} %add.14), channel_id=1, source_target_pairs={{0,6},{2,4},{4,2},{6,0},{1,7},{3,5},{5,3},{7,1},{8,14},{10,12},{12... | collective-permute-start | bytes 442376 | tf_op jit(solution)/shard_map/ppermute | solution.py:471
  172.5 8.1 %collective-permute-start.12 = (f32[104,384]{1,0:T(8,128)S(1)}, f32[104,384]{1,0:T(8,128)S(1)}, u32[]{:S(2)}, u32[]{:S(2)}) collective-permute-start(f32[104,384]{1,0:T(8,128)S(1)} %add.13.a_ref), channel_id=1, source_target_pairs={{0,6},{2,4},{4,2},{6,0},{1,7},{3,5},{5,3},{7,1},{8,14},{10,12},{12... | collective-permute-start | bytes 479240 | tf_op jit(solution)/shard_map/ppermute | solution.py:471
  175.4 5.2 %collective-permute-start.15 = (f32[96,384]{1,0:T(8,128)S(1)}, f32[96,384]{1,0:T(8,128)S(1)}, u32[]{:S(2)}, u32[]{:S(2)}) collective-permute-start(f32[96,384]{1,0:T(8,128)S(1)} %add.15.b_ref), channel_id=1, source_target_pairs={{0,2},{2,0},{4,6},{6,4},{1,3},{3,1},{5,7},{7,5},{8,10},{10,8},{12,... | collective-permute-start | bytes 442376 | tf_op jit(solution)/shard_map/ppermute | solution.py:471
  181.5 14.6 %collective-permute-start.16 = (f32[192,384]{1,0:T(8,128)S(1)}, f32[192,384]{1,0:T(8,128)S(1)}, u32[]{:S(2)}, u32[]{:S(2)}) collective-permute-start(f32[192,384]{1,0:T(8,128)S(1)} %get-tuple-element.30.own_ref), channel_id=1, source_target_pairs={{0,1},{1,0},{2,3},{3,2},{4,5},{5,4},{6,7},{7,6},{8,9},{9,8},{10,11... | collective-permute-start | bytes 884744 | tf_op jit(solution)/shard_map/ppermute | solution.py:461
  181.5 14.6 %all-to-all-start.3 = ((f32[64,1,128]{2,1,0:T(1,128)}), f32[64,1,128]{2,1,0:T(1,128)S(1)}, u32[]{:S(2)}, u32[]{:S(2)}) async-start(f32[64,1,128]{2,1,0:T(1,128)} %get-tuple-element.29), calls=%async_computation.3 | async-start | bytes 65536 | tf_op jit(solution)/shard_map/all_to_all | solution.py:508
  (18 other events, 208.9 us)

commit v7 on v6

--- a/solution.py
+++ b/solution.py
@@ -101,10 +101,6 @@
     return pltpu.VMEM(shape, F32)
 
 
-def whole(array):
-    return pl.BlockSpec(array.shape, lambda i: (0,) * array.ndim)
-
-
 def times_i(value):
     rolled = pltpu.roll(value, HALF, 1)
     return jnp.where(lax.broadcasted_iota(jnp.int32, value.shape, 1) < HALF, -rolled, rolled)
@@ -192,36 +188,47 @@
     )(tiles, *arrived)
 
 
-def forward_y_kernel(d_ref, s_ref, maps_ref, spread_ref, high_ref, low_ref, out_ref):
-    flipped = d_ref[...].reshape(LANES, N).T
-    wide = dot(jnp.concatenate(split(flipped), axis=1), spread_ref[...])
-    for p in range(2):
-        images, turned = [], []
-        for r in (2 * p, 2 * p + 1):
-            maps = dot(s_ref[r], maps_ref[...])
-            real_map, imag_map = maps[:, :LANES], maps[:, LANES:]
-            d = wide[:, 2 * r * LANES:(2 * r + 1) * LANES]
-            turned_d = wide[:, (2 * r + 1) * LANES:(2 * r + 2) * LANES]
-            images.append(real_map * d + imag_map * turned_d)
-            turned.append(real_map * turned_d - imag_map * d)
-        done = transform(high_ref, low_ref, images, turned)
-        store_outgoing(out_ref, 24 * p, done[:, :LANES], done[:, LANES:])
+def forward_y_kernel(d_ref, s_ref, maps_ref, spread_hbm, high_ref, low_ref, out_hbm, spread_ref, out_ref, load_sem, sem):
+    load = pltpu.make_async_copy(spread_hbm, spread_ref, load_sem)
+    load.start()
+    load.wait()
+    stores = []
+    for g in range(ROWS // 4):
+        flipped = d_ref[4 * g:4 * g + 4].reshape(LANES, N).T
+        wide = dot(jnp.concatenate(split(flipped), axis=1), spread_ref[...])
+        for p in range(2):
+            images, turned = [], []
+            for r in (2 * p, 2 * p + 1):
+                maps = dot(s_ref[4 * g + r], maps_ref[...])
+                real_map, imag_map = maps[:, :LANES], maps[:, LANES:]
+                d = wide[:, 2 * r * LANES:(2 * r + 1) * LANES]
+                turned_d = wide[:, (2 * r + 1) * LANES:(2 * r + 2) * LANES]
+                images.append(real_map * d + imag_map * turned_d)
+                turned.append(real_map * turned_d - imag_map * d)
+            done = transform(high_ref, low_ref, images, turned)
+            pair = 2 * g + p
+            store_outgoing(out_ref, 24 * pair, done[:, :LANES], done[:, LANES:])
+            rows = pl.ds(24 * pair, 24)
+            stores.append(pltpu.make_async_copy(out_ref.at[:, rows, :], out_hbm.at[:, rows, :], sem.at[pair]))
+            stores[-1].start()
+    for copy in stores:
+        copy.wait()
 
 
 def forward_y(direction, maps, sel_maps, sel_spread, table):
+    vmem = pl.BlockSpec(memory_space=pltpu.VMEM)
+    hbm = pl.BlockSpec(memory_space=pltpu.HBM)
     return pl.pallas_call(
         forward_y_kernel,
-        grid=(ROWS // 4,),
-        in_specs=[
-            pl.BlockSpec((4, 2 * PLANES, N), lambda i: (i, 0, 0)),
-            pl.BlockSpec((4, N, LANES), lambda i: (i, 0, 0)),
-            whole(sel_maps),
-            whole(sel_spread),
-            whole(table[0]),
-            whole(table[1]),
+        in_specs=[vmem, vmem, vmem, hbm, vmem, vmem],
+        out_specs=hbm,
+        out_shape=pltpu.HBM((SLABS, BLOCK, LANES), F32),
+        scratch_shapes=[
+            pltpu.VMEM(sel_spread.shape, BF16),
+            pltpu.VMEM((SLABS, BLOCK, LANES), F32),
+            pltpu.SemaphoreType.DMA,
+            pltpu.SemaphoreType.DMA((PAIRS,)),
         ],
-        out_specs=pl.BlockSpec((SLABS, 48, LANES), lambda i: (0, i, 0)),
-        out_shape=pltpu.HBM((SLABS, 24 * PAIRS, LANES), F32),
         compiler_params=pltpu.CompilerParams(vmem_limit_bytes=VMEM_LIMIT),
         name="forward_y",
     )(*near(direction, maps, sel_maps), *far(sel_spread), *near(*table))

time: 200 us -> 199 us (level)
  no operation moved by 1% of the time
where the time goes in v7:
time: 199 us; the launch traced here: 197 us
  blocking collectives  64.2 us (32%)
  waiting for transfers between devices  59.4 us (30%)
  starting transfers between devices  36.5 us (18%)
  Pallas kernels  32.3 us (16%)
  local copies, waits for them, and re-layouts  2.74 us (1%)
    all_to_all x1, blocking collectives, body(): lax.all_to_all(outgoing, SLAB, split_axis=0, concat_axis=0, tiled=True)  64.2 us
    all_to_all x1, waiting for transfers between devices, body(): lax.all_to_all(outgoing, SLAB, split_axis=0, concat_axis=0, tiled=True)  22.6 us
    pallas_call x1, Pallas kernels, middle(): pl.pallas_call(middle_kernel, in_specs=[vmem] * 2 + [hbm] * 12, out_specs...  9.35 us
    all_to_all x1, starting transfers between devices, body(): lax.all_to_all(grams.reshape(ZS, YS, 16, LANES), 'z', split_axis=0, conca...  8.47 us
    ppermute x3, waiting for transfers between devices, from_x(): lax.ppermute(value, 'x', [(i, (i + d) % 4) for i in range(4)])  8.38 us
    all_to_all x1, waiting for transfers between devices, body(): lax.all_to_all(parts, SLAB + ('core',), split_axis=0, concat_axis=0, tile...  7.58 us
    ppermute x4, waiting for transfers between devices, swap_x(): return lax.ppermute(value, 'x', [(i, i ^ mask) for i in range(4)])  7.37 us
    ppermute x3, waiting for transfers between devices, to_next(): lax.ppermute(values[d], axis, [(i, (i + d) % count) for i in range(count)])  7.34 us
  transfers between devices with their start and end apart: 20, of which 12 were waited for; matrix products, arithmetic and copies ran while one was open for 0% of the time, Pallas kernels for 6%

profile of v7, /device:TPU:8, one launch (start us, length us, event | category | flops | bytes accessed | tf_op | source)
XLA Modules:
  0.0 196.9 jit_solution(8245407665672118308)
XLA Ops:
  0.7 4.0 %gram_rows.1 = f32[32,16,128]{2,1,0:T(8,128)} custom-call(s32[4,32]{1,0:T(4,128)} %bitcast.41, f32[32,4,64,128]{3,2,1,0:T(8,128)} %bitcast.39), custom_call_target="tpu_custom_call" | custom-call | tf_op jit(solution)/shard_map/gram_rows/pallas_call | solution.py:387
  4.7 8.5 %all-to-all-start = ((f32[8,4,16,128]{3,2,1,0:T(8,128)}), f32[8,4,16,128]{3,2,1,0:T(8,128)S(1)}, u32[]{:S(2)}, u32[]{:S(2)}) async-start(f32[8,4,16,128]{3,2,1,0:T(8,128)} %bitcast.6), calls=%async_computation | async-start | bytes 524288 | tf_op jit(solution)/shard_map/all_to_all | solution.py:491
  13.2 6.6 %forward_y.1 = f32[32,144,128]{2,1,0:T(8,128)} custom-call(f32[12,32,384]{2,1,0:T(8,128)S(1)} %bitcast.34, bf16[12,384,128]{2,1,0:T(8,128)(2,1)S(1)} %copy-done.1, bf16[128,256]{1,0:T(8,128)(2,1)S(1)} %copy-done.9, bf16[256,1024]{1,0:T(8,128)(2,1)} %constant.33.clone.spread_hbm, bf16[384,768]{1,0:T(8,128)(2,1)S(1)} %copy-done.7, bf16[384,768]{1,0:T(8,128)(2,1)S(1)} %copy-done.6), custom_call_target="tpu_custom_call" | custom-call | tf_op jit(solution)/shard_map/forward_y/pallas_call | solution.py:221
  19.8 5.2 %all-to-all-done.in_ref = f32[8,4,16,128]{3,2,1,0:T(8,128)S(1)} async-done(((f32[8,4,16,128]{3,2,1,0:T(8,128)}), f32[8,4,16,128]{3,2,1,0:T(8,128)S(1)}, u32[]{:S(2)}, u32[]{:S(2)}) %all-to-all-start) | async-done | bytes 262176 | tf_op jit(solution)/shard_map/all_to_all | solution.py:491
  25.8 5.2 %all-to-all-start.1 = ((f32[32,144,128]{2,1,0:T(8,128)}), f32[32,144,128]{2,1,0:T(8,128)S(1)}, u32[]{:S(2)}, u32[]{:S(2)}) async-start(f32[32,144,128]{2,1,0:T(8,128)} %forward_y.1), calls=%async_computation.1 | async-start | bytes 4718592 | tf_op jit(solution)/shard_map/all_to_all | solution.py:499
  31.0 1.7 regroup.1
  35.0 2.4 %collective-permute-start.2 = (f32[8,16,128]{2,1,0:T(8,128)}, f32[8,16,128]{2,1,0:T(8,128)S(1)}, u32[]{:S(2)}, u32[]{:S(2)}) collective-permute-start(f32[8,16,128]{2,1,0:T(8,128)} %get-tuple-element.23), channel_id=1, source_target_pairs={{0,24},{8,0},{16,8},{24,16},{1,25},{9,1},{17,9},{25,17},{2,26},{10... | collective-permute-start | bytes 196616 | tf_op jit(solution)/shard_map/ppermute | solution.py:473
  37.4 2.1 %collective-permute-done.rest_1_ = f32[8,16,128]{2,1,0:T(8,128)S(1)} collective-permute-done((f32[8,16,128]{2,1,0:T(8,128)}, f32[8,16,128]{2,1,0:T(8,128)S(1)}, u32[]{:S(2)}, u32[]{:S(2)}) %collective-permute-start) | collective-permute-done | bytes 65568 | tf_op jit(solution)/shard_map/ppermute | solution.py:473
  39.5 2.8 %collective-permute-done.1.rest_2_ = f32[8,16,128]{2,1,0:T(8,128)S(1)} collective-permute-done((f32[8,16,128]{2,1,0:T(8,128)}, f32[8,16,128]{2,1,0:T(8,128)S(1)}, u32[]{:S(2)}, u32[]{:S(2)}) %collective-permute-start.1) | collective-permute-done | bytes 65568 | tf_op jit(solution)/shard_map/ppermute | solution.py:473
  42.3 2.4 %collective-permute-done.2.rest_3_ = f32[8,16,128]{2,1,0:T(8,128)S(1)} collective-permute-done((f32[8,16,128]{2,1,0:T(8,128)}, f32[8,16,128]{2,1,0:T(8,128)S(1)}, u32[]{:S(2)}, u32[]{:S(2)}) %collective-permute-start.2) | collective-permute-done | bytes 65568 | tf_op jit(solution)/shard_map/ppermute | solution.py:473
  45.3 2.3 %gram_sum.1.rest_0_ = f32[288,128]{1,0:T(8,128)} custom-call(s32[4,32]{1,0:T(4,128)} %bitcast.42, f32[8,16,128]{2,1,0:T(8,128)} %get-tuple-element.20.rest_0_, f32[8,16,128]{2,1,0:T(8,128)} %copy-done.19, f32[8,16,128]{2,1,0:T(8,128)} %copy-done.20, f32[8,16,128]{2,1,0:T(8,128)} %copy-done.21), custom_call_target="tpu_custom_call" | custom-call | tf_op jit(solution)/shard_map/gram_sum/pallas_call | solution.py:180
  47.6 2.7 %collective-permute-start.5 = (f32[288,128]{1,0:T(8,128)}, f32[288,128]{1,0:T(8,128)S(1)}, u32[]{:S(2)}, u32[]{:S(2)}) collective-permute-start(f32[288,128]{1,0:T(8,128)} %gram_sum.1.rest_0_), channel_id=1, source_target_pairs={{0,6},{2,0},{4,2},{6,4},{1,7},{3,1},{5,3},{7,5},{8,14},{10,8},{12,... | collective-permute-start | bytes 442376 | tf_op jit(solution)/shard_map/ppermute | solution.py:482
  52.1 4.8 %collective-permute-done.5.rest_3_ = f32[288,128]{1,0:T(8,128)S(1)} collective-permute-done((f32[288,128]{1,0:T(8,128)}, f32[288,128]{1,0:T(8,128)S(1)}, u32[]{:S(2)}, u32[]{:S(2)}) %collective-permute-start.5) | collective-permute-done | bytes 147488 | tf_op jit(solution)/shard_map/ppermute | solution.py:482
  56.9 1.9 collective-permute-done.4.rest_2_
  62.6 22.6 %all-to-all-done.1 = f32[32,144,128]{2,1,0:T(8,128)S(1)} async-done(((f32[32,144,128]{2,1,0:T(8,128)}), f32[32,144,128]{2,1,0:T(8,128)S(1)}, u32[]{:S(2)}, u32[]{:S(2)}) %all-to-all-start.1) | async-done | bytes 2359328 | tf_op jit(solution)/shard_map/all_to_all | solution.py:499
  85.3 9.4 %middle.1 = f32[32,152,128]{2,1,0:T(8,128)S(1)} custom-call(f32[1,1]{1,0:T(1,128)} %bitcast.1.norm_ref, f32[4608,128]{1,0:T(8,128)S(1)} %bitcast.33, f32[288,128]{1,0:T(8,128)} %gram_sum.1.rest_0_, f32[288,128]{1,0:T(8,128)} %copy-done.15, f32[288,128]{1,0:T(8,128)} %copy-done.14, f32[288,128]{1,0:T(8,128)} %copy-done.13, f32[288,128]{1,0:T(8,128)} %copy-done.16, ...), custom_call_target="tpu_custom_call" | custom-call | tf_op jit(solution)/shard_map/middle/pallas_call | solution.py:297
  94.7 64.2 %all_to_all.20 = f32[32,152,128]{2,1,0:T(8,128)S(1)} all-to-all(f32[32,152,128]{2,1,0:T(8,128)S(1)} %middle.1), channel_id=1, replica_groups=mesh['z'=8,'y'=4,'x'=4,'core'=2] {'z','y'}, dimensions={0} | all-to-all | bytes 4980736 | tf_op jit(solution)/shard_map/all_to_all | solution.py:502
  159.0 5.5 %backward_y.1 = (f32[104,384]{1,0:T(8,128)S(1)}, f32[96,384]{1,0:T(8,128)S(1)}, f32[104,384]{1,0:T(8,128)S(1)}, f32[96,384]{1,0:T(8,128)S(1)}) custom-call(f32[4864,128]{1,0:T(8,128)S(1)} %bitcast.32, bf16[12,384,128]{2,1,0:T(8,128)(2,1)S(1)} %copy-done.2, bf16[128,256]{1,0:T(8,128)(2,1)S(1)} %copy-done.10, bf16[1024,128]{1,0:T(8,128)(2,1)S(1)} %copy-done.11, ...), custom_call_target="tpu_custom_call" | custom-call | tf_op jit(solution)/shard_map/backward_y/pallas_call | solution.py:355
  167.6 2.2 %collective-permute-start.14 = (f32[96,384]{1,0:T(8,128)S(1)}, f32[96,384]{1,0:T(8,128)S(1)}, u32[]{:S(2)}, u32[]{:S(2)}) collective-permute-start(f32[96,384]{1,0:T(8,128)S(1)} %add.14), channel_id=1, source_target_pairs={{0,6},{2,4},{4,2},{6,0},{1,7},{3,5},{5,3},{7,1},{8,14},{10,12},{12... | collective-permute-start | bytes 442376 | tf_op jit(solution)/shard_map/ppermute | solution.py:478
  169.7 2.5 %collective-permute-done.11 = f32[104,384]{1,0:T(8,128)S(1)} collective-permute-done((f32[104,384]{1,0:T(8,128)S(1)}, f32[104,384]{1,0:T(8,128)S(1)}, u32[]{:S(2)}, u32[]{:S(2)}) %collective-permute-start.11) | collective-permute-done | bytes 159776 | tf_op jit(solution)/shard_map/ppermute | solution.py:478
  172.2 2.8 %collective-permute-start.12 = (f32[104,384]{1,0:T(8,128)S(1)}, f32[104,384]{1,0:T(8,128)S(1)}, u32[]{:S(2)}, u32[]{:S(2)}) collective-permute-start(f32[104,384]{1,0:T(8,128)S(1)} %add.13.a_ref), channel_id=1, source_target_pairs={{0,6},{2,4},{4,2},{6,0},{1,7},{3,5},{5,3},{7,1},{8,14},{10,12},{12... | collective-permute-start | bytes 479240 | tf_op jit(solution)/shard_map/ppermute | solution.py:478
  175.4 4.9 %collective-permute-done.15.more_b_ref = f32[96,384]{1,0:T(8,128)S(1)} collective-permute-done((f32[96,384]{1,0:T(8,128)S(1)}, f32[96,384]{1,0:T(8,128)S(1)}, u32[]{:S(2)}, u32[]{:S(2)}) %collective-permute-start.15) | collective-permute-done | bytes 147488 | tf_op jit(solution)/shard_map/ppermute | solution.py:478
  181.1 6.1 %all-to-all-start.3 = ((f32[64,1,128]{2,1,0:T(1,128)}), f32[64,1,128]{2,1,0:T(1,128)S(1)}, u32[]{:S(2)}, u32[]{:S(2)}) async-start(f32[64,1,128]{2,1,0:T(1,128)} %get-tuple-element.29), calls=%async_computation.3 | async-start | bytes 65536 | tf_op jit(solution)/shard_map/all_to_all | solution.py:515
  188.2 7.6 %all-to-all-done.3.parts_ref = f32[64,1,128]{2,1,0:T(1,128)S(1)} async-done(((f32[64,1,128]{2,1,0:T(1,128)}), f32[64,1,128]{2,1,0:T(1,128)S(1)}, u32[]{:S(2)}, u32[]{:S(2)}) %all-to-all-start.3) | async-done | bytes 32800 | tf_op jit(solution)/shard_map/all_to_all | solution.py:515
  (75 shorter events, 15.6 us)
Async XLA Ops:
  4.7 20.4 %all-to-all-start = ((f32[8,4,16,128]{3,2,1,0:T(8,128)}), f32[8,4,16,128]{3,2,1,0:T(8,128)S(1)}, u32[]{:S(2)}, u32[]{:S(2)}) async-start(f32[8,4,16,128]{3,2,1,0:T(8,128)} %bitcast.6), calls=%async_computation | async-start | bytes 524288 | tf_op jit(solution)/shard_map/all_to_all | solution.py:491
  25.8 59.5 %all-to-all-start.1 = ((f32[32,144,128]{2,1,0:T(8,128)}), f32[32,144,128]{2,1,0:T(8,128)S(1)}, u32[]{:S(2)}, u32[]{:S(2)}) async-start(f32[32,144,128]{2,1,0:T(8,128)} %forward_y.1), calls=%async_computation.1 | async-start | bytes 4718592 | tf_op jit(solution)/shard_map/all_to_all | solution.py:499
  32.7 6.8 %collective-permute-start = (f32[8,16,128]{2,1,0:T(8,128)}, f32[8,16,128]{2,1,0:T(8,128)S(1)}, u32[]{:S(2)}, u32[]{:S(2)}) collective-permute-start(f32[8,16,128]{2,1,0:T(8,128)} %get-tuple-element.21), channel_id=1, source_target_pairs={{0,8},{8,16},{16,24},{24,0},{1,9},{9,17},{17,25},{25,1},{2,10},{10... | collective-permute-start | bytes 196616 | tf_op jit(solution)/shard_map/ppermute | solution.py:473
  34.1 8.1 %collective-permute-start.1 = (f32[8,16,128]{2,1,0:T(8,128)}, f32[8,16,128]{2,1,0:T(8,128)S(1)}, u32[]{:S(2)}, u32[]{:S(2)}) collective-permute-start(f32[8,16,128]{2,1,0:T(8,128)} %get-tuple-element.22), channel_id=1, source_target_pairs={{0,16},{8,24},{16,0},{24,8},{1,17},{9,25},{17,1},{25,9},{2,18},{10... | collective-permute-start | bytes 196616 | tf_op jit(solution)/shard_map/ppermute | solution.py:473
  35.0 9.7 %collective-permute-start.2 = (f32[8,16,128]{2,1,0:T(8,128)}, f32[8,16,128]{2,1,0:T(8,128)S(1)}, u32[]{:S(2)}, u32[]{:S(2)}) collective-permute-start(f32[8,16,128]{2,1,0:T(8,128)} %get-tuple-element.23), channel_id=1, source_target_pairs={{0,24},{8,0},{16,8},{24,16},{1,25},{9,1},{17,9},{25,17},{2,26},{10... | collective-permute-start | bytes 196616 | tf_op jit(solution)/shard_map/ppermute | solution.py:473
  47.6 9.3 %collective-permute-start.5 = (f32[288,128]{1,0:T(8,128)}, f32[288,128]{1,0:T(8,128)S(1)}, u32[]{:S(2)}, u32[]{:S(2)}) collective-permute-start(f32[288,128]{1,0:T(8,128)} %gram_sum.1.rest_0_), channel_id=1, source_target_pairs={{0,6},{2,0},{4,2},{6,4},{1,7},{3,1},{5,3},{7,5},{8,14},{10,8},{12,... | collective-permute-start | bytes 442376 | tf_op jit(solution)/shard_map/ppermute | solution.py:482
  50.3 8.5 %collective-permute-start.4 = (f32[288,128]{1,0:T(8,128)}, f32[288,128]{1,0:T(8,128)S(1)}, u32[]{:S(2)}, u32[]{:S(2)}) collective-permute-start(f32[288,128]{1,0:T(8,128)} %gram_sum.1.rest_0_), channel_id=1, source_target_pairs={{0,4},{2,6},{4,0},{6,2},{1,5},{3,7},{5,1},{7,3},{8,12},{10,14},{12... | collective-permute-start | bytes 442376 | tf_op jit(solution)/shard_map/ppermute | solution.py:482
  51.1 9.3 %collective-permute-start.3 = (f32[288,128]{1,0:T(8,128)}, f32[288,128]{1,0:T(8,128)S(1)}, u32[]{:S(2)}, u32[]{:S(2)}) collective-permute-start(f32[288,128]{1,0:T(8,128)} %gram_sum.1.rest_0_), channel_id=1, source_target_pairs={{0,2},{2,4},{4,6},{6,0},{1,3},{3,5},{5,7},{7,1},{8,10},{10,12},{12... | collective-permute-start | bytes 442376 | tf_op jit(solution)/shard_map/ppermute | solution.py:482
  52.1 9.2 %collective-permute-start.6 = (f32[288,128]{1,0:T(8,128)}, f32[288,128]{1,0:T(8,128)S(1)}, u32[]{:S(2)}, u32[]{:S(2)}) collective-permute-start(f32[288,128]{1,0:T(8,128)} %gram_sum.1.rest_0_), channel_id=1, source_target_pairs={{0,1},{1,0},{2,3},{3,2},{4,5},{5,4},{6,7},{7,6},{8,9},{9,8},{10,11... | collective-permute-start | bytes 442376 | tf_op jit(solution)/shard_map/ppermute | solution.py:468
  56.9 4.4 %collective-permute-start.9 = (f32[288,128]{1,0:T(8,128)S(1)}, f32[288,128]{1,0:T(8,128)S(1)}, u32[]{:S(2)}, u32[]{:S(2)}) collective-permute-start(f32[288,128]{1,0:T(8,128)S(1)} %collective-permute-done.5.rest_3_), channel_id=1, source_target_pairs={{0,1},{1,0},{2,3},{3,2},{4,5},{5,4},{6,7},{7,6},{8,9},{9,8},{10,11... | collective-permute-start | bytes 442376 | tf_op jit(solution)/shard_map/ppermute | solution.py:468
  58.8 2.4 %collective-permute-start.8 = (f32[288,128]{1,0:T(8,128)S(1)}, f32[288,128]{1,0:T(8,128)S(1)}, u32[]{:S(2)}, u32[]{:S(2)}) collective-permute-start(f32[288,128]{1,0:T(8,128)S(1)} %collective-permute-done.4.rest_2_), channel_id=1, source_target_pairs={{0,1},{1,0},{2,3},{3,2},{4,5},{5,4},{6,7},{7,6},{8,9},{9,8},{10,11... | collective-permute-start | bytes 442376 | tf_op jit(solution)/shard_map/ppermute | solution.py:468
  60.5 2.2 %collective-permute-start.7 = (f32[288,128]{1,0:T(8,128)S(1)}, f32[288,128]{1,0:T(8,128)}, u32[]{:S(2)}, u32[]{:S(2)}) collective-permute-start(f32[288,128]{1,0:T(8,128)S(1)} %collective-permute-done.3.rest_1_), channel_id=1, source_target_pairs={{0,1},{1,0},{2,3},{3,2},{4,5},{5,4},{6,7},{7,6},{8,9},{9,8},{10,11... | collective-permute-start | bytes 442376 | tf_op jit(solution)/shard_map/ppermute | solution.py:468
  94.6 64.3 %copy-start.2 = (bf16[12,384,128]{2,1,0:T(8,128)(2,1)S(1)}, bf16[12,384,128]{2,1,0:T(8,128)(2,1)}, u32[]{:S(2)}) copy-start(bf16[12,384,128]{2,1,0:T(8,128)(2,1)} %s_ref.3) | copy-start | bytes 3538948
  94.6 64.3 %copy-start.4 = (bf16[384,768]{1,0:T(8,128)(2,1)S(1)}, bf16[384,768]{1,0:T(8,128)(2,1)}, u32[]{:S(2)}) copy-start(bf16[384,768]{1,0:T(8,128)(2,1)} %constant.31.clone.low_ref) | copy-start | bytes 1769476
  94.7 64.3 %copy-start.5 = (bf16[384,768]{1,0:T(8,128)(2,1)S(1)}, bf16[384,768]{1,0:T(8,128)(2,1)}, u32[]{:S(2)}) copy-start(bf16[384,768]{1,0:T(8,128)(2,1)} %constant.30.clone.high_ref) | copy-start | bytes 1769476
  94.7 64.3 %copy-start.10 = (bf16[128,256]{1,0:T(8,128)(2,1)S(1)}, bf16[128,256]{1,0:T(8,128)(2,1)}, u32[]{:S(2)}) copy-start(bf16[128,256]{1,0:T(8,128)(2,1)} %constant.32.clone.maps_ref) | copy-start | bytes 196612
  164.4 1.5 collective-permute-start.10
  164.6 3.0 %collective-permute-start.13 = (f32[96,384]{1,0:T(8,128)S(1)}, f32[96,384]{1,0:T(8,128)S(1)}, u32[]{:S(2)}, u32[]{:S(2)}) collective-permute-start(f32[96,384]{1,0:T(8,128)S(1)} %get-tuple-element.27), channel_id=1, source_target_pairs={{0,1},{1,0},{2,3},{3,2},{4,5},{5,4},{6,7},{7,6},{8,9},{9,8},{10,11... | collective-permute-start | bytes 442376 | tf_op jit(solution)/shard_map/ppermute | solution.py:468
  165.9 6.2 %collective-permute-start.11 = (f32[104,384]{1,0:T(8,128)S(1)}, f32[104,384]{1,0:T(8,128)S(1)}, u32[]{:S(2)}, u32[]{:S(2)}) collective-permute-start(f32[104,384]{1,0:T(8,128)S(1)} %add.12), channel_id=1, source_target_pairs={{0,2},{2,0},{4,6},{6,4},{1,3},{3,1},{5,7},{7,5},{8,10},{10,8},{12,... | collective-permute-start | bytes 479240 | tf_op jit(solution)/shard_map/ppermute | solution.py:478
  167.6 7.5 %collective-permute-start.14 = (f32[96,384]{1,0:T(8,128)S(1)}, f32[96,384]{1,0:T(8,128)S(1)}, u32[]{:S(2)}, u32[]{:S(2)}) collective-permute-start(f32[96,384]{1,0:T(8,128)S(1)} %add.14), channel_id=1, source_target_pairs={{0,6},{2,4},{4,2},{6,0},{1,7},{3,5},{5,3},{7,1},{8,14},{10,12},{12... | collective-permute-start | bytes 442376 | tf_op jit(solution)/shard_map/ppermute | solution.py:478
  172.2 8.1 %collective-permute-start.12 = (f32[104,384]{1,0:T(8,128)S(1)}, f32[104,384]{1,0:T(8,128)S(1)}, u32[]{:S(2)}, u32[]{:S(2)}) collective-permute-start(f32[104,384]{1,0:T(8,128)S(1)} %add.13.a_ref), channel_id=1, source_target_pairs={{0,6},{2,4},{4,2},{6,0},{1,7},{3,5},{5,3},{7,1},{8,14},{10,12},{12... | collective-permute-start | bytes 479240 | tf_op jit(solution)/shard_map/ppermute | solution.py:478
  175.1 5.2 %collective-permute-start.15 = (f32[96,384]{1,0:T(8,128)S(1)}, f32[96,384]{1,0:T(8,128)S(1)}, u32[]{:S(2)}, u32[]{:S(2)}) collective-permute-start(f32[96,384]{1,0:T(8,128)S(1)} %add.15.b_ref), channel_id=1, source_target_pairs={{0,2},{2,0},{4,6},{6,4},{1,3},{3,1},{5,7},{7,5},{8,10},{10,8},{12,... | collective-permute-start | bytes 442376 | tf_op jit(solution)/shard_map/ppermute | solution.py:478
  181.1 14.6 %collective-permute-start.16 = (f32[192,384]{1,0:T(8,128)S(1)}, f32[192,384]{1,0:T(8,128)S(1)}, u32[]{:S(2)}, u32[]{:S(2)}) collective-permute-start(f32[192,384]{1,0:T(8,128)S(1)} %get-tuple-element.30.own_ref), channel_id=1, source_target_pairs={{0,1},{1,0},{2,3},{3,2},{4,5},{5,4},{6,7},{7,6},{8,9},{9,8},{10,11... | collective-permute-start | bytes 884744 | tf_op jit(solution)/shard_map/ppermute | solution.py:468
  181.1 14.6 %all-to-all-start.3 = ((f32[64,1,128]{2,1,0:T(1,128)}), f32[64,1,128]{2,1,0:T(1,128)S(1)}, u32[]{:S(2)}, u32[]{:S(2)}) async-start(f32[64,1,128]{2,1,0:T(1,128)} %get-tuple-element.29), calls=%async_computation.3 | async-start | bytes 65536 | tf_op jit(solution)/shard_map/all_to_all | solution.py:515
  (18 other events, 209.0 us)
